TPU v7x, 32 devices: a whole 2x2x4 slice. The times are simulated.
32 devices in a mesh: seq: 8 (over z, y), fsdp: 4 (over x, core).
Axes of the slice: x: 2, y: 2, z: 4, core: 2. Of those that a mesh axis runs over, the one named last changes fastest.
Arguments:
- latents: float32 [8, 1024, 64], P('fsdp', 'seq'), may hold values from -6 to 6
- gaussian_noise: float32 [8, 1024, 64], P('fsdp', 'seq'), may hold values from -6 to 6
- timesteps: float32 [8], P('fsdp'), may hold values from 0.05 to 0.95
- lengths: int32 [8], P('fsdp'), may hold values from 385 to 1024, as said below
- buckets: int32 [8], P('fsdp'), may hold values from 0 to 3
- context: bfloat16 [8, 128, 768], P('fsdp'), may hold values from -6 to 6
- attention_weights: float32 [6, 1536, 1536], P(None, None, ('seq', 'fsdp')), may hold values from -0.15625 to 0.15625
- attention_moment: float32 [6, 1536, 1536], P(None, None, ('seq', 'fsdp')), may hold values from -2.2888184e-05 to 2.2888184e-05
- cross_weights: float32 [2, 1536, 768], P(None, None, ('seq', 'fsdp')), may hold values from -0.21875 to 0.21875
- cross_moment: float32 [2, 1536, 768], P(None, None, ('seq', 'fsdp')), may hold values from -2.2888184e-05 to 2.2888184e-05
- gate_up_weights: float32 [12288, 1536], P(('seq', 'fsdp')), may hold values from -0.15625 to 0.15625
- gate_up_first: float32 [12288, 1536], P(('seq', 'fsdp')), may hold values from -2.3841858e-06 to 2.3841858e-06
- gate_up_second: float32 [12288, 1536], P(('seq', 'fsdp')), may hold values from 1.1667414e-13 to 4.622937e-13
- down_weights: float32 [6144, 1536], P(('seq', 'fsdp')), may hold values from -0.078125 to 0.078125
- down_first: float32 [6144, 1536], P(('seq', 'fsdp')), may hold values from -2.3841858e-06 to 2.3841858e-06
- down_second: float32 [6144, 1536], P(('seq', 'fsdp')), may hold values from 1.1667414e-13 to 4.622937e-13
- latent_weights: float32 [2, 64, 1536], P(None, None, ('seq', 'fsdp')), may hold values from -0.375 to 0.375
- latent_first: float32 [2, 64, 1536], P(None, None, ('seq', 'fsdp')), may hold values from -2.3841858e-06 to 2.3841858e-06
- latent_second: float32 [2, 64, 1536], P(None, None, ('seq', 'fsdp')), may hold values from 1.1667414e-13 to 4.622937e-13
- timing_weights: float32 [256, 1536], P(None, ('seq', 'fsdp')), may hold values from -0.375 to 0.375
- timing_first: float32 [256, 1536], P(None, ('seq', 'fsdp')), may hold values from -2.3841858e-06 to 2.3841858e-06
- timing_second: float32 [256, 1536], P(None, ('seq', 'fsdp')), may hold values from 1.1667414e-13 to 4.622937e-13
- norm_params: float32 [6, 1536], P(None, ('seq', 'fsdp'))
- norm_first: float32 [6, 1536], P(None, ('seq', 'fsdp')), may hold values from -7.6293945e-06 to 7.6293945e-06
- norm_second: float32 [6, 1536], P(None, ('seq', 'fsdp')), may hold values from 1.0566714e-12 to 4.1826577e-12
Outputs:
- loss_value: float32 [], replicated
- clip_norm: float32 [], replicated
- attention_new: float32 [6, 1536, 1536], P(None, None, ('seq', 'fsdp'))
- attention_moment_new: float32 [6, 1536, 1536], P(None, None, ('seq', 'fsdp'))
- attention_copy: bfloat16 [6, 1536, 1536], P(None, None, ('seq', 'fsdp'))
- cross_new: float32 [2, 1536, 768], P(None, None, ('seq', 'fsdp'))
- cross_moment_new: float32 [2, 1536, 768], P(None, None, ('seq', 'fsdp'))
- cross_copy: bfloat16 [2, 1536, 768], P(None, None, ('seq', 'fsdp'))
- gate_up_new: float32 [12288, 1536], P(('seq', 'fsdp'))
- gate_up_first_new: float32 [12288, 1536], P(('seq', 'fsdp'))
- gate_up_second_new: float32 [12288, 1536], P(('seq', 'fsdp'))
- gate_up_copy: bfloat16 [12288, 1536], P(('seq', 'fsdp'))
- down_new: float32 [6144, 1536], P(('seq', 'fsdp'))
- down_first_new: float32 [6144, 1536], P(('seq', 'fsdp'))
- down_second_new: float32 [6144, 1536], P(('seq', 'fsdp'))
- down_copy: bfloat16 [6144, 1536], P(('seq', 'fsdp'))
- latent_new: float32 [2, 64, 1536], P(None, None, ('seq', 'fsdp'))
- latent_first_new: float32 [2, 64, 1536], P(None, None, ('seq', 'fsdp'))
- latent_second_new: float32 [2, 64, 1536], P(None, None, ('seq', 'fsdp'))
- latent_copy: bfloat16 [2, 64, 1536], P(None, None, ('seq', 'fsdp'))
- timing_new: float32 [256, 1536], P(None, ('seq', 'fsdp'))
- timing_first_new: float32 [256, 1536], P(None, ('seq', 'fsdp'))
- timing_second_new: float32 [256, 1536], P(None, ('seq', 'fsdp'))
- timing_copy: bfloat16 [256, 1536], P(None, ('seq', 'fsdp'))
- norm_new: float32 [6, 1536], P(None, ('seq', 'fsdp'))
- norm_first_new: float32 [6, 1536], P(None, ('seq', 'fsdp'))
- norm_second_new: float32 [6, 1536], P(None, ('seq', 'fsdp'))
Inputs may be any that keep to these rules, and one draw needn't show every extreme that they name: `lengths`: in each block of 2 consecutive items at least one item has the full length 1024, which one drawn.
All inputs are finite; a program needn't handle non-finite values.
Results may differ from a plain program's by a relative error of at most 0.0015.
The roundings to bfloat16 on the way count: a program that leaves them out, or rounds other values in their place, can miss the bound.
Values may be sent and summed in bfloat16 or wider, within the bound.
A program may use at most 512 MiB of HBM per device.

v0:
```python
import math

import jax
import jax.numpy as jnp
from jax import lax
from jax.sharding import PartitionSpec as P

D = 1536
HEADS = 24
HEAD_DIM = 64
FF = 6144
E = 768
LAT = 64
FOUR = 256
NBUCK = 4
STEP = 10


HIGHEST = lax.Precision.HIGHEST
NS_COEF = (3.4445, -4.775, 2.0315)
CLIP_AT = 0.01
MUON_RATE = 0.5
ADAM_RATE = 0.02
GAIN_RATE = 0.2
DECAY_RATE = 0.01


def times_transposed(left, weight):
    return lax.dot_general(
        left, weight, (((left.ndim - 1,), (1,)), ((), ())), preferred_element_type=jnp.float32
    )


def matmul_low(left, right):
    return jnp.dot(left, right, preferred_element_type=jnp.float32)


def rows_product(left, right):
    return lax.dot_general(
        left, right, (((0,), (0,)), ((), ())), preferred_element_type=jnp.float32
    )


def rows_precise(left, right):
    return lax.dot_general(left, right, (((0,), (0,)), ((), ())), precision=HIGHEST)


def layer_norm(hidden, gain, shift):
    centred = hidden - jnp.mean(hidden, axis=-1, keepdims=True)
    spread = jnp.mean(centred * centred, axis=-1, keepdims=True)
    return centred * lax.rsqrt(spread + 1e-05) * gain + shift


def rotate(values, cosine, sine_table):
    half_dim = values.shape[-1] // 2
    first = values[..., :half_dim]
    second = values[..., half_dim:]
    return jnp.concatenate(
        [first * cosine - second * sine_table, second * cosine + first * sine_table], axis=-1
    )


def time_features(timesteps):
    count = FOUR // 2
    freqs = jnp.exp(jnp.arange(count, dtype=jnp.float32) * (math.log(100.0) / max(count - 1, 1)))
    phases = 2.0 * math.pi * timesteps[:, None] * freqs[None, :]
    return jnp.concatenate([jnp.cos(phases), jnp.sin(phases)], axis=1)


def split_heads(values):
    return values.reshape(values.shape[0], values.shape[1], HEADS, HEAD_DIM)


def scores_of(queries, key_rows):
    return jnp.einsum(
        "bqhd,bkhd->bhqk", queries, key_rows, preferred_element_type=jnp.float32
    ) / math.sqrt(HEAD_DIM)


def masked_scores(queries, key_rows, lengths):
    key_live = jnp.arange(key_rows.shape[1])[None, :] < lengths[:, None]
    return jnp.where(key_live[:, None, None, :], scores_of(queries, key_rows), -1e30)


def attention_forward(queries, key_low, value_low, lengths):
    item_count, frames = (queries.shape[0], queries.shape[1])
    running_top = jnp.full((item_count, HEADS, frames), -1e29, jnp.float32)
    scores = masked_scores(
        queries, split_heads(lax.all_gather(key_low, "seq", axis=1, tiled=True)), lengths
    )
    new_top = jnp.maximum(running_top, jnp.max(scores, axis=-1))
    running_sum = jnp.sum(jnp.exp(scores - new_top[..., None]), axis=-1)
    running_top, running_sum = (new_top, running_sum)
    log_total = running_top + jnp.log(running_sum)
    scores = masked_scores(
        queries, split_heads(lax.all_gather(key_low, "seq", axis=1, tiled=True)), lengths
    )
    weights = jnp.exp(scores - log_total[..., None]).astype(jnp.bfloat16)
    mixed = jnp.einsum(
        "bhqk,bkhd->bqhd",
        weights,
        split_heads(lax.all_gather(value_low, "seq", axis=1, tiled=True)),
        preferred_element_type=jnp.float32,
    )
    return (mixed, log_total)


def attention_backward(
    queries, key_low, value_low, grad_out, log_total, row_delta, lengths, position
):
    key_heads = split_heads(key_low)
    value_heads = split_heads(value_low)
    local_live = (position[None, :] < lengths[:, None])[:, None, None, :]
    query_flat = queries.reshape(key_low.shape).astype(jnp.float32)
    grad_flat = grad_out.reshape(key_low.shape).astype(jnp.float32)
    total_flat = jnp.transpose(log_total, (0, 2, 1))
    pieces = (
        lax.all_gather(query_flat.astype(jnp.bfloat16), "seq", axis=1, tiled=True).astype(
            jnp.float32
        ),
        lax.all_gather(grad_flat.astype(jnp.bfloat16), "seq", axis=1, tiled=True).astype(
            jnp.float32
        ),
        lax.all_gather(total_flat.astype(jnp.bfloat16), "seq", axis=1, tiled=True).astype(
            jnp.float32
        ),
        lax.all_gather(row_delta.astype(jnp.bfloat16), "seq", axis=1, tiled=True).astype(
            jnp.float32
        ),
    )
    query_rows = split_heads(pieces[0].astype(jnp.bfloat16))
    grad_rows = split_heads(pieces[1].astype(jnp.bfloat16))
    total_rows = jnp.transpose(pieces[2], (0, 2, 1))[..., None]
    delta_rows = jnp.transpose(pieces[3], (0, 2, 1))[..., None]
    scores = jnp.where(local_live, scores_of(query_rows, key_heads), -1e30)
    weights = jnp.exp(scores - total_rows)
    grad_value = jnp.einsum(
        "bhqk,bqhd->bkhd",
        weights.astype(jnp.bfloat16),
        grad_rows,
        preferred_element_type=jnp.float32,
    )
    grad_scores = jnp.einsum(
        "bqhd,bkhd->bhqk", grad_rows, value_heads, preferred_element_type=jnp.float32
    )
    pushed = (weights * (grad_scores - delta_rows)).astype(jnp.bfloat16)
    grad_key = jnp.einsum("bhqk,bqhd->bkhd", pushed, query_rows, preferred_element_type=jnp.float32)
    grad_key, grad_value = (grad_key, grad_value)
    delta_heads = jnp.transpose(row_delta, (0, 2, 1))[..., None]
    pieces = (
        lax.all_gather(key_low, "seq", axis=1, tiled=True),
        lax.all_gather(value_low, "seq", axis=1, tiled=True),
    )
    key_rows = split_heads(pieces[0])
    scores = masked_scores(queries, key_rows, lengths)
    weights = jnp.exp(scores - log_total[..., None])
    grad_scores = jnp.einsum(
        "bqhd,bkhd->bhqk", grad_out, split_heads(pieces[1]), preferred_element_type=jnp.float32
    )
    pushed = (weights * (grad_scores - delta_heads)).astype(jnp.bfloat16)
    grad_query = jnp.einsum("bhqk,bkhd->bqhd", pushed, key_rows, preferred_element_type=jnp.float32)
    score_scale = math.sqrt(HEAD_DIM)
    return (grad_query / score_scale, grad_key / score_scale, grad_value)


def layer_forward(weights, noisy_input, features, context, lengths, cosine, sine_table):
    attention, cross, gate_up, down, latent, timing, norms = weights
    norms = norms.astype(jnp.float32)
    item_count, frames, latent_dim = noisy_input.shape
    tokens = item_count * frames
    noisy_low = noisy_input.reshape(tokens, latent_dim).astype(jnp.bfloat16)
    feat_low = features.astype(jnp.bfloat16)
    timed = matmul_low(feat_low, timing)
    start_state = (
        matmul_low(noisy_low, latent[0]).reshape(item_count, frames, D) + timed[:, None, :]
    ).reshape(tokens, D)
    normed_one, back_one = jax.vjp(layer_norm, start_state, norms[0], norms[1])
    normed_one = normed_one.astype(jnp.bfloat16)
    triple = times_transposed(normed_one, attention[:3].reshape(3 * D, D)).reshape(
        item_count, frames, 3, HEADS, HEAD_DIM
    )
    queries = rotate(triple[:, :, 0], cosine, sine_table).astype(jnp.bfloat16)
    key_low = (
        rotate(triple[:, :, 1], cosine, sine_table)
        .astype(jnp.bfloat16)
        .reshape(item_count, frames, D)
    )
    value_low = triple[:, :, 2].astype(jnp.bfloat16).reshape(item_count, frames, D)
    mixed, log_total = attention_forward(queries, key_low, value_low, lengths)
    mixed_low = mixed.reshape(tokens, D).astype(jnp.bfloat16)
    after_self = start_state + times_transposed(mixed_low, attention[3])
    normed_two, back_two = jax.vjp(layer_norm, after_self, norms[2], norms[3])
    normed_two = normed_two.astype(jnp.bfloat16)
    cross_query = (
        times_transposed(normed_two, attention[4])
        .astype(jnp.bfloat16)
        .reshape(item_count, frames, HEADS, HEAD_DIM)
    )
    context_len = context.shape[1]
    cross_pair = times_transposed(
        context.reshape(item_count * context_len, E), cross.reshape(2 * D, E)
    ).astype(jnp.bfloat16)
    cross_pair = cross_pair.reshape(item_count, context_len, 2, HEADS, HEAD_DIM)
    cross_key, cross_value = (cross_pair[:, :, 0], cross_pair[:, :, 1])
    cross_weights = jax.nn.softmax(scores_of(cross_query, cross_key), axis=-1)
    cross_low = cross_weights.astype(jnp.bfloat16)
    cross_out = (
        jnp.einsum("bhqk,bkhd->bqhd", cross_low, cross_value, preferred_element_type=jnp.float32)
        .reshape(tokens, D)
        .astype(jnp.bfloat16)
    )
    after_cross = after_self + times_transposed(cross_out, attention[5])
    normed_three, back_three = jax.vjp(layer_norm, after_cross, norms[4], norms[5])
    normed_three = normed_three.astype(jnp.bfloat16)
    gate_both = times_transposed(normed_three, gate_up)
    gate_half, up_half = (gate_both[:, :FF], gate_both[:, FF:])
    inner_act = (jax.nn.silu(gate_half) * up_half).astype(jnp.bfloat16)
    final_state = (after_cross + matmul_low(inner_act, down)).astype(jnp.bfloat16)
    predicted = times_transposed(final_state, latent[1])
    saved = (
        noisy_low,
        feat_low,
        back_one,
        normed_one,
        queries,
        key_low,
        value_low,
        mixed,
        log_total,
        mixed_low,
        back_two,
        normed_two,
        cross_query,
        cross_key,
        cross_value,
        cross_weights,
        cross_low,
        cross_out,
        back_three,
        normed_three,
        gate_half,
        up_half,
        inner_act,
        final_state,
    )
    return (predicted, saved)


def layer_backward(weights, saved, grad_pred, context, lengths, cosine, sine_table, position):
    attention, cross, gate_up, down, latent, timing, norms = weights
    (
        noisy_low,
        feat_low,
        back_one,
        normed_one,
        queries,
        key_low,
        value_low,
        mixed,
        log_total,
        mixed_low,
        back_two,
        normed_two,
        cross_query,
        cross_key,
        cross_value,
        cross_weights,
        cross_low,
        cross_out,
        back_three,
        normed_three,
        gate_half,
        up_half,
        inner_act,
        final_state,
    ) = saved
    item_count, frames = (queries.shape[0], queries.shape[1])
    tokens = item_count * frames
    grad_out_proj = rows_product(grad_pred, final_state)
    grad_state = matmul_low(grad_pred, latent[1])
    grad_branch = grad_state.astype(jnp.bfloat16)
    down_reduced = lax.psum_scatter(
        rows_product(inner_act, grad_branch), ("seq", "fsdp"), scatter_dimension=0, tiled=True
    )
    grad_inner = times_transposed(grad_branch, down)
    sigmoid_gate = jax.nn.sigmoid(gate_half)
    grad_gate = grad_inner * up_half * sigmoid_gate * (1.0 + gate_half * (1.0 - sigmoid_gate))
    grad_both = jnp.concatenate([grad_gate, grad_inner * gate_half * sigmoid_gate], axis=1).astype(
        jnp.bfloat16
    )
    gate_up_reduced = lax.psum_scatter(
        rows_product(grad_both, normed_three), ("seq", "fsdp"), scatter_dimension=0, tiled=True
    )
    residual_part, gain_three, shift_three = back_three(matmul_low(grad_both, gate_up))
    grad_state = grad_state + residual_part
    grad_branch = grad_state.astype(jnp.bfloat16)
    grad_cross_out = rows_product(grad_branch, cross_out)
    grad_mix = (
        matmul_low(grad_branch, attention[5])
        .astype(jnp.bfloat16)
        .reshape(item_count, frames, HEADS, HEAD_DIM)
    )
    grad_scores = jnp.einsum(
        "bqhd,bkhd->bhqk", grad_mix, cross_value, preferred_element_type=jnp.float32
    )
    grad_cross_value = jnp.einsum(
        "bhqk,bqhd->bkhd", cross_low, grad_mix, preferred_element_type=jnp.float32
    )
    pushed = (
        cross_weights * (grad_scores - jnp.sum(cross_weights * grad_scores, axis=-1, keepdims=True))
    ).astype(jnp.bfloat16)
    score_scale = math.sqrt(HEAD_DIM)
    grad_cross_query = (
        (
            jnp.einsum("bhqk,bkhd->bqhd", pushed, cross_key, preferred_element_type=jnp.float32)
            / score_scale
        )
        .astype(jnp.bfloat16)
        .reshape(tokens, D)
    )
    grad_cross_key = (
        jnp.einsum("bhqk,bqhd->bkhd", pushed, cross_query, preferred_element_type=jnp.float32)
        / score_scale
    )
    context_len = context.shape[1]
    grad_pair = jnp.stack([grad_cross_key, grad_cross_value], axis=2).reshape(
        item_count * context_len, 2 * D
    )
    grad_cross = rows_precise(
        grad_pair, context.reshape(item_count * context_len, E).astype(jnp.float32)
    ).reshape(2, D, E)
    grad_cross_q = rows_product(grad_cross_query, normed_two)
    residual_part, gain_two, shift_two = back_two(matmul_low(grad_cross_query, attention[4]))
    grad_state = grad_state + residual_part
    grad_branch = grad_state.astype(jnp.bfloat16)
    grad_self_out = rows_product(grad_branch, mixed_low)
    grad_mixed = (
        matmul_low(grad_branch, attention[3])
        .astype(jnp.bfloat16)
        .reshape(item_count, frames, HEADS, HEAD_DIM)
    )
    row_delta = jnp.sum(grad_mixed.astype(jnp.float32) * mixed, axis=-1)
    grad_query, grad_key, grad_value = attention_backward(
        queries, key_low, value_low, grad_mixed, log_total, row_delta, lengths, position
    )
    grad_query = rotate(grad_query, cosine, -sine_table)
    grad_key = rotate(grad_key, cosine, -sine_table)
    grad_triple = (
        jnp.stack([grad_query, grad_key, grad_value], axis=2)
        .astype(jnp.bfloat16)
        .reshape(tokens, 3 * D)
    )
    grad_qkv = rows_product(grad_triple, normed_one).reshape(3, D, D)
    residual_part, gain_one, shift_one = back_one(
        matmul_low(grad_triple, attention[:3].reshape(3 * D, D))
    )
    grad_state = grad_state + residual_part
    grad_in_proj = rows_product(noisy_low, grad_state.astype(jnp.bfloat16))
    grad_timed = jnp.sum(grad_state.reshape(item_count, frames, D), axis=1)
    grad_timing = rows_precise(feat_low.astype(jnp.float32), grad_timed)
    grad_attention = jnp.concatenate(
        [grad_qkv, jnp.stack([grad_self_out, grad_cross_q, grad_cross_out])], axis=0
    )
    grad_latent = jnp.stack([grad_in_proj, grad_out_proj])
    grad_norms = jnp.stack([gain_one, shift_one, gain_two, shift_two, gain_three, shift_three])
    return (
        (grad_attention, grad_cross, grad_latent, grad_timing, grad_norms),
        gate_up_reduced,
        down_reduced,
    )


def gram_of(blocks):
    return jnp.einsum("sbik,sbjk->sbij", blocks, blocks, precision=HIGHEST)


def gram_sum(first, second):
    return lax.psum((gram_of(first), gram_of(second)), ("seq", "fsdp"))


def newton_schulz(first_moment, second_moment):
    moments = (first_moment, second_moment)
    blocks = [
        moment.reshape(moment.shape[0], moment.shape[1] // HEAD_DIM, HEAD_DIM, moment.shape[2])
        for moment in moments
    ]
    gram_list = gram_sum(blocks[0], blocks[1])
    block_norm = [
        jnp.sqrt(jnp.trace(gram, axis1=2, axis2=3))[..., None, None] + 1e-07 for gram in gram_list
    ]
    current = [block / norm_value for block, norm_value in zip(blocks, block_norm)]
    products = [gram / (norm_value * norm_value) for gram, norm_value in zip(gram_list, block_norm)]
    for newton_step in range(5):
        if newton_step > 0:
            products = gram_sum(current[0], current[1])
        updated = []
        for block, product in zip(current, products):
            squared = jnp.einsum("sbij,sbjk->sbik", product, product, precision=HIGHEST)
            mixer = NS_COEF[1] * product + NS_COEF[2] * squared
            updated.append(
                NS_COEF[0] * block + jnp.einsum("sbij,sbjk->sbik", mixer, block, precision=HIGHEST)
            )
        current = updated
    return [block.reshape(moment.shape) for block, moment in zip(current, moments)]


def adam_update(weight, first, second, grad, rate, decay):
    first_new = 0.9 * first + 0.1 * grad
    second_new = 0.95 * second + 0.05 * grad * grad
    first_hat = first_new / (1.0 - 0.9**STEP)
    second_hat = second_new / (1.0 - 0.95**STEP)
    weight_new = weight - rate * (first_hat / (jnp.sqrt(second_hat) + 1e-08) + decay * weight)
    return (weight_new, first_new, second_new)


def body(
    latents,
    gaussian_noise,
    timesteps,
    lengths,
    buckets,
    context,
    attention_weights,
    attention_moment,
    cross_weights,
    cross_moment,
    gate_up_weights,
    gate_up_first,
    gate_up_second,
    down_weights,
    down_first,
    down_second,
    latent_weights,
    latent_first,
    latent_second,
    timing_weights,
    timing_first,
    timing_second,
    norm_params,
    norm_first,
    norm_second,
):
    low_type = jnp.bfloat16
    item_count, frames, latent_dim = latents.shape
    tokens = item_count * frames
    onehot = (buckets[:, None] == jnp.arange(NBUCK)[None, :]).astype(jnp.float32)
    counts = lax.psum(jnp.dot(lengths.astype(jnp.float32), onehot, precision=HIGHEST), "fsdp")
    present = jnp.sum((counts > 0).astype(jnp.float32))
    bucket_scale = 1.0 / (present * LAT * jnp.maximum(counts, 1.0))
    item_scale = jnp.dot(onehot, bucket_scale, precision=HIGHEST)
    shards = (
        attention_weights.astype(low_type),
        cross_weights.astype(low_type),
        gate_up_weights.astype(low_type),
        down_weights.astype(low_type),
        latent_weights.astype(low_type),
        timing_weights.astype(low_type),
        norm_params.astype(low_type),
    )
    weights = (
        lax.all_gather(shards[0], ("seq", "fsdp"), axis=2, tiled=True),
        lax.all_gather(shards[1], ("seq", "fsdp"), axis=2, tiled=True),
        lax.all_gather(shards[2], ("seq", "fsdp"), axis=0, tiled=True),
        lax.all_gather(shards[3], ("seq", "fsdp"), axis=0, tiled=True),
        lax.all_gather(shards[4], ("seq", "fsdp"), axis=2, tiled=True),
        lax.all_gather(shards[5], ("seq", "fsdp"), axis=1, tiled=True),
        lax.all_gather(shards[6], ("seq", "fsdp"), axis=1, tiled=True),
    )
    signal = jnp.cos(0.5 * math.pi * timesteps)[:, None, None]
    noise_level = jnp.sin(0.5 * math.pi * timesteps)[:, None, None]
    noisy_input = signal * latents + noise_level * gaussian_noise
    target = (signal * gaussian_noise - noise_level * latents).reshape(tokens, latent_dim)
    features = time_features(timesteps)
    position = lax.axis_index("seq") * frames + jnp.arange(frames)
    live_mask = position[None, :] < lengths[:, None]
    half_dim = HEAD_DIM // 2
    inverse = 10000.0 ** (-jnp.arange(half_dim, dtype=jnp.float32) / half_dim)
    angles = position.astype(jnp.float32)[:, None] * inverse[None, :]
    cosine = jnp.cos(angles)[None, :, None, :]
    sine_table = jnp.sin(angles)[None, :, None, :]
    predicted, saved = layer_forward(
        weights, noisy_input, features, context, lengths, cosine, sine_table
    )
    difference = predicted - target
    errors = jnp.sum(difference * difference, axis=1).reshape(item_count, frames)
    per_item = jnp.sum(jnp.where(live_mask, errors, 0.0), axis=1)
    partial_sums = jnp.dot(per_item, onehot, precision=HIGHEST)
    bucket_sums = lax.psum(partial_sums, ("seq", "fsdp"))
    frame_scale = jnp.where(live_mask, item_scale[:, None], 0.0).reshape(tokens, 1)
    grad_pred = (2.0 * difference * frame_scale).astype(low_type)
    local_grads, gate_up_grad, down_grad = layer_backward(
        weights, saved, grad_pred, context, lengths, cosine, sine_table, position
    )
    reduced = (
        lax.psum_scatter(local_grads[0], ("seq", "fsdp"), scatter_dimension=2, tiled=True),
        lax.psum_scatter(local_grads[1], ("seq", "fsdp"), scatter_dimension=2, tiled=True),
        lax.psum_scatter(local_grads[2], ("seq", "fsdp"), scatter_dimension=2, tiled=True),
        lax.psum_scatter(local_grads[3], ("seq", "fsdp"), scatter_dimension=1, tiled=True),
        lax.psum_scatter(local_grads[4], ("seq", "fsdp"), scatter_dimension=1, tiled=True),
    )
    everything = tuple(reduced) + (gate_up_grad, down_grad)
    squares = sum((jnp.sum(grad * grad) for grad in everything))
    squares = lax.psum(squares, ("seq", "fsdp"))
    loss_value = jnp.sum(bucket_sums * bucket_scale)
    clip_norm = jnp.sqrt(squares)
    factor = CLIP_AT / jnp.maximum(clip_norm, CLIP_AT)
    attention_moment_new = 0.95 * attention_moment + reduced[0] * factor
    cross_moment_new = 0.95 * cross_moment + reduced[1] * factor
    attention_orth, cross_orth = newton_schulz(attention_moment_new, cross_moment_new)
    attention_new = attention_weights * (1.0 - MUON_RATE * DECAY_RATE) - MUON_RATE * attention_orth
    cross_new = cross_weights * (1.0 - MUON_RATE * DECAY_RATE) - MUON_RATE * cross_orth
    gate_up_new, gate_up_first_new, gate_up_second_new = adam_update(
        gate_up_weights, gate_up_first, gate_up_second, gate_up_grad * factor, ADAM_RATE, DECAY_RATE
    )
    down_new, down_first_new, down_second_new = adam_update(
        down_weights, down_first, down_second, down_grad * factor, ADAM_RATE, DECAY_RATE
    )
    latent_new, latent_first_new, latent_second_new = adam_update(
        latent_weights, latent_first, latent_second, reduced[2] * factor, ADAM_RATE, DECAY_RATE
    )
    timing_new, timing_first_new, timing_second_new = adam_update(
        timing_weights, timing_first, timing_second, reduced[3] * factor, ADAM_RATE, DECAY_RATE
    )
    norm_new, norm_first_new, norm_second_new = adam_update(
        norm_params, norm_first, norm_second, reduced[4] * factor, GAIN_RATE, 0.0
    )
    return (
        loss_value,
        clip_norm,
        attention_new,
        attention_moment_new,
        attention_new.astype(low_type),
        cross_new,
        cross_moment_new,
        cross_new.astype(low_type),
        gate_up_new,
        gate_up_first_new,
        gate_up_second_new,
        gate_up_new.astype(low_type),
        down_new,
        down_first_new,
        down_second_new,
        down_new.astype(low_type),
        latent_new,
        latent_first_new,
        latent_second_new,
        latent_new.astype(low_type),
        timing_new,
        timing_first_new,
        timing_second_new,
        timing_new.astype(low_type),
        norm_new,
        norm_first_new,
        norm_second_new,
    )


def solution(mesh):
    return jax.shard_map(
        body,
        mesh=mesh,
        in_specs=(
            P("fsdp", "seq", None),
            P("fsdp", "seq", None),
            P("fsdp"),
            P("fsdp"),
            P("fsdp"),
            P("fsdp", None, None),
            P(None, None, ("seq", "fsdp")),
            P(None, None, ("seq", "fsdp")),
            P(None, None, ("seq", "fsdp")),
            P(None, None, ("seq", "fsdp")),
            P(("seq", "fsdp"), None),
            P(("seq", "fsdp"), None),
            P(("seq", "fsdp"), None),
            P(("seq", "fsdp"), None),
            P(("seq", "fsdp"), None),
            P(("seq", "fsdp"), None),
            P(None, None, ("seq", "fsdp")),
            P(None, None, ("seq", "fsdp")),
            P(None, None, ("seq", "fsdp")),
            P(None, ("seq", "fsdp")),
            P(None, ("seq", "fsdp")),
            P(None, ("seq", "fsdp")),
            P(None, ("seq", "fsdp")),
            P(None, ("seq", "fsdp")),
            P(None, ("seq", "fsdp")),
        ),
        out_specs=(
            P(),
            P(),
            P(None, None, ("seq", "fsdp")),
            P(None, None, ("seq", "fsdp")),
            P(None, None, ("seq", "fsdp")),
            P(None, None, ("seq", "fsdp")),
            P(None, None, ("seq", "fsdp")),
            P(None, None, ("seq", "fsdp")),
            P(("seq", "fsdp"), None),
            P(("seq", "fsdp"), None),
            P(("seq", "fsdp"), None),
            P(("seq", "fsdp"), None),
            P(("seq", "fsdp"), None),
            P(("seq", "fsdp"), None),
            P(("seq", "fsdp"), None),
            P(("seq", "fsdp"), None),
            P(None, None, ("seq", "fsdp")),
            P(None, None, ("seq", "fsdp")),
            P(None, None, ("seq", "fsdp")),
            P(None, None, ("seq", "fsdp")),
            P(None, ("seq", "fsdp")),
            P(None, ("seq", "fsdp")),
            P(None, ("seq", "fsdp")),
            P(None, ("seq", "fsdp")),
            P(None, ("seq", "fsdp")),
            P(None, ("seq", "fsdp")),
            P(None, ("seq", "fsdp")),
        ),
        check_vma=False,
    )
```

profile of v0, /device:TPU:0, one launch (start us, length us, event | category | flops | bytes accessed | tf_op | source)
XLA Modules:
  0.0 4258.9 jit_solution(10382724464078080606)
XLA Ops:
  11.0 48.0 %all_gather.42 = bf16[2,64,1536]{1,0,2:T(2,128)(2,1)S(1)} all-gather(bf16[2,64,48]{1,0,2:T(2,128)(2,1)S(1)} %copy.368), channel_id=1, replica_groups=mesh['seq'=8,'fsdp'=4] {'seq','fsdp'}, dimensions={2}, use_global_device_ids=true | all-gather | bytes 405504 | tf_op jit(solution)/shard_map/all_gather | solution.py:465
  61.3 37.5 all-gather
  100.5 44.8 %all_gather.43 = bf16[256,1536]{0,1:T(8,128)(2,1)S(1)} all-gather(bf16[256,48]{0,1:T(8,128)(2,1)S(1)} %convert_element_type.217), channel_id=1, replica_groups=mesh['seq'=8,'fsdp'=4] {'seq','fsdp'}, dimensions={1}, use_global_device_ids=true | all-gather | bytes 811008 | tf_op jit(solution)/shard_map/all_gather | solution.py:466
  148.1 44.7 %all-gather.10.cloned.1.call-done = bf16[6,1536,1536]{1,2,0:T(8,128)(2,1)} async-done(((bf16[6,1536,48]{1,2,0:T(8,128)(2,1)}), bf16[6,1536,1536]{1,2,0:T(8,128)(2,1)}) %all-gather.10.cloned.1.call-update) | async-done | bytes 28311568 | tf_op jit(solution)/shard_map/all_gather | solution.py:461
  289.6 71.5 %all-gather.14.cloned.1.call-done = bf16[2,1024,1536]{1,2,0:T(8,128)(2,1)} async-done(((bf16[2,128,1536]{1,2,0:T(8,128)(2,1)}), bf16[2,1024,1536]{1,2,0:T(8,128)(2,1)}) %all-gather.14.cloned.1.call-update) | async-done | bytes 6291472 | tf_op jit(solution)/shard_map/all_gather | solution.py:96
  385.6 76.2 %all-gather.12.cloned.1.call-done = bf16[2,1024,1536]{1,2,0:T(8,128)(2,1)} async-done(((bf16[2,128,1536]{1,2,0:T(8,128)(2,1)}), bf16[2,1024,1536]{1,2,0:T(8,128)(2,1)}) %all-gather.12.cloned.1.call-update) | async-done | bytes 6291472 | tf_op jit(solution)/shard_map/all_gather | solution.py:102
  501.3 177.0 %all-gather.18.cloned.1.call-done = bf16[12288,1536]{1,0:T(8,128)(2,1)} async-done(((bf16[384,1536]{1,0:T(8,128)(2,1)}), bf16[12288,1536]{1,0:T(8,128)(2,1)}) %all-gather.18.cloned.1.call-update) | async-done | bytes 37748752 | tf_op jit(solution)/shard_map/all_gather | solution.py:463
  705.4 99.1 %all-gather.20.cloned.1.call-done = bf16[6144,1536]{1,0:T(8,128)(2,1)} async-done(((bf16[192,1536]{1,0:T(8,128)(2,1)}), bf16[6144,1536]{1,0:T(8,128)(2,1)}) %all-gather.20.cloned.1.call-update) | async-done | bytes 18874384 | tf_op jit(solution)/shard_map/all_gather | solution.py:464
  883.2 28.7 all_gather.52
  941.8 26.9 all_gather.54
  1134.3 38.0 pad_maximum_fusion
  1172.3 67.5 %copy.260 = f32[6,1536,1536]{1,0,2:T(8,128)} copy(f32[6,1536,1536]{2,1,0:T(8,128)} %pad_maximum_fusion) | data formatting | bytes 113246208 | tf_op jit(solution)/shard_map/concatenate | solution.py:361
  1241.2 30.0 fusion.44
  1300.7 138.8 %reduce-scatter.11.cloned.1.call-done = f32[2,1536,24]{1,2,0:T(8,128)} async-done(((f32[2,1536,768]{1,2,0:T(8,128)}), f32[2,1536,24]{1,2,0:T(8,128)}) %reduce-scatter.11.cloned.1.call-update) | async-done | bytes 294928 | tf_op jit(solution)/shard_map/reduce_scatter | solution.py:496
  1441.2 101.1 %reduce-scatter.13.cloned.1.call-done = f32[256,48]{0,1:T(8,128)} async-done(((f32[256,1536]{0,1:T(8,128)}), f32[256,48]{0,1:T(8,128)}) %reduce-scatter.13.cloned.1.call-update) | async-done | bytes 49168 | tf_op jit(solution)/shard_map/reduce_scatter | solution.py:498
  1543.7 353.5 %reduce-scatter.17.cloned.1.call-done = f32[192,1536]{1,0:T(8,128)} async-done(((f32[6144,1536]{1,0:T(8,128)}), f32[192,1536]{1,0:T(8,128)}) %reduce-scatter.17.cloned.1.call-update) | async-done | bytes 1179664 | tf_op jit(solution)/shard_map/reduce_scatter | solution.py:282
  1899.4 659.8 %reduce-scatter.9.cloned.1.call-done = f32[6,1536,48]{1,0,2:T(8,128)} async-done(((f32[6,1536,1536]{1,0,2:T(8,128)}), f32[6,1536,48]{1,0,2:T(8,128)}) %reduce-scatter.9.cloned.1.call-update) | async-done | bytes 1769488 | tf_op jit(solution)/shard_map/reduce_scatter | solution.py:495
  2565.5 656.6 %reduce-scatter.15.cloned.1.call-done = f32[384,1536]{1,0:T(8,128)} async-done(((f32[12288,1536]{1,0:T(8,128)}), f32[384,1536]{1,0:T(8,128)}) %reduce-scatter.15.cloned.1.call-update) | async-done | bytes 2359312 | tf_op jit(solution)/shard_map/reduce_scatter | solution.py:291
  3226.2 39.6 all-reduce.1
  3291.7 155.7 %all-reduce.24.cloned.1.call-done = (f32[6,24,64,64]{3,2,1,0:T(8,128)}, f32[2,24,64,64]{3,2,1,0:T(8,128)}) async-done(((f32[6,24,64,64]{3,2,1,0:T(8,128)}, f32[2,24,64,64]{3,2,1,0:T(8,128)}), (f32[6,24,64,64]{3,2,1,0:T(8,128)}, f32[2,24,64,64]{3,2,1,0:T(8,128)})) %all-reduce.24.cloned.1.call-update) | async-done | bytes 3145744 | tf_op jit(solution)/shard_map/psum | solution.py:378
  3485.3 156.0 %all-reduce.22.cloned.1.call-done = (f32[6,24,64,64]{3,2,1,0:T(8,128)}, f32[2,24,64,64]{3,2,1,0:T(8,128)}) async-done(((f32[6,24,64,64]{3,2,1,0:T(8,128)}, f32[2,24,64,64]{3,2,1,0:T(8,128)}), (f32[6,24,64,64]{3,2,1,0:T(8,128)}, f32[2,24,64,64]{3,2,1,0:T(8,128)})) %all-reduce.22.cloned.1.call-update) | async-done | bytes 3145744 | tf_op jit(solution)/shard_map/psum | solution.py:378
  3677.5 156.0 %all-reduce.20.cloned.1.call-done = (f32[6,24,64,64]{3,2,1,0:T(8,128)}, f32[2,24,64,64]{3,2,1,0:T(8,128)}) async-done(((f32[6,24,64,64]{3,2,1,0:T(8,128)}, f32[2,24,64,64]{3,2,1,0:T(8,128)}), (f32[6,24,64,64]{3,2,1,0:T(8,128)}, f32[2,24,64,64]{3,2,1,0:T(8,128)})) %all-reduce.20.cloned.1.call-update) | async-done | bytes 3145744 | tf_op jit(solution)/shard_map/psum | solution.py:378
  3872.2 153.0 %all-reduce.18.cloned.1.call-done = (f32[6,24,64,64]{3,2,1,0:T(8,128)}, f32[2,24,64,64]{3,2,1,0:T(8,128)}) async-done(((f32[6,24,64,64]{3,2,1,0:T(8,128)}, f32[2,24,64,64]{3,2,1,0:T(8,128)}), (f32[6,24,64,64]{3,2,1,0:T(8,128)}, f32[2,24,64,64]{3,2,1,0:T(8,128)})) %all-reduce.18.cloned.1.call-update) | async-done | bytes 3145744 | tf_op jit(solution)/shard_map/psum | solution.py:378
  4074.3 142.8 %all-reduce.16.cloned.1.call-done = (f32[6,24,64,64]{3,2,1,0:T(8,128)}, f32[2,24,64,64]{3,2,1,0:T(8,128)}) async-done(((f32[6,24,64,64]{3,2,1,0:T(8,128)}, f32[2,24,64,64]{3,2,1,0:T(8,128)}), (f32[6,24,64,64]{3,2,1,0:T(8,128)}, f32[2,24,64,64]{3,2,1,0:T(8,128)})) %all-reduce.16.cloned.1.call-update) | async-done | bytes 3145744 | tf_op jit(solution)/shard_map/psum | solution.py:378
  (561 shorter events, 732.4 us)
Async XLA Ops:
  7.3 185.5 %all-gather.10.cloned.1.call-start = ((), (), s32[]{:S(2)}) async-start(), calls=%async_computation.6 | async-start | bytes 29196288 | tf_op jit(solution)/shard_map/all_gather | solution.py:461
  9.9 249.8 %all-gather.16.cloned.1.call-start = ((), (), s32[]{:S(2)}) async-start(), calls=%async_computation.9 | async-start | bytes 4866048 | tf_op jit(solution)/shard_map/all_gather | solution.py:462
  10.8 350.3 %all-gather.14.cloned.1.call-start = ((), (), s32[]{:S(2)}) async-start(), calls=%async_computation.8 | async-start | bytes 7077888 | tf_op jit(solution)/shard_map/all_gather | solution.py:96
  99.6 754.1 %copy-start.95 = (f32[1536]{0:T(1024)}, f32[1536]{0:T(1024)S(1)}, u32[]{:S(2)}) copy-start(f32[1536]{0:T(1024)S(1)} %get-tuple-element.171) | copy-start | bytes 18436
  99.6 776.9 %copy-start.97 = (f32[1536]{0:T(1024)}, f32[1536]{0:T(1024)S(1)}, u32[]{:S(2)}) copy-start(f32[1536]{0:T(1024)S(1)} %get-tuple-element.174) | copy-start | bytes 18436
  146.1 331.0 %copy-start.12 = (f32[2,128,1536]{2,1,0:T(8,128)}, f32[2,128,1536]{2,1,0:T(8,128)S(1)}, u32[]{:S(2)}) copy-start(f32[2,128,1536]{2,1,0:T(8,128)S(1)} %get-tuple-element.261) | copy-start | bytes 4718596
  237.0 224.8 %all-gather.12.cloned.1.call-start = ((), (), s32[]{:S(2)}) async-start(), calls=%async_computation.7 | async-start | bytes 7077888 | tf_op jit(solution)/shard_map/all_gather | solution.py:102
  239.6 438.7 %all-gather.18.cloned.1.call-start = ((), (), s32[]{:S(2)}) async-start(), calls=%async_computation.10 | async-start | bytes 38928384 | tf_op jit(solution)/shard_map/all_gather | solution.py:463
  242.8 561.7 %all-gather.20.cloned.1.call-start = ((), (), s32[]{:S(2)}) async-start(), calls=%async_computation.11 | async-start | bytes 19464192 | tf_op jit(solution)/shard_map/all_gather | solution.py:464
  243.8 668.8 %all-gather.22.cloned.1.call-start = ((), (), s32[]{:S(2)}) async-start(), calls=%async_computation.12 | async-start | bytes 7077888 | tf_op jit(solution)/shard_map/all_gather | solution.py:118
  289.4 718.0 %all-gather.24.cloned.1.call-start = ((), (), s32[]{:S(2)}) async-start(), calls=%async_computation.13 | async-start | bytes 7077888 | tf_op jit(solution)/shard_map/all_gather | solution.py:121
  882.6 389.6 %reduce-scatter.19.cloned.1.call-start = ((), (), s32[]{:S(2)}) async-start(), calls=%async_computation.19 | async-start | bytes 811008
  1069.0 230.3 %all-reduce.14.cloned.1.call-start = ((), (), s32[]{:S(2)}) async-start(), calls=%async_computation.20 | async-start | bytes 3145728
  1074.5 365.1 %reduce-scatter.11.cloned.1.call-start = ((), (), s32[]{:S(2)}) async-start(), calls=%async_computation.15 | async-start | bytes 9732096 | tf_op jit(solution)/shard_map/reduce_scatter | solution.py:496
  1083.0 459.3 %reduce-scatter.13.cloned.1.call-start = ((), (), s32[]{:S(2)}) async-start(), calls=%async_computation.16 | async-start | bytes 1622016 | tf_op jit(solution)/shard_map/reduce_scatter | solution.py:498
  1087.2 810.0 %reduce-scatter.17.cloned.1.call-start = ((), (), s32[]{:S(2)}) async-start(), calls=%async_computation.18 | async-start | bytes 38928384 | tf_op jit(solution)/shard_map/reduce_scatter | solution.py:282
  1104.6 1454.6 %reduce-scatter.9.cloned.1.call-start = ((), (), s32[]{:S(2)}) async-start(), calls=%async_computation.14 | async-start | bytes 77856768 | tf_op jit(solution)/shard_map/reduce_scatter | solution.py:495
  1239.8 1982.2 %reduce-scatter.15.cloned.1.call-start = ((), (), s32[]{:S(2)}) async-start(), calls=%async_computation.17 | async-start | bytes 77856768 | tf_op jit(solution)/shard_map/reduce_scatter | solution.py:291
  1271.2 2176.2 %all-reduce.24.cloned.1.call-start = ((), (), s32[]{:S(2)}) async-start(), calls=%async_computation.25 | async-start | bytes 12582912 | tf_op jit(solution)/shard_map/psum | solution.py:378
  2559.2 707.4 %copy-start.37 = (f32[6,1536,48]{1,0,2:T(8,128)S(1)}, f32[6,1536,48]{1,0,2:T(8,128)}, u32[]{:S(2)}) copy-start(f32[6,1536,48]{1,0,2:T(8,128)} %reduce-scatter.9.cloned.1.call-done) | copy-start | bytes 5308420
  3291.3 350.1 %all-reduce.22.cloned.1.call-start = ((), (), s32[]{:S(2)}) async-start(), calls=%async_computation.24 | async-start | bytes 12582912 | tf_op jit(solution)/shard_map/psum | solution.py:378
  3485.3 348.3 %all-reduce.20.cloned.1.call-start = ((), (), s32[]{:S(2)}) async-start(), calls=%async_computation.23 | async-start | bytes 12582912 | tf_op jit(solution)/shard_map/psum | solution.py:378
  3677.4 347.8 %all-reduce.18.cloned.1.call-start = ((), (), s32[]{:S(2)}) async-start(), calls=%async_computation.22 | async-start | bytes 12582912 | tf_op jit(solution)/shard_map/psum | solution.py:378
  3869.1 347.9 %all-reduce.16.cloned.1.call-start = ((), (), s32[]{:S(2)}) async-start(), calls=%async_computation.21 | async-start | bytes 12582912 | tf_op jit(solution)/shard_map/psum | solution.py:378
  (154 other events, 2924.1 us)
Sparse Core Ops, SparseCore 0:
  11.6 181.1 all-gather.9
  196.3 63.3 all-gather.15
  262.3 98.8 all-gather.13
  363.7 98.1 all-gather.11
  465.1 213.1 all-gather.17
  681.6 122.8 all-gather.19
  806.6 98.0 all-gather.21
  907.5 99.8 all-gather.23
  1069.1 93.8 reduce-scatter.18
  1168.1 131.1 all-reduce.13
  1305.2 134.3 reduce-scatter.10
  1446.1 96.1 reduce-scatter.12
  1549.9 347.3 reduce-scatter.16
  1903.5 655.6 reduce-scatter.8
  2566.6 655.4 reduce-scatter.14
  3291.4 156.0 all-reduce.23
  3485.4 155.9 all-reduce.21
  3677.6 155.9 all-reduce.19
  3869.3 155.9 all-reduce.17
  4061.1 155.9 all-reduce.15
where the time goes:
time: 4270 us; the launch traced here: 4260 us
  waiting for transfers between devices  3190 us (75%)
  matrix products  488 us (11%)
  blocking collectives  233 us (5%)
  local copies, waits for them, and re-layouts  194 us (5%)
  other arithmetic  128 us (3%)
    psum x5, waiting for transfers between devices, gram_sum(): return lax.psum((gram_of(first), gram_of(second)), ('seq', 'fsdp'))  764 us
    reduce_scatter x1, waiting for transfers between devices, body(): lax.psum_scatter(local_grads[0], ('seq', 'fsdp'), scatter_dimension=2, ti...  660 us
    reduce_scatter x1, waiting for transfers between devices, layer_backward(): lax.psum_scatter(rows_product(grad_both, normed_three), ('seq', 'fsdp'),...  657 us
    reduce_scatter x1, waiting for transfers between devices, layer_backward(): lax.psum_scatter(rows_product(inner_act, grad_branch), ('seq', 'fsdp'), s...  354 us
    all_gather x1, waiting for transfers between devices, body(): lax.all_gather(shards[2], ('seq', 'fsdp'), axis=0, tiled=True)  177 us
    reduce_scatter x1, waiting for transfers between devices, body(): lax.psum_scatter(local_grads[1], ('seq', 'fsdp'), scatter_dimension=2, ti...  139 us
    reduce_scatter x1, waiting for transfers between devices, body(): lax.psum_scatter(local_grads[3], ('seq', 'fsdp'), scatter_dimension=1, ti...  101 us
    all_gather x1, waiting for transfers between devices, body(): lax.all_gather(shards[3], ('seq', 'fsdp'), axis=0, tiled=True)  99.1 us
  transfers between devices with their start and end apart: 20, of which 18 were waited for; matrix products, arithmetic and copies ran while one was open for 12% of the time, Pallas kernels for 0%

commit v1 on v0

--- a/solution.py
+++ b/solution.py
@@ -3,6 +3,8 @@
 import jax
 import jax.numpy as jnp
 from jax import lax
+from jax.experimental import pallas as pl
+from jax.experimental.pallas import tpu as pltpu
 from jax.sharding import PartitionSpec as P
 
 D = 1536
@@ -555,7 +557,7 @@
     )
 
 
-def solution(mesh):
+def general(mesh):
     return jax.shard_map(
         body,
         mesh=mesh,
@@ -617,3 +619,551 @@
         ),
         check_vma=False,
     )
+
+
+LAYER = ("y", "f")
+ALL = ("z", "y", "f")
+RANKS = 8
+LOCAL_HEADS = HEADS // RANKS
+COLS = LOCAL_HEADS * HEAD_DIM
+LOW = jnp.bfloat16
+
+
+def attend_kernel(lengths_ref, q_ref, k_ref, v_ref, o_ref, lse_ref):
+    frames = q_ref.shape[1]
+    length = lengths_ref[pl.program_id(0) // LOCAL_HEADS]
+    keys = k_ref[0]
+    values = v_ref[0]
+    chunk = 256
+    live = lax.broadcasted_iota(jnp.int32, (chunk, frames), 1) < length
+    for part in range(frames // chunk):
+        rows = pl.ds(part * chunk, chunk)
+        scores = lax.dot_general(
+            q_ref[0, rows, :], keys, (((1,), (1,)), ((), ())), preferred_element_type=jnp.float32
+        ) * (1.0 / math.sqrt(HEAD_DIM))
+        scores = jnp.where(live, scores, -1e30)
+        top = jnp.max(scores, axis=1, keepdims=True)
+        grown = jnp.exp(scores - top)
+        total = jnp.sum(grown, axis=1, keepdims=True)
+        weights = (grown * (1.0 / total)).astype(LOW)
+        o_ref[0, rows, :] = jnp.dot(weights, values, preferred_element_type=jnp.float32)
+        lse_ref[0, rows, :] = top + jnp.log(total)
+
+
+def attend(queries, key_rows, values, lengths):
+    count, frames, width = queries.shape
+    block = pl.BlockSpec((1, frames, width), lambda i: (i, 0, 0))
+    return pl.pallas_call(
+        attend_kernel,
+        grid=(count,),
+        out_shape=(
+            jax.ShapeDtypeStruct((count, frames, width), jnp.float32),
+            jax.ShapeDtypeStruct((count, frames, 1), jnp.float32),
+        ),
+        in_specs=[pl.BlockSpec(memory_space=pltpu.SMEM), block, block, block],
+        out_specs=(block, pl.BlockSpec((1, frames, 1), lambda i: (i, 0, 0))),
+        compiler_params=pltpu.CompilerParams(vmem_limit_bytes=48 << 20),
+        cost_estimate=pl.CostEstimate(
+            flops=4 * count * frames * frames * width,
+            bytes_accessed=10 * count * frames * width,
+            transcendentals=count * frames * frames,
+        ),
+    )(lengths, queries, key_rows, values)
+
+
+def attend_back_kernel(
+    lengths_ref, q_ref, k_ref, v_ref, o_ref, lse_ref, do_ref, dq_ref, dk_ref, dv_ref
+):
+    frames = q_ref.shape[1]
+    length = lengths_ref[pl.program_id(0) // LOCAL_HEADS]
+    keys = k_ref[0]
+    values = v_ref[0]
+    chunk = 256
+    scale = 1.0 / math.sqrt(HEAD_DIM)
+    live = lax.broadcasted_iota(jnp.int32, (chunk, frames), 1) < length
+    grad_key = jnp.zeros((frames, HEAD_DIM), jnp.float32)
+    grad_value = jnp.zeros((frames, HEAD_DIM), jnp.float32)
+    for part in range(frames // chunk):
+        rows = pl.ds(part * chunk, chunk)
+        queries = q_ref[0, rows, :]
+        grads = do_ref[0, rows, :]
+        scores = (
+            lax.dot_general(
+                queries, keys, (((1,), (1,)), ((), ())), preferred_element_type=jnp.float32
+            )
+            * scale
+        )
+        scores = jnp.where(live, scores, -1e30)
+        weights = jnp.exp(scores - lse_ref[0, rows, :])
+        delta = jnp.sum(grads.astype(jnp.float32) * o_ref[0, rows, :], axis=1, keepdims=True)
+        pulled = lax.dot_general(
+            grads, values, (((1,), (1,)), ((), ())), preferred_element_type=jnp.float32
+        )
+        pushed = (weights * (pulled - delta)).astype(LOW)
+        dq_ref[0, rows, :] = jnp.dot(pushed, keys, preferred_element_type=jnp.float32) * scale
+        grad_key = grad_key + rows_product(pushed, queries)
+        grad_value = grad_value + rows_product(weights.astype(LOW), grads)
+    dk_ref[0] = grad_key * scale
+    dv_ref[0] = grad_value
+
+
+def attend_back(queries, key_rows, values, mixed, log_total, grads, lengths):
+    count, frames, width = queries.shape
+    block = pl.BlockSpec((1, frames, width), lambda i: (i, 0, 0))
+    shape = jax.ShapeDtypeStruct((count, frames, width), jnp.float32)
+    return pl.pallas_call(
+        attend_back_kernel,
+        grid=(count,),
+        out_shape=(shape,) * 3,
+        in_specs=[
+            pl.BlockSpec(memory_space=pltpu.SMEM),
+            block,
+            block,
+            block,
+            block,
+            pl.BlockSpec((1, frames, 1), lambda i: (i, 0, 0)),
+            block,
+        ],
+        out_specs=(block,) * 3,
+        compiler_params=pltpu.CompilerParams(vmem_limit_bytes=48 << 20),
+        cost_estimate=pl.CostEstimate(
+            flops=10 * count * frames * frames * width,
+            bytes_accessed=24 * count * frames * width,
+            transcendentals=count * frames * frames,
+        ),
+    )(lengths, queries, key_rows, values, mixed, log_total, grads)
+
+
+def cross_forward(cross_query, cross_key, cross_value):
+    probs = jax.nn.softmax(scores_of(cross_query, cross_key), axis=-1)
+    probs_low = probs.astype(LOW)
+    out = jnp.einsum("bhqk,bkhd->bqhd", probs_low, cross_value, preferred_element_type=jnp.float32)
+    return probs, probs_low, out
+
+
+def newton_products(gram):
+    trace = jnp.trace(gram, axis1=1, axis2=2)[:, None, None]
+    norm_value = jnp.sqrt(trace) + 1e-07
+    product = gram / (norm_value * norm_value)
+    eye = jnp.eye(HEAD_DIM, dtype=jnp.float32)[None]
+
+    def mul(left, right):
+        return jnp.einsum("bij,bjk->bik", left, right, precision=HIGHEST)
+
+    total = None
+    for newton_step in range(5):
+        mixer = NS_COEF[0] * eye + NS_COEF[1] * product + NS_COEF[2] * mul(product, product)
+        total = mixer if total is None else mul(mixer, total)
+        if newton_step < 4:
+            product = mul(mul(mixer, product), mixer)
+    return total / norm_value
+
+
+def fast_body(
+    latents,
+    gaussian_noise,
+    timesteps,
+    lengths,
+    buckets,
+    context,
+    attention_weights,
+    attention_moment,
+    cross_weights,
+    cross_moment,
+    gate_up_weights,
+    gate_up_first,
+    gate_up_second,
+    down_weights,
+    down_first,
+    down_second,
+    latent_weights,
+    latent_first,
+    latent_second,
+    timing_weights,
+    timing_first,
+    timing_second,
+    norm_params,
+    norm_first,
+    norm_second,
+):
+    f32 = jnp.float32
+    planes = lax.axis_size("z")
+    z_at = lax.axis_index("z")
+    rank = lax.axis_index("y") * lax.axis_size("f") + lax.axis_index("f")
+    item_count, span, latent_dim = latents.shape
+    frames = span * RANKS
+    tokens = item_count * span
+    group_tokens = item_count * frames
+    flip = lambda array: jnp.swapaxes(array, 1, 2)
+
+    attention_t = flip(attention_weights)
+    cross_t = flip(cross_weights)
+    attention_low = attention_t.astype(LOW)
+    cross_low_t = cross_t.astype(LOW)
+    small_low = jnp.concatenate(
+        [
+            latent_weights.reshape(-1, latent_weights.shape[2]),
+            timing_weights,
+            norm_params,
+        ],
+        axis=0,
+    ).astype(LOW)
+    small_all = lax.all_gather(small_low, ALL, axis=1, tiled=True)
+    latent_in = small_all[:LAT]
+    latent_out = small_all[LAT : 2 * LAT]
+    timing = small_all[2 * LAT : 2 * LAT + FOUR]
+    norms = small_all[2 * LAT + FOUR :].astype(f32)
+
+    meta = lax.all_gather(
+        jnp.stack([timesteps, lengths.astype(f32), buckets.astype(f32)]), "f", axis=1, tiled=True
+    )
+    times_all = meta[0]
+    lengths_all = meta[1]
+    onehot_all = (meta[2][:, None] == jnp.arange(NBUCK, dtype=f32)[None, :]).astype(f32)
+    counts = jnp.dot(lengths_all, onehot_all, precision=HIGHEST)
+    present = jnp.sum((counts > 0).astype(f32))
+    bucket_scale = 1.0 / (present * LAT * jnp.maximum(counts, 1.0))
+    own_at = z_at * item_count
+    onehot = lax.dynamic_slice_in_dim(onehot_all, own_at, item_count, 0)
+    item_scale = jnp.dot(onehot, bucket_scale, precision=HIGHEST)
+    own_lengths = lax.dynamic_slice_in_dim(lengths_all, own_at, item_count, 0).astype(jnp.int32)
+    features_all = time_features(times_all).astype(LOW)
+    features = lax.dynamic_slice_in_dim(features_all, own_at, item_count, 0)
+
+    signal = jnp.cos(0.5 * math.pi * timesteps)[:, None, None]
+    noise_level = jnp.sin(0.5 * math.pi * timesteps)[:, None, None]
+    noisy_own = (signal * latents + noise_level * gaussian_noise).astype(LOW)
+    target_own = signal * gaussian_noise - noise_level * latents
+    noisy_all = lax.all_gather(noisy_own, ALL, axis=0, tiled=False)
+    noisy_all = noisy_all.reshape(RANKS, planes, item_count, span, latent_dim)
+    noisy_low = jnp.swapaxes(
+        lax.dynamic_index_in_dim(noisy_all, z_at, 1, keepdims=False), 0, 1
+    ).reshape(item_count, frames, latent_dim)
+    target = lax.ppermute(
+        target_own, ALL, [(4 * s + g, RANKS * g + s) for s in range(RANKS) for g in range(planes)]
+    ).reshape(tokens, latent_dim)
+    context_all = lax.all_gather(context, "f", axis=0, tiled=True)
+    context_own = lax.dynamic_slice_in_dim(context_all, own_at, item_count, 0).reshape(-1, E)
+    context_len = context.shape[1]
+
+    qkv_slab = lax.all_to_all(attention_low[:3], LAYER, split_axis=2, concat_axis=1, tiled=True)
+    qkv_t = lax.all_gather(qkv_slab, "z", axis=1, tiled=True)
+    cross_slab = lax.all_to_all(cross_low_t, LAYER, split_axis=2, concat_axis=1, tiled=True)
+    cross_w = lax.all_gather(cross_slab, "z", axis=1, tiled=True)
+    rest_t = lax.all_gather(attention_low[3:], ALL, axis=1, tiled=True)
+    gate_up = lax.all_gather(gate_up_weights.astype(LOW), "z", axis=0, tiled=True)
+    down_pairs = []
+    for p in range(planes):
+        for r in range(RANKS):
+            down_pairs.append((2 * RANKS * (p // 2) + 2 * r + p % 2, RANKS * p + r))
+    down = lax.all_gather(
+        lax.ppermute(down_weights.astype(LOW), ALL, down_pairs), "z", axis=0, tiled=True
+    )
+
+    half_dim = HEAD_DIM // 2
+    inverse = 10000.0 ** (-jnp.arange(half_dim, dtype=f32) / half_dim)
+    angles = jnp.arange(frames, dtype=f32)[:, None] * inverse[None, :]
+    cosine = jnp.cos(angles)[None, None]
+    sine_table = jnp.sin(angles)[None, None]
+
+    timed = matmul_low(features, timing)
+    start_all = (
+        matmul_low(noisy_low.reshape(group_tokens, latent_dim), latent_in).reshape(
+            item_count, frames, D
+        )
+        + timed[:, None, :]
+    )
+    start_own = lax.dynamic_slice_in_dim(start_all, rank * span, span, 1).reshape(tokens, D)
+    noisy_mine = lax.dynamic_slice_in_dim(noisy_low, rank * span, span, 1).reshape(
+        tokens, latent_dim
+    )
+    normed_one, back_one = jax.vjp(
+        layer_norm, start_all.reshape(group_tokens, D), norms[0], norms[1]
+    )
+    normed_one = normed_one.astype(LOW)
+
+    def heads_of(flat):
+        return jnp.swapaxes(
+            flat.reshape(item_count, frames, LOCAL_HEADS, HEAD_DIM), 1, 2
+        )
+
+    def packed(heads):
+        return heads.reshape(item_count * LOCAL_HEADS, frames, HEAD_DIM)
+
+    def flat_of(heads):
+        return jnp.swapaxes(
+            heads.reshape(item_count, LOCAL_HEADS, frames, HEAD_DIM), 1, 2
+        ).reshape(group_tokens, COLS)
+
+    queries = packed(
+        rotate(heads_of(matmul_low(normed_one, qkv_t[0])), cosine, sine_table).astype(LOW)
+    )
+    key_rows = packed(
+        rotate(heads_of(matmul_low(normed_one, qkv_t[1])), cosine, sine_table).astype(LOW)
+    )
+    values = packed(heads_of(matmul_low(normed_one, qkv_t[2])).astype(LOW))
+    mixed, log_total = attend(queries, key_rows, values, own_lengths)
+
+    def to_tokens(flat):
+        moved = flat.reshape(item_count, RANKS, span, COLS)
+        return lax.all_to_all(moved, LAYER, split_axis=1, concat_axis=3, tiled=True).reshape(
+            tokens, D
+        )
+
+    def to_heads(flat):
+        moved = flat.reshape(item_count, 1, span, D)
+        return lax.all_to_all(moved, LAYER, split_axis=3, concat_axis=1, tiled=True).reshape(
+            group_tokens, COLS
+        )
+
+    mixed_low = to_tokens(flat_of(mixed.astype(LOW)))
+    after_self = start_own + matmul_low(mixed_low, rest_t[0])
+    normed_two, back_two = jax.vjp(layer_norm, after_self, norms[2], norms[3])
+    normed_two = normed_two.astype(LOW)
+    cross_query = (
+        matmul_low(normed_two, rest_t[1]).astype(LOW).reshape(item_count, span, HEADS, HEAD_DIM)
+    )
+    pair_own = jnp.stack(
+        [matmul_low(context_own, cross_w[0]), matmul_low(context_own, cross_w[1])]
+    ).astype(LOW)
+    pair_all = lax.all_gather(pair_own, LAYER, axis=2, tiled=True).reshape(
+        2, item_count, context_len, HEADS, HEAD_DIM
+    )
+    cross_key, cross_value = (pair_all[0], pair_all[1])
+    probs, probs_low, cross_mixed = cross_forward(cross_query, cross_key, cross_value)
+    cross_out = cross_mixed.reshape(tokens, D).astype(LOW)
+    after_cross = after_self + matmul_low(cross_out, rest_t[2])
+    normed_three, back_three = jax.vjp(layer_norm, after_cross, norms[4], norms[5])
+    normed_three = normed_three.astype(LOW)
+    normed_group = lax.all_gather(normed_three, LAYER, axis=0, tiled=True)
+    gate_both = times_transposed(normed_group, gate_up)
+    units = gate_both.shape[1] // 2
+    gate_half, up_half = (gate_both[:, :units], gate_both[:, units:])
+    inner_act = (jax.nn.silu(gate_half) * up_half).astype(LOW)
+    final_state = (
+        after_cross
+        + lax.psum_scatter(matmul_low(inner_act, down), LAYER, scatter_dimension=0, tiled=True)
+    ).astype(LOW)
+    predicted = times_transposed(final_state, latent_out)
+
+    position = rank * span + jnp.arange(span)
+    live_mask = position[None, :] < own_lengths[:, None]
+    difference = predicted - target
+    errors = jnp.sum(difference * difference, axis=1).reshape(item_count, span)
+    per_item = jnp.sum(jnp.where(live_mask, errors, 0.0), axis=1)
+    partial_loss = jnp.sum(per_item * item_scale)
+    frame_scale = jnp.where(live_mask, item_scale[:, None], 0.0).reshape(tokens, 1)
+    grad_pred = (2.0 * difference * frame_scale).astype(LOW)
+
+    grad_out_proj = rows_product(grad_pred, final_state)
+    grad_state = matmul_low(grad_pred, latent_out)
+    grad_group = lax.all_gather(grad_state.astype(LOW), LAYER, axis=0, tiled=True)
+    down_slab = lax.psum_scatter(
+        rows_product(inner_act, grad_group), "z", scatter_dimension=0, tiled=True
+    )
+    down_grad = lax.ppermute(down_slab, ALL, [(b, a) for a, b in down_pairs])
+    grad_inner = times_transposed(grad_group, down)
+    sigmoid_gate = jax.nn.sigmoid(gate_half)
+    grad_gate = grad_inner * up_half * sigmoid_gate * (1.0 + gate_half * (1.0 - sigmoid_gate))
+    grad_both = jnp.concatenate([grad_gate, grad_inner * gate_half * sigmoid_gate], axis=1).astype(
+        LOW
+    )
+    gate_up_grad = lax.psum_scatter(
+        rows_product(grad_both, normed_group), "z", scatter_dimension=0, tiled=True
+    )
+    grad_three = lax.psum_scatter(
+        matmul_low(grad_both, gate_up), LAYER, scatter_dimension=0, tiled=True
+    )
+    residual_part, gain_three, shift_three = back_three(grad_three)
+    grad_state = grad_state + residual_part
+    grad_branch = grad_state.astype(LOW)
+    grad_cross_out = rows_product(cross_out, grad_branch)
+    grad_mix = (
+        times_transposed(grad_branch, rest_t[2])
+        .astype(LOW)
+        .reshape(item_count, span, HEADS, HEAD_DIM)
+    )
+    grad_scores = jnp.einsum("bqhd,bkhd->bhqk", grad_mix, cross_value, preferred_element_type=f32)
+    grad_cross_value = jnp.einsum(
+        "bhqk,bqhd->bkhd", probs_low, grad_mix, preferred_element_type=f32
+    )
+    pushed = (probs * (grad_scores - jnp.sum(probs * grad_scores, axis=-1, keepdims=True))).astype(
+        LOW
+    )
+    score_scale = math.sqrt(HEAD_DIM)
+    grad_cross_query = (
+        (jnp.einsum("bhqk,bkhd->bqhd", pushed, cross_key, preferred_element_type=f32) / score_scale)
+        .astype(LOW)
+        .reshape(tokens, D)
+    )
+    grad_cross_key = (
+        jnp.einsum("bhqk,bqhd->bkhd", pushed, cross_query, preferred_element_type=f32) / score_scale
+    )
+    grad_pair = jnp.stack([grad_cross_key, grad_cross_value]).reshape(
+        2, item_count * context_len, D
+    )
+    grad_pair = lax.psum_scatter(grad_pair, LAYER, scatter_dimension=2, tiled=True)
+    grad_cross_w = jnp.einsum(
+        "te,ptc->pec", context_own.astype(f32), grad_pair, precision=HIGHEST
+    )
+    grad_cross_w = lax.psum_scatter(grad_cross_w, "z", scatter_dimension=1, tiled=True)
+    cross_grad = lax.all_to_all(grad_cross_w, LAYER, split_axis=1, concat_axis=2, tiled=True)
+    grad_cross_q = rows_product(normed_two, grad_cross_query)
+    residual_part, gain_two, shift_two = back_two(times_transposed(grad_cross_query, rest_t[1]))
+    grad_state = grad_state + residual_part
+    grad_branch = grad_state.astype(LOW)
+    grad_self_out = rows_product(mixed_low, grad_branch)
+    grad_mixed = times_transposed(grad_branch, rest_t[0]).astype(LOW)
+    rest_grad = lax.psum_scatter(
+        jnp.stack([grad_self_out, grad_cross_q, grad_cross_out]),
+        ALL,
+        scatter_dimension=1,
+        tiled=True,
+    )
+    grad_mixed = packed(heads_of(to_heads(grad_mixed)))
+    grad_query, grad_key, grad_value = attend_back(
+        queries, key_rows, values, mixed, log_total, grad_mixed, own_lengths
+    )
+    unpacked = lambda heads: heads.reshape(item_count, LOCAL_HEADS, frames, HEAD_DIM)
+    grad_triple = [
+        flat_of(rotate(unpacked(grad_query), cosine, -sine_table).astype(LOW)),
+        flat_of(rotate(unpacked(grad_key), cosine, -sine_table).astype(LOW)),
+        flat_of(grad_value.astype(LOW)),
+    ]
+    qkv_grad = jnp.stack([rows_product(normed_one, part) for part in grad_triple])
+    qkv_grad = lax.psum_scatter(qkv_grad, "z", scatter_dimension=1, tiled=True)
+    qkv_grad = lax.all_to_all(qkv_grad, LAYER, split_axis=1, concat_axis=2, tiled=True)
+    grad_one = sum(times_transposed(part, qkv_t[i]) for i, part in enumerate(grad_triple))
+    residual_part, gain_one, shift_one = back_one(grad_one)
+    grad_in_proj = rows_precise(
+        noisy_low.reshape(group_tokens, latent_dim).astype(f32), residual_part
+    ) + rows_precise(noisy_mine.astype(f32), grad_state)
+    grad_timed = jnp.sum(residual_part.reshape(item_count, frames, D), axis=1) + jnp.sum(
+        grad_state.reshape(item_count, span, D), axis=1
+    )
+    timed_slots = lax.dynamic_update_slice(
+        jnp.zeros((item_count * planes, D), f32), grad_timed, (own_at, 0)
+    )
+    small_grad = jnp.concatenate(
+        [
+            grad_in_proj,
+            grad_out_proj,
+            jnp.stack([gain_one, shift_one, gain_two, shift_two, gain_three, shift_three]),
+            timed_slots,
+        ],
+        axis=0,
+    )
+    small_grad = lax.psum_scatter(small_grad, ALL, scatter_dimension=1, tiled=True)
+    latent_grad = small_grad[: 2 * LAT].reshape(2, LAT, -1)
+    norm_grad = small_grad[2 * LAT : 2 * LAT + 6]
+    timing_grad = rows_precise(features_all.astype(f32), small_grad[2 * LAT + 6 :])
+    attention_grad = jnp.concatenate([qkv_grad, rest_grad], axis=0)
+
+    everything = (
+        attention_grad,
+        cross_grad,
+        latent_grad,
+        timing_grad,
+        norm_grad,
+        gate_up_grad,
+        down_grad,
+    )
+    squares = sum((jnp.sum(grad * grad) for grad in everything))
+    squares, loss_value = lax.psum((squares, partial_loss), ALL)
+    clip_norm = jnp.sqrt(squares)
+    factor = CLIP_AT / jnp.maximum(clip_norm, CLIP_AT)
+
+    moment_t = 0.95 * flip(attention_moment) + attention_grad * factor
+    cross_moment_t = 0.95 * flip(cross_moment) + cross_grad * factor
+    blocks = [
+        moment.reshape(moment.shape[0], moment.shape[1], D // HEAD_DIM, HEAD_DIM)
+        for moment in (moment_t, cross_moment_t)
+    ]
+    grams = jnp.concatenate(
+        [
+            jnp.einsum("skbi,skbj->sbij", block, block, precision=HIGHEST).reshape(
+                -1, HEAD_DIM, HEAD_DIM
+            )
+            for block in blocks
+        ]
+    )
+    mixers = newton_products(lax.psum_scatter(grams, ALL, scatter_dimension=0, tiled=True))
+    mixers = lax.all_gather(mixers, ALL, axis=0, tiled=True).reshape(
+        -1, D // HEAD_DIM, HEAD_DIM, HEAD_DIM
+    )
+    stacks = attention_t.shape[0]
+    orth = [
+        jnp.einsum("skbj,sbji->skbi", block, mixer, precision=HIGHEST).reshape(moment.shape)
+        for block, mixer, moment in zip(
+            blocks, (mixers[:stacks], mixers[stacks:]), (moment_t, cross_moment_t)
+        )
+    ]
+    attention_new = attention_t * (1.0 - MUON_RATE * DECAY_RATE) - MUON_RATE * orth[0]
+    cross_new = cross_t * (1.0 - MUON_RATE * DECAY_RATE) - MUON_RATE * orth[1]
+    gate_up_new, gate_up_first_new, gate_up_second_new = adam_update(
+        gate_up_weights, gate_up_first, gate_up_second, gate_up_grad * factor, ADAM_RATE, DECAY_RATE
+    )
+    down_new, down_first_new, down_second_new = adam_update(
+        down_weights, down_first, down_second, down_grad * factor, ADAM_RATE, DECAY_RATE
+    )
+    latent_new, latent_first_new, latent_second_new = adam_update(
+        latent_weights, latent_first, latent_second, latent_grad * factor, ADAM_RATE, DECAY_RATE
+    )
+    timing_new, timing_first_new, timing_second_new = adam_update(
+        timing_weights, timing_first, timing_second, timing_grad * factor, ADAM_RATE, DECAY_RATE
+    )
+    norm_new, norm_first_new, norm_second_new = adam_update(
+        norm_params, norm_first, norm_second, norm_grad * factor, GAIN_RATE, 0.0
+    )
+    return (
+        loss_value,
+        clip_norm,
+        flip(attention_new),
+        flip(moment_t),
+        flip(attention_new.astype(LOW)),
+        flip(cross_new),
+        flip(cross_moment_t),
+        flip(cross_new.astype(LOW)),
+        gate_up_new,
+        gate_up_first_new,
+        gate_up_second_new,
+        gate_up_new.astype(LOW),
+        down_new,
+        down_first_new,
+        down_second_new,
+        down_new.astype(LOW),
+        latent_new,
+        latent_first_new,
+        latent_second_new,
+        latent_new.astype(LOW),
+        timing_new,
+        timing_first_new,
+        timing_second_new,
+        timing_new.astype(LOW),
+        norm_new,
+        norm_first_new,
+        norm_second_new,
+    )
+
+
+def solution(mesh):
+    if tuple(mesh.devices.shape) != (RANKS, 4):
+        return general(mesh)
+    mesh3 = jax.sharding.Mesh(mesh.devices.reshape(4, 2, 4), ALL)
+    seq = ("z", "y")
+    row = P(ALL, None)
+    col2 = P(None, ALL)
+    col3 = P(None, None, ALL)
+    return jax.shard_map(
+        fast_body,
+        mesh=mesh3,
+        in_specs=(P("f", seq, None),) * 2
+        + (P("f"),) * 3
+        + (P("f", None, None),)
+        + (col3,) * 4
+        + (row,) * 6
+        + (col3,) * 3
+        + (col2,) * 6,
+        out_specs=(P(),) * 2 + (col3,) * 6 + (row,) * 8 + (col3,) * 4 + (col2,) * 7,
+        check_vma=False,
+    )

time: 4270 us -> 1940 us (0.45)
  waiting for transfers between devices: 3190 us -> 1210 us
  matrix products: 488 us -> 225 us
  blocking collectives: 233 us -> 99.9 us
  starting transfers between devices: 1.45 us -> 51.3 us
    reduce_scatter x5 -> x8, waiting for transfers between devices: 1910 us -> 676 us  [the longest x1 261 us: fast_body(): lax.psum_scatter(jnp.stack([grad_self_out, grad_cross_q, grad_cross_out])...]
    psum x5 -> x0, waiting for transfers between devices: 764 us -> none  [gram_sum(): return lax.psum((gram_of(first), gram_of(second)), ('seq', 'fsdp'))]
    dot_general x42 -> x29, matrix products: 257 us -> 40.2 us  [the longest x2 12.2 us: fast_body(): jnp.einsum('skbi,skbj->sbij', block, block, precision=HIGHEST)]
    all_gather x5 -> x2, blocking collectives: 186 us -> 26.7 us  [the longest x1 21.1 us: fast_body(): cross_w = lax.all_gather(cross_slab, 'z', axis=1, tiled=True)]
    all_gather x8 -> x11, waiting for transfers between devices: 491 us -> 390 us  [the longest x1 64.9 us: fast_body(): lax.all_gather(gate_up_weights.astype(LOW), 'z', axis=0, tiled=True)]
    unnamed x22 -> x23, waiting for transfers between devices: 26 us -> 103 us
    concatenate x1 -> x2, local copies, waits for them, and re-layouts: 67.5 us -> 1.63 us  [the longest x1 1.23 us: fast_body(): attention_grad = jnp.concatenate([qkv_grad, rest_grad], axis=0)]
    all_to_all x0 -> x4, starting transfers between devices: none -> 44.1 us  [the longest x1 32.2 us: fast_body(): lax.all_to_all(qkv_grad, LAYER, split_axis=1, concat_axis=2, tiled=True)]
  transfers between devices with their start and end apart: 20 -> 28, of which waited for: 18 -> 18; matrix products, arithmetic and copies ran while one was open for 12% -> 18% of each run, Pallas kernels for 0% -> 2%
where the time goes in v1:
time: 1940 us; the launch traced here: 1930 us
  waiting for transfers between devices  1210 us (62%)
  matrix products  225 us (12%)
  local copies, waits for them, and re-layouts  154 us (8%)
  other arithmetic  125 us (6%)
  blocking collectives  99.9 us (5%)
  starting transfers between devices  51.3 us (3%)
  Pallas kernels  39.7 us (2%)
  between operations  23.4 us (1%)
    reduce_scatter x1, waiting for transfers between devices, fast_body(): lax.psum_scatter(jnp.stack([grad_self_out, grad_cross_q, grad_cross_out])...  261 us
    reduce_scatter x1, waiting for transfers between devices, fast_body(): lax.psum_scatter(rows_product(grad_both, normed_group), 'z', scatter_dime...  121 us
    reduce_scatter x1, waiting for transfers between devices, fast_body(): lax.psum_scatter(grams, ALL, scatter_dimension=0, tiled=True)  113 us
    unnamed x23, waiting for transfers between devices  103 us
    reduce_scatter x1, waiting for transfers between devices, fast_body(): lax.psum_scatter(matmul_low(grad_both, gate_up), LAYER, scatter_dimension...  92.3 us
    reduce_scatter x1, waiting for transfers between devices, fast_body(): lax.psum_scatter(matmul_low(inner_act, down), LAYER, scatter_dimension=0,...  88.2 us
    dot_general x9, matrix products, times_transposed(): lax.dot_general(left, weight, (((left.ndim - 1,), (1,)), ((), ())), prefe...  72.3 us
    all_gather x1, waiting for transfers between devices, fast_body(): lax.all_gather(gate_up_weights.astype(LOW), 'z', axis=0, tiled=True)  64.9 us
  transfers between devices with their start and end apart: 28, of which 18 were waited for; matrix products, arithmetic and copies ran while one was open for 18% of the time, Pallas kernels for 2%

profile of v1, /device:TPU:0, one launch (start us, length us, event | category | flops | bytes accessed | tf_op | source)
XLA Modules:
  0.0 1928.6 jit_solution(4128857749223006988)
XLA Ops:
  19.1 17.0 all_to_all.93
  54.9 21.1 %all_gather.49 = bf16[2,768,192]{2,1,0:T(8,128)(2,1)S(1)} all-gather(bf16[2,192,192]{2,1,0:T(8,128)(2,1)S(1)} %bitcast.510), channel_id=1, replica_groups=mesh['z'=4,'y'=2,'f'=4] {'z'}, dimensions={1}, use_global_device_ids=true | all-gather | bytes 737280 | tf_op jit(solution)/shard_map/all_gather | solution.py:852
  98.5 51.9 %all-gather.34.cloned.1.call-done = bf16[64,128,64]{1,2,0:T(8,128)(2,1)} async-done(((bf16[2,128,64]{1,2,0:T(8,128)(2,1)}), bf16[64,128,64]{1,2,0:T(8,128)(2,1)}) %all-gather.34.cloned.1.call-update) | async-done | bytes 1048592 | tf_op jit(solution)/shard_map/all_gather | solution.py:837
  162.4 39.5 %all-gather.16.cloned.1.call-done = bf16[3,1536,192]{2,1,0:T(8,128)(2,1)} async-done(((bf16[3,384,192]{2,1,0:T(8,128)(2,1)}), bf16[3,1536,192]{2,1,0:T(8,128)(2,1)}) %all-gather.16.cloned.1.call-update) | async-done | bytes 1769488 | tf_op jit(solution)/shard_map/all_gather | solution.py:850
  235.1 17.5 shard_map.448
  265.1 18.4 all-to-all-done.1
  292.3 51.5 %all-gather.18.cloned.1.call-done = bf16[3,1536,1536]{2,1,0:T(8,128)(2,1)} async-done(((bf16[3,48,1536]{2,1,0:T(8,128)(2,1)}), bf16[3,1536,1536]{2,1,0:T(8,128)(2,1)}) %all-gather.18.cloned.1.call-update) | async-done | bytes 14155792 | tf_op jit(solution)/shard_map/all_gather | solution.py:853
  372.8 64.9 %all-gather.26.cloned.1.call-done = bf16[1536,1536]{1,0:T(8,128)(2,1)} async-done(((bf16[384,1536]{1,0:T(8,128)(2,1)}), bf16[1536,1536]{1,0:T(8,128)(2,1)}) %all-gather.26.cloned.1.call-update) | async-done | bytes 4718608 | tf_op jit(solution)/shard_map/all_gather | solution.py:854
  437.7 48.4 %all-gather.24.cloned.1.call-done = bf16[2048,1536]{1,0:T(8,128)(2,1)} async-done(((bf16[256,1536]{1,0:T(8,128)(2,1)}), bf16[2048,1536]{1,0:T(8,128)(2,1)}) %all-gather.24.cloned.1.call-update) | async-done | bytes 6291472 | tf_op jit(solution)/shard_map/all_gather | solution.py:938
  507.3 30.9 %all-gather.28.cloned.1.call-done = bf16[768,1536]{1,0:T(8,128)(2,1)} async-done(((bf16[192,1536]{1,0:T(8,128)(2,1)}), bf16[768,1536]{1,0:T(8,128)(2,1)}) %all-gather.28.cloned.1.call-update) | async-done | bytes 2359312 | tf_op jit(solution)/shard_map/all_gather | solution.py:859
  551.5 88.2 %reduce-scatter.15.cloned.1.call-done = f32[256,1536]{1,0:T(8,128)} async-done(((f32[2048,1536]{1,0:T(8,128)}), f32[256,1536]{1,0:T(8,128)}) %reduce-scatter.15.cloned.1.call-update) | async-done | bytes 1572880 | tf_op jit(solution)/shard_map/reduce_scatter | solution.py:945
  645.8 45.4 %all-gather.30.cloned.1.call-done = bf16[2048,1536]{1,0:T(8,128)(2,1)} async-done(((bf16[256,1536]{1,0:T(8,128)(2,1)}), bf16[2048,1536]{1,0:T(8,128)(2,1)}) %all-gather.30.cloned.1.call-update) | async-done | bytes 6291472 | tf_op jit(solution)/shard_map/all_gather | solution.py:960
  721.2 92.3 %reduce-scatter.17.cloned.1.call-done = f32[256,1536]{1,0:T(8,128)} async-done(((f32[2048,1536]{1,0:T(8,128)}), f32[256,1536]{1,0:T(8,128)}) %reduce-scatter.17.cloned.1.call-update) | async-done | bytes 1572880 | tf_op jit(solution)/shard_map/reduce_scatter | solution.py:974
  900.3 22.2 %shard_map.449 = (f32[6,1024,64]{2,1,0:T(8,128)}, f32[6,1024,64]{2,1,0:T(8,128)}, f32[6,1024,64]{2,1,0:T(8,128)}) custom-call(s32[2]{0:T(128)S(1)} %fusion.122.lengths_ref, bf16[6,1024,64]{2,1,0:T(8,128)(2,1)S(1)} %copy-done.3, bf16[6,1024,64]{2,1,0:T(8,128)(2,1)S(1)} %copy-done.1, bf16[6,1024,64]{2,1,0:T(8,128)(2,1)S(1)} %bitcast.455, ...), custom_call_target="tpu_custom_call" | custom-call | flops 4026531840 | bytes 9437184 | tf_op jit(solution)/shard_map/pallas_call | solution.py:714
  1018.8 18.2 multiply_reduce_fusion
  1057.1 21.0 %pad_maximum_fusion = f32[3,1536,1536]{2,1,0:T(8,128)} fusion(f32[1,1536,1536]{2,1,0:T(8,128)} %convolution_bitcast_fusion, f32[1,1536,1536]{2,1,0:T(8,128)} %convolution_bitcast_fusion.1, f32[1,1536,1536]{2,1,0:T(8,128)} %convolution_bitcast_fusion.2), kind=kLoop, calls=%fused_computation.1 | loop fusion | flops 14155776 | bytes 56623104 | tf_op jit(solution)/shard_map/stack | solution.py:1018
  1091.1 17.6 all-to-all-done.5
  1108.8 32.2 %all-to-all-start.4 = ((f32[3,384,192]{2,0,1:T(4,128)}), f32[3,384,192]{2,0,1:T(4,128)S(1)}, u32[]{:S(2)}, u32[]{:S(2)}) async-start(f32[3,384,192]{2,0,1:T(4,128)} %copy.398), calls=%async_computation.7 | async-start | bytes 3145728 | tf_op jit(solution)/shard_map/all_to_all | solution.py:1035
  1141.0 121.5 %reduce-scatter.25.cloned.1.call-done = f32[384,1536]{1,0:T(8,128)} async-done(((f32[1536,1536]{1,0:T(8,128)}), f32[384,1536]{1,0:T(8,128)}) %reduce-scatter.25.cloned.1.call-update) | async-done | bytes 2359312 | tf_op jit(solution)/shard_map/reduce_scatter | solution.py:971
  1265.4 101.3 %reduce-scatter.33.cloned.1.call-done = f32[48,142]{1,0:T(8,128)} async-done(((f32[1536,142]{1,0:T(8,128)}), f32[48,142]{1,0:T(8,128)}) %reduce-scatter.33.cloned.1.call-update) | async-done | bytes 27280
  1374.2 261.1 %reduce-scatter.21.cloned.1.call-done = f32[3,48,1536]{2,1,0:T(8,128)} async-done(((f32[3,1536,1536]{2,1,0:T(8,128)}), f32[3,48,1536]{2,1,0:T(8,128)}) %reduce-scatter.21.cloned.1.call-update) | async-done | bytes 884752 | tf_op jit(solution)/shard_map/reduce_scatter | solution.py:1017
  1642.1 40.5 %all-reduce = (f32[]{:T(128)}, f32[]{:T(128)}) all-reduce(f32[]{:T(128)} %multiply_reduce_fusion.20, f32[]{:T(128)S(6)} %add.391), channel_id=1, replica_groups=mesh['z'=4,'y'=2,'f'=4] {'z','y','f'}, use_global_device_ids=true, to_apply=%region_13.14 | all-reduce | flops 2 | bytes 16 | tf_op jit(solution)/shard_map/psum | solution.py:1072
  1708.3 113.3 %reduce-scatter.29.cloned.1.call-done = f32[6,64,64]{2,1,0:T(8,128)} async-done(((f32[192,64,64]{2,1,0:T(8,128)}), f32[6,64,64]{2,1,0:T(8,128)}) %reduce-scatter.29.cloned.1.call-update) | async-done | bytes 98320 | tf_op jit(solution)/shard_map/reduce_scatter | solution.py:1090
  1848.9 51.2 %all-gather.32.cloned.1.call-done = f32[192,64,64]{2,1,0:T(8,128)} async-done(((f32[6,64,64]{2,1,0:T(8,128)}), f32[192,64,64]{2,1,0:T(8,128)}) %all-gather.32.cloned.1.call-update) | async-done | bytes 3145744 | tf_op jit(solution)/shard_map/all_gather | solution.py:1091
  (552 shorter events, 517.9 us)
Async XLA Ops:
  7.2 68.8 %all-gather.20.cloned.1.call-start = ((), (), s32[]{:S(2)}) async-start(), calls=%async_computation.19 | async-start | bytes 1966080 | tf_op jit(solution)/shard_map/all_gather | solution.py:845
  7.9 86.5 %all-gather.14.cloned.1.call-start = ((), (), s32[]{:S(2)}) async-start(), calls=%async_computation.16 | async-start | bytes 1622016 | tf_op jit(solution)/shard_map/all_gather | solution.py:811
  11.2 139.3 %all-gather.34.cloned.1.call-start = ((), (), s32[]{:S(2)}) async-start(), calls=%async_computation.34 | async-start | bytes 1081344 | tf_op jit(solution)/shard_map/all_gather | solution.py:837
  13.5 188.4 %all-gather.16.cloned.1.call-start = ((), (), s32[]{:S(2)}) async-start(), calls=%async_computation.17 | async-start | bytes 2949120 | tf_op jit(solution)/shard_map/all_gather | solution.py:850
  46.9 237.4 %all-gather.22.cloned.1.call-start = ((), (), s32[]{:S(2)}) async-start(), calls=%async_computation.20 | async-start | bytes 1769472 | tf_op jit(solution)/shard_map/all_gather | solution.py:929
  78.9 264.9 %all-gather.18.cloned.1.call-start = ((), (), s32[]{:S(2)}) async-start(), calls=%async_computation.18 | async-start | bytes 14598144 | tf_op jit(solution)/shard_map/all_gather | solution.py:853
  79.5 358.2 %all-gather.26.cloned.1.call-start = ((), (), s32[]{:S(2)}) async-start(), calls=%async_computation.22 | async-start | bytes 5898240 | tf_op jit(solution)/shard_map/all_gather | solution.py:854
  262.2 223.9 %all-gather.24.cloned.1.call-start = ((), (), s32[]{:S(2)}) async-start(), calls=%async_computation.21 | async-start | bytes 7077888 | tf_op jit(solution)/shard_map/all_gather | solution.py:938
  369.4 168.8 %all-gather.28.cloned.1.call-start = ((), (), s32[]{:S(2)}) async-start(), calls=%async_computation.23 | async-start | bytes 2949120 | tf_op jit(solution)/shard_map/all_gather | solution.py:859
  372.3 267.4 %reduce-scatter.15.cloned.1.call-start = ((), (), s32[]{:S(2)}) async-start(), calls=%async_computation.24 | async-start | bytes 14155776 | tf_op jit(solution)/shard_map/reduce_scatter | solution.py:945
  548.3 143.0 %all-gather.30.cloned.1.call-start = ((), (), s32[]{:S(2)}) async-start(), calls=%async_computation.25 | async-start | bytes 7077888 | tf_op jit(solution)/shard_map/all_gather | solution.py:960
  549.1 92.5 %collective-permute-start.1 = (f32[2,128,64]{1,2,0:T(8,128)S(1)}, f32[2,128,64]{1,2,0:T(8,128)S(1)}, u32[]{:S(2)}, u32[]{:S(2)}) collective-permute-start(f32[2,128,64]{1,2,0:T(8,128)S(1)} %copy-done.84), channel_id=1, source_target_pairs={{0,0},{1,8},{2,16},{3,24},{4,1},{5,9},{6,17},{7,25},{8,2},{9,10},{... | collective-permute-start | bytes 196616 | tf_op jit(solution)/shard_map/ppermute | solution.py:842
  645.6 167.9 %reduce-scatter.17.cloned.1.call-start = ((), (), s32[]{:S(2)}) async-start(), calls=%async_computation.26 | async-start | bytes 14155776 | tf_op jit(solution)/shard_map/reduce_scatter | solution.py:974
  721.0 229.3 %reduce-scatter.23.cloned.1.call-start = ((), (), s32[]{:S(2)}) async-start(), calls=%async_computation.29 | async-start | bytes 3538944 | tf_op jit(solution)/shard_map/reduce_scatter | solution.py:1005
  851.0 227.1 %reduce-scatter.27.cloned.1.call-start = ((), (), s32[]{:S(2)}) async-start(), calls=%async_computation.31 | async-start | bytes 5898240 | tf_op jit(solution)/shard_map/reduce_scatter | solution.py:961
  861.0 219.2 %reduce-scatter.31.cloned.1.call-start = ((), (), s32[]{:S(2)}) async-start(), calls=%async_computation.35 | async-start | bytes 1474560
  955.1 133.5 %reduce-scatter.19.cloned.1.call-start = ((), (), s32[]{:S(2)}) async-start(), calls=%async_computation.27 | async-start | bytes 4423680 | tf_op jit(solution)/shard_map/reduce_scatter | solution.py:1034
  966.5 296.1 %reduce-scatter.25.cloned.1.call-start = ((), (), s32[]{:S(2)}) async-start(), calls=%async_computation.30 | async-start | bytes 11796480 | tf_op jit(solution)/shard_map/reduce_scatter | solution.py:971
  983.2 383.5 %reduce-scatter.33.cloned.1.call-start = ((), (), s32[]{:S(2)}) async-start(), calls=%async_computation.36 | async-start | bytes 1622016
  1057.0 578.3 %reduce-scatter.21.cloned.1.call-start = ((), (), s32[]{:S(2)}) async-start(), calls=%async_computation.28 | async-start | bytes 29196288 | tf_op jit(solution)/shard_map/reduce_scatter | solution.py:1017
  1082.3 26.5 %all-to-all-start.5 = ((f32[2,192,192]{2,0,1:T(2,128)}), f32[2,192,192]{2,0,1:T(2,128)S(1)}, u32[]{:S(2)}, u32[]{:S(2)}) async-start(f32[2,192,192]{2,0,1:T(2,128)} %bitcast.114), calls=%async_computation.10 | async-start | bytes 786432 | tf_op jit(solution)/shard_map/all_to_all | solution.py:1010
  1108.8 264.0 %all-to-all-start.4 = ((f32[3,384,192]{2,0,1:T(4,128)}), f32[3,384,192]{2,0,1:T(4,128)S(1)}, u32[]{:S(2)}, u32[]{:S(2)}) async-start(f32[3,384,192]{2,0,1:T(4,128)} %copy.398), calls=%async_computation.7 | async-start | bytes 3145728 | tf_op jit(solution)/shard_map/all_to_all | solution.py:1035
  1141.0 680.6 %reduce-scatter.29.cloned.1.call-start = ((), (), s32[]{:S(2)}) async-start(), calls=%async_computation.32 | async-start | bytes 6488064 | tf_op jit(solution)/shard_map/reduce_scatter | solution.py:1090
  1707.5 192.6 %all-gather.32.cloned.1.call-start = ((), (), s32[]{:S(2)}) async-start(), calls=%async_computation.33 | async-start | bytes 6488064 | tf_op jit(solution)/shard_map/all_gather | solution.py:1091
  (126 other events, 2106.0 us)
Sparse Core Ops, SparseCore 0:
  9.6 25.6 all-gather.19
  38.7 55.6 all-gather.13
  97.9 52.5 all-gather.33
  152.4 49.3 all-gather.15
  204.2 24.5 all-gather.21
  232.2 111.5 all-gather.17
  345.9 91.7 all-gather.25
  440.2 45.8 all-gather.23
  487.7 50.4 all-gather.27
  548.4 91.2 reduce-scatter.14
  645.7 45.4 all-gather.29
  721.1 92.3 reduce-scatter.16
  851.1 46.9 reduce-scatter.22
  900.4 85.2 reduce-scatter.26
  988.5 29.6 reduce-scatter.30
  1020.5 65.0 reduce-scatter.18
  1087.9 174.5 reduce-scatter.24
  1269.0 97.6 reduce-scatter.32
  1374.3 260.9 reduce-scatter.20
  1707.6 113.9 reduce-scatter.28
  1831.3 68.7 all-gather.31

commit v2 on v1

--- a/solution.py
+++ b/solution.py
@@ -629,126 +629,505 @@
 LOW = jnp.bfloat16
 
 
-def attend_kernel(lengths_ref, q_ref, k_ref, v_ref, o_ref, lse_ref):
-    frames = q_ref.shape[1]
-    length = lengths_ref[pl.program_id(0) // LOCAL_HEADS]
-    keys = k_ref[0]
-    values = v_ref[0]
-    chunk = 256
-    live = lax.broadcasted_iota(jnp.int32, (chunk, frames), 1) < length
-    for part in range(frames // chunk):
-        rows = pl.ds(part * chunk, chunk)
-        scores = lax.dot_general(
-            q_ref[0, rows, :], keys, (((1,), (1,)), ((), ())), preferred_element_type=jnp.float32
-        ) * (1.0 / math.sqrt(HEAD_DIM))
-        scores = jnp.where(live, scores, -1e30)
-        top = jnp.max(scores, axis=1, keepdims=True)
-        grown = jnp.exp(scores - top)
-        total = jnp.sum(grown, axis=1, keepdims=True)
-        weights = (grown * (1.0 / total)).astype(LOW)
-        o_ref[0, rows, :] = jnp.dot(weights, values, preferred_element_type=jnp.float32)
-        lse_ref[0, rows, :] = top + jnp.log(total)
-
-
-def attend(queries, key_rows, values, lengths):
-    count, frames, width = queries.shape
-    block = pl.BlockSpec((1, frames, width), lambda i: (i, 0, 0))
+MESH = pl.DeviceIdType.MESH
+
+
+def place():
+    at = lax.axis_index("f")
+    return lax.axis_index("z"), lax.axis_index("y"), at // 2, at % 2
+
+
+def turned(me, flip):
+    z_at, y_at, x_at, core = me
+    low = z_at % 2
+    high = z_at // 2
+    low = 1 - low if flip[0] & 1 else low
+    high = 1 - high if flip[0] & 2 else high
+    return (
+        2 * high + low,
+        1 - y_at if flip[1] else y_at,
+        1 - x_at if flip[2] else x_at,
+        1 - core if flip[3] else core,
+    )
+
+
+def device_of(where):
+    return (where[0], where[1], 2 * where[2] + where[3])
+
+
+def rank_of(where):
+    return 4 * where[1] + 2 * where[2] + where[3]
+
+
+def greet(peers):
+    barrier = pltpu.get_barrier_semaphore()
+    for peer in peers:
+        pl.semaphore_signal(barrier, inc=1, device_id=device_of(peer), device_id_type=MESH)
+    pl.semaphore_wait(barrier, len(peers))
+
+
+LAYER_FLIPS = [(0, y, x, c) for y in range(2) for x in range(2) for c in range(2)][1:]
+
+
+def comm_call(kernel, out_shape, arrays, scratch, ident, vmem=False, cost_us=20):
+    spec = pl.BlockSpec(memory_space=pl.ANY)
     return pl.pallas_call(
-        attend_kernel,
-        grid=(count,),
-        out_shape=(
-            jax.ShapeDtypeStruct((count, frames, width), jnp.float32),
-            jax.ShapeDtypeStruct((count, frames, 1), jnp.float32),
+        kernel,
+        out_shape=out_shape,
+        in_specs=[spec] * len(arrays),
+        out_specs=jax.tree.map(lambda _: spec, out_shape),
+        scratch_shapes=scratch,
+        compiler_params=pltpu.CompilerParams(
+            collective_id=ident, has_side_effects=True, vmem_limit_bytes=(40 << 20) if vmem else None
         ),
-        in_specs=[pl.BlockSpec(memory_space=pltpu.SMEM), block, block, block],
-        out_specs=(block, pl.BlockSpec((1, frames, 1), lambda i: (i, 0, 0))),
-        compiler_params=pltpu.CompilerParams(vmem_limit_bytes=48 << 20),
         cost_estimate=pl.CostEstimate(
-            flops=4 * count * frames * frames * width,
-            bytes_accessed=10 * count * frames * width,
-            transcendentals=count * frames * frames,
+            flops=cost_us * 10**9, bytes_accessed=1 << 20, transcendentals=0
         ),
-    )(lengths, queries, key_rows, values)
-
-
-def attend_back_kernel(
-    lengths_ref, q_ref, k_ref, v_ref, o_ref, lse_ref, do_ref, dq_ref, dk_ref, dv_ref
-):
-    frames = q_ref.shape[1]
-    length = lengths_ref[pl.program_id(0) // LOCAL_HEADS]
-    keys = k_ref[0]
-    values = v_ref[0]
-    chunk = 256
-    scale = 1.0 / math.sqrt(HEAD_DIM)
-    live = lax.broadcasted_iota(jnp.int32, (chunk, frames), 1) < length
-    grad_key = jnp.zeros((frames, HEAD_DIM), jnp.float32)
-    grad_value = jnp.zeros((frames, HEAD_DIM), jnp.float32)
-    for part in range(frames // chunk):
-        rows = pl.ds(part * chunk, chunk)
-        queries = q_ref[0, rows, :]
-        grads = do_ref[0, rows, :]
-        scores = (
-            lax.dot_general(
-                queries, keys, (((1,), (1,)), ((), ())), preferred_element_type=jnp.float32
+    )(*arrays)
+
+
+LINE_FLIPS = [(1, 0, 0, 0), (2, 0, 0, 0), (3, 0, 0, 0)]
+
+
+def line_start(me, ins, outs, sent, got):
+    copies = []
+    for i, (src, dst) in enumerate(zip(ins, outs)):
+        for k, flip in enumerate(LINE_FLIPS):
+            peer = turned(me, flip)
+            copy = pltpu.make_async_remote_copy(
+                src_ref=src if len(src.shape) == 2 else src.at[peer[0]],
+                dst_ref=dst.at[k],
+                send_sem=sent.at[i, k],
+                recv_sem=got.at[i, k],
+                device_id=device_of(peer),
+                device_id_type=MESH,
             )
-            * scale
+            copy.start()
+            copies.append(copy)
+    return copies
+
+
+def line_shapes(arrays):
+    return tuple(
+        jax.ShapeDtypeStruct((3,) + (a.shape if a.ndim == 2 else a.shape[1:]), a.dtype)
+        for a in arrays
+    )
+
+
+LEVELS = 32000.0
+
+
+def line_pack(parts):
+    tops = jnp.max(jnp.abs(parts), axis=2)
+    codes = jnp.round(parts * (LEVELS / jnp.maximum(tops, 1e-30))[:, :, None]).astype(jnp.int32)
+    half = parts.shape[1] // 2
+    return tops, lax.shift_left(codes[:, :half], 16) | (codes[:, half:] & 65535)
+
+
+def line_total(part, tops, words):
+    z_at = lax.axis_index("z")
+    total = lax.dynamic_index_in_dim(part, z_at, 0, keepdims=False)
+    steps = lax.dynamic_index_in_dim(tops, z_at, 1, keepdims=False) * (1.0 / LEVELS)
+    for k in range(3):
+        high = lax.shift_right_arithmetic(words[k], 16)
+        low = lax.shift_right_arithmetic(lax.shift_left(words[k], 16), 16)
+        codes = jnp.concatenate([high, low], axis=0).astype(jnp.float32)
+        total = total + codes * steps[k][:, None]
+    return total
+
+
+def layer_swap(arrays, ident):
+    count = len(arrays)
+
+    def kernel(*refs):
+        x_refs, o_refs, (sent, got, own) = refs[:count], refs[count : 2 * count], refs[2 * count :]
+        me = place()
+        peers = [turned(me, flip) for flip in LAYER_FLIPS]
+        greet(peers)
+        mine = rank_of(me)
+        copies = [
+            pltpu.make_async_remote_copy(
+                src_ref=x_refs[j].at[rank_of(peer)],
+                dst_ref=o_refs[j].at[mine],
+                send_sem=sent.at[j, i],
+                recv_sem=got.at[j, i],
+                device_id=device_of(peer),
+                device_id_type=MESH,
+            )
+            for i, peer in enumerate(peers)
+            for j in range(count)
+        ]
+        for copy in copies:
+            copy.start()
+        for j in range(count):
+            local = pltpu.make_async_copy(x_refs[j].at[mine], o_refs[j].at[mine], own.at[j])
+            local.start()
+            local.wait()
+        for copy in copies:
+            copy.wait()
+
+    dma = pltpu.SemaphoreType.DMA
+    return comm_call(
+        kernel,
+        tuple(jax.ShapeDtypeStruct(a.shape, a.dtype) for a in arrays),
+        tuple(arrays),
+        [dma((count, 7)), dma((count, 7)), dma((count,))],
+        ident,
+    )
+
+
+def layer_gather(array, ident, carry=()):
+    half = array.shape[0] // 2
+    extra = len(carry)
+
+    def kernel(x_ref, *refs):
+        carry_in, o_ref, carry_out = refs[:extra], refs[extra], refs[extra + 1 : 2 * extra + 1]
+        sent, got, own, csent, cgot = refs[2 * extra + 1 :]
+        me = place()
+        by_x, by_y, by_xy = (turned(me, (0, y, x, 0)) for y, x in ((0, 1), (1, 0), (1, 1)))
+        other = turned(me, (0, 0, 0, 1))
+        line = [turned(me, flip) for flip in LINE_FLIPS] if extra else []
+        greet([by_x, by_y, other] + line)
+        carried = line_start(me, carry_in, carry_out, csent, cgot)
+
+        def send(which, src, dst, peer):
+            copy = pltpu.make_async_remote_copy(
+                src_ref=src,
+                dst_ref=dst,
+                send_sem=sent.at[which],
+                recv_sem=got.at[which],
+                device_id=device_of(peer),
+                device_id_type=MESH,
+            )
+            copy.start()
+            return copy
+
+        slot = o_ref.at[rank_of(me)]
+        first, second = pl.ds(0, half), pl.ds(half, half)
+        copies = [
+            send(0, x_ref.at[first], slot.at[first], by_x),
+            send(1, x_ref.at[second], slot.at[second], by_y),
+            send(2, x_ref.at[second], slot.at[second], by_x),
+            send(3, x_ref.at[first], slot.at[first], by_y),
+            send(4, x_ref, slot, other),
+        ]
+        local = pltpu.make_async_copy(x_ref, slot, own)
+        local.start()
+        from_x, from_y, from_xy = (o_ref.at[rank_of(p)] for p in (by_x, by_y, by_xy))
+        copies[0].wait_recv()
+        copies.append(send(5, from_x.at[first], from_x.at[first], by_y))
+        copies[1].wait_recv()
+        copies.append(send(6, from_y.at[second], from_y.at[second], by_x))
+        copies[2].wait_recv()
+        copies.append(send(7, from_x, from_x, other))
+        copies[3].wait_recv()
+        copies.append(send(8, from_y, from_y, other))
+        copies[5].wait_recv()
+        copies[6].wait_recv()
+        copies.append(send(9, from_xy, from_xy, other))
+        local.wait()
+        for i in (4, 7, 8, 9):
+            copies[i].wait_recv()
+        for copy in copies:
+            copy.wait_send()
+        for copy in carried:
+            copy.wait()
+
+    dma = pltpu.SemaphoreType.DMA
+    out = comm_call(
+        kernel,
+        (jax.ShapeDtypeStruct((RANKS,) + array.shape, array.dtype),) + line_shapes(carry),
+        (array,) + tuple(carry),
+        [dma((10,)), dma((10,)), dma] + [dma((max(extra, 1), 3))] * 2,
+        ident,
+        cost_us=30,
+    )
+    return out if extra else out[0]
+
+
+def layer_sum(array, ident, carry=(), low=jnp.float32):
+    _, rows, width = array.shape
+    half = rows // 2
+    f32 = jnp.float32
+
+    extra = len(carry)
+
+    def kernel(p_ref, *refs):
+        carry_in, o_ref, carry_out = refs[:extra], refs[extra], refs[extra + 1 : 2 * extra + 1]
+        mine, theirs, out_one, in_one, out_two, in_two, sent, got, own, csent, cgot = refs[
+            2 * extra + 1 :
+        ]
+        me = place()
+        z_at, y_at, x_at, core = me
+        by_x, by_y = (turned(me, flip) for flip in ((0, 0, 1, 0), (0, 1, 0, 0)))
+        other = turned(me, (0, 0, 0, 1))
+        line = [turned(me, flip) for flip in LINE_FLIPS] if extra else []
+        greet([by_x, by_y, other] + line)
+        carried = line_start(me, carry_in, carry_out, csent, cgot)
+
+        def send(which, src, dst, peer):
+            copy = pltpu.make_async_remote_copy(
+                src_ref=src,
+                dst_ref=dst,
+                send_sem=sent.at[which],
+                recv_sem=got.at[which],
+                device_id=device_of(peer),
+                device_id_type=MESH,
+            )
+            copy.start()
+            return copy
+
+        cores, locals_ = [], []
+        for dy in (1, 0):
+            for dx in (1, 0):
+                slot = 2 * dy + dx
+                chip = turned(me, (0, dy, dx, 0))
+                local = pltpu.make_async_copy(p_ref.at[rank_of(chip)], mine.at[slot], own.at[slot])
+                local.start()
+                locals_.append(local)
+                cores.append(
+                    send(slot, p_ref.at[rank_of(turned(chip, (0, 0, 0, 1)))], theirs.at[slot], other)
+                )
+        first, second = pl.ds(0, half), pl.ds(half, half)
+        for i, slot in enumerate((3, 2, 1, 0)):
+            locals_[i].wait()
+            cores[i].wait_recv()
+            mine[slot] = mine[slot] + theirs[slot]
+        for k, slot in enumerate((3, 1)):
+            out_one[0, k] = mine[slot, first, :].astype(low)
+        over_x = send(4, out_one.at[0], in_one.at[0], by_x)
+        for k, slot in enumerate((3, 2)):
+            out_one[1, k] = mine[slot, second, :].astype(low)
+        over_y = send(5, out_one.at[1], in_one.at[1], by_y)
+        over_x.wait_recv()
+        out_two[0] = (mine[2, first, :] + in_one[0, 0].astype(f32)).astype(low)
+        next_y = send(6, out_two.at[0], in_two.at[0], by_y)
+        over_y.wait_recv()
+        out_two[1] = (mine[1, second, :] + in_one[1, 0].astype(f32)).astype(low)
+        next_x = send(7, out_two.at[1], in_two.at[1], by_x)
+        mine[0, first, :] = mine[0, first, :] + in_one[0, 1].astype(f32)
+        mine[0, second, :] = mine[0, second, :] + in_one[1, 1].astype(f32)
+        next_y.wait_recv()
+        mine[0, first, :] = mine[0, first, :] + in_two[0].astype(f32)
+        next_x.wait_recv()
+        mine[0, second, :] = mine[0, second, :] + in_two[1].astype(f32)
+        done = pltpu.make_async_copy(mine.at[0], o_ref, own.at[4])
+        done.start()
+        done.wait()
+        for copy in cores + [over_x, over_y, next_y, next_x]:
+            copy.wait_send()
+        for copy in carried:
+            copy.wait()
+
+    dma = pltpu.SemaphoreType.DMA
+    out = comm_call(
+        kernel,
+        (jax.ShapeDtypeStruct((rows, width), f32),) + line_shapes(carry),
+        (array,) + tuple(carry),
+        [
+            pltpu.VMEM((4, rows, width), f32),
+            pltpu.VMEM((4, rows, width), f32),
+            pltpu.VMEM((2, 2, half, width), low),
+            pltpu.VMEM((2, 2, half, width), low),
+            pltpu.VMEM((2, half, width), low),
+            pltpu.VMEM((2, half, width), low),
+            dma((8,)),
+            dma((8,)),
+            dma((5,)),
+        ]
+        + [dma((max(extra, 1), 3))] * 2,
+        ident,
+        vmem=True,
+        cost_us=65 if rows * width > 300000 else 25,
+    )
+    return out if extra else out[0]
+
+
+def all_fold(vector, ident, fold):
+    flips = [(z, y, x, c) for z in range(4) for y in range(2) for x in range(2) for c in range(2)][1:]
+    count = len(flips)
+
+    def kernel(v_ref, o_ref, slots, sent, got):
+        me = place()
+        peers = [turned(me, flip) for flip in flips]
+        greet(peers)
+        mine = RANKS * me[0] + rank_of(me)
+        slots[mine] = v_ref[...]
+        copies = [
+            pltpu.make_async_remote_copy(
+                src_ref=v_ref,
+                dst_ref=slots.at[mine],
+                send_sem=sent.at[i],
+                recv_sem=got.at[i],
+                device_id=device_of(peer),
+                device_id_type=MESH,
+            )
+            for i, peer in enumerate(peers)
+        ]
+        for copy in copies:
+            copy.start()
+        for copy in copies:
+            copy.wait()
+        total = slots[0]
+        for i in range(1, count + 1):
+            total = fold(total, slots[i])
+        o_ref[...] = total
+
+    dma = pltpu.SemaphoreType.DMA
+    spec = pl.BlockSpec(memory_space=pltpu.VMEM)
+    return pl.pallas_call(
+        kernel,
+        out_shape=jax.ShapeDtypeStruct(vector.shape, vector.dtype),
+        in_specs=[spec],
+        out_specs=spec,
+        scratch_shapes=[
+            pltpu.VMEM((count + 1,) + vector.shape, vector.dtype),
+            dma((count,)),
+            dma((count,)),
+        ],
+        compiler_params=pltpu.CompilerParams(collective_id=ident, has_side_effects=True),
+    )(vector)
+
+
+def lanes_of(values):
+    row = jnp.concatenate([jnp.stack(values), jnp.zeros((128 - len(values),), jnp.float32)])
+    return jnp.broadcast_to(row[None, :], (8, 128))
+
+
+def full_sum_steps(me, mine, theirs, in_a, in_b, in_c, in_d, in_z, put):
+    z_at, y_at, x_at, core = me
+    half = mine.shape[3] // 2
+    first, second = pl.ds(0, half), pl.ds(half, half)
+    by_x, by_y = (turned(me, flip) for flip in ((0, 0, 1, 0), (0, 1, 0, 0)))
+    over_x = put(mine.at[1 - x_at, :, :, first], in_a, by_x)
+    over_y = put(mine.at[:, 1 - y_at, :, second], in_b, by_y)
+    over_x.wait_recv()
+    mine[x_at, :, :, first] = mine[x_at, :, :, first] + in_a[...]
+    next_y = put(mine.at[x_at, 1 - y_at, :, first], in_c, by_y)
+    over_y.wait_recv()
+    mine[:, y_at, :, second] = mine[:, y_at, :, second] + in_b[...]
+    next_x = put(mine.at[1 - x_at, y_at, :, second], in_d, by_x)
+    next_y.wait_recv()
+    mine[x_at, y_at, :, first] = mine[x_at, y_at, :, first] + in_c[...]
+    next_x.wait_recv()
+    mine[x_at, y_at, :, second] = mine[x_at, y_at, :, second] + in_d[...]
+    sends = []
+    for k in (1, 2, 3):
+        peer = turned(me, (k, 0, 0, 0))
+        sends.append(put(mine.at[x_at, y_at, peer[0]], in_z.at[k - 1], peer))
+    for send in sends:
+        send.wait_recv()
+    return mine[x_at, y_at, z_at] + in_z[0] + in_z[1] + in_z[2], [
+        over_x,
+        over_y,
+        next_y,
+        next_x,
+    ] + sends
+
+
+def putter(sent, got):
+    count = [0]
+
+    def put(src, dst, peer):
+        at = count[0]
+        count[0] += 1
+        copy = pltpu.make_async_remote_copy(
+            src_ref=src,
+            dst_ref=dst,
+            send_sem=sent.at[at],
+            recv_sem=got.at[at],
+            device_id=device_of(peer),
+            device_id_type=MESH,
         )
-        scores = jnp.where(live, scores, -1e30)
-        weights = jnp.exp(scores - lse_ref[0, rows, :])
-        delta = jnp.sum(grads.astype(jnp.float32) * o_ref[0, rows, :], axis=1, keepdims=True)
-        pulled = lax.dot_general(
-            grads, values, (((1,), (1,)), ((), ())), preferred_element_type=jnp.float32
-        )
-        pushed = (weights * (pulled - delta)).astype(LOW)
-        dq_ref[0, rows, :] = jnp.dot(pushed, keys, preferred_element_type=jnp.float32) * scale
-        grad_key = grad_key + rows_product(pushed, queries)
-        grad_value = grad_value + rows_product(weights.astype(LOW), grads)
-    dk_ref[0] = grad_key * scale
-    dv_ref[0] = grad_value
-
-
-def attend_back(queries, key_rows, values, mixed, log_total, grads, lengths):
-    count, frames, width = queries.shape
-    block = pl.BlockSpec((1, frames, width), lambda i: (i, 0, 0))
-    shape = jax.ShapeDtypeStruct((count, frames, width), jnp.float32)
-    return pl.pallas_call(
-        attend_back_kernel,
-        grid=(count,),
-        out_shape=(shape,) * 3,
-        in_specs=[
-            pl.BlockSpec(memory_space=pltpu.SMEM),
-            block,
-            block,
-            block,
-            block,
-            pl.BlockSpec((1, frames, 1), lambda i: (i, 0, 0)),
-            block,
-        ],
-        out_specs=(block,) * 3,
-        compiler_params=pltpu.CompilerParams(vmem_limit_bytes=48 << 20),
-        cost_estimate=pl.CostEstimate(
-            flops=10 * count * frames * frames * width,
-            bytes_accessed=24 * count * frames * width,
-            transcendentals=count * frames * frames,
-        ),
-    )(lengths, queries, key_rows, values, mixed, log_total, grads)
-
-
-def cross_forward(cross_query, cross_key, cross_value):
-    probs = jax.nn.softmax(scores_of(cross_query, cross_key), axis=-1)
-    probs_low = probs.astype(LOW)
-    out = jnp.einsum("bhqk,bkhd->bqhd", probs_low, cross_value, preferred_element_type=jnp.float32)
-    return probs, probs_low, out
-
-
-def newton_products(gram):
-    trace = jnp.trace(gram, axis1=1, axis2=2)[:, None, None]
-    norm_value = jnp.sqrt(trace) + 1e-07
+        copy.start()
+        return copy
+
+    return put
+
+
+NEAR_FLIPS = [(0, 0, 0, 1), (0, 0, 1, 0), (0, 1, 0, 0), (1, 0, 0, 0), (2, 0, 0, 0), (3, 0, 0, 0)]
+
+
+def full_scratch(rows, lanes):
+    half = rows // 2
+    f32 = jnp.float32
+    return [
+        pltpu.VMEM((2, 2, 4, rows, lanes), f32),
+        pltpu.VMEM((2, 2, 4, rows, lanes), f32),
+        pltpu.VMEM((2, 4, half, lanes), f32),
+        pltpu.VMEM((2, 4, half, lanes), f32),
+        pltpu.VMEM((4, half, lanes), f32),
+        pltpu.VMEM((4, half, lanes), f32),
+        pltpu.VMEM((3, rows, lanes), f32),
+    ]
+
+
+def full_start(p_ref, me, mine, theirs, own, put):
+    core = me[3]
+    local = pltpu.make_async_copy(p_ref.at[core], mine, own)
+    local.start()
+    swap = put(p_ref.at[1 - core], theirs, turned(me, (0, 0, 0, 1)))
+    local.wait()
+    swap.wait_recv()
+    for x in range(2):
+        for y in range(2):
+            mine[x, y] = mine[x, y] + theirs[x, y]
+    return swap
+
+
+def full_scatter(parts, ident, carry):
+    rows, lanes = parts.shape[4:]
+    extra = len(carry)
+
+    def kernel(p_ref, *refs):
+        carry_in, o_ref, carry_out = refs[:extra], refs[extra], refs[extra + 1 : 2 * extra + 1]
+        mine, theirs, in_a, in_b, in_c, in_d, in_z, total, sent, got, own, csent, cgot = refs[
+            2 * extra + 1 :
+        ]
+        me = place()
+        greet([turned(me, flip) for flip in NEAR_FLIPS])
+        carried = line_start(me, carry_in, carry_out, csent, cgot)
+        put = putter(sent, got)
+        swap = full_start(p_ref, me, mine, theirs, own.at[0], put)
+        value, copies = full_sum_steps(me, mine, theirs, in_a, in_b, in_c, in_d, in_z, put)
+        total[...] = value
+        done = pltpu.make_async_copy(total, o_ref, own.at[1])
+        done.start()
+        done.wait()
+        for copy in [swap] + copies:
+            copy.wait_send()
+        for copy in carried:
+            copy.wait()
+
+    dma = pltpu.SemaphoreType.DMA
+    return comm_call(
+        kernel,
+        (jax.ShapeDtypeStruct((rows, lanes), jnp.float32),) + line_shapes(carry),
+        (parts,) + tuple(carry),
+        full_scratch(rows, lanes)
+        + [pltpu.VMEM((rows, lanes), jnp.float32), dma((8,)), dma((8,)), dma((2,))]
+        + [dma((extra, 3))] * 2,
+        ident,
+        vmem=True,
+        cost_us=40,
+    )
+
+
+def newton_pair(pair):
+    wide = 2 * HEAD_DIM
+    row = lax.broadcasted_iota(jnp.int32, (wide, wide), 0)
+    lane = lax.broadcasted_iota(jnp.int32, (wide, wide), 1)
+    same = (row < HEAD_DIM) == (lane < HEAD_DIM)
+    gram = jnp.where(same, jnp.concatenate([pair, pair], axis=0), 0.0)
+    diagonal = jnp.where(row == lane, gram, 0.0)
+    lone = jnp.sum(jnp.where(row < HEAD_DIM, diagonal, 0.0), keepdims=True)
+    ltwo = jnp.sum(jnp.where(row < HEAD_DIM, 0.0, diagonal), keepdims=True)
+    norm_value = jnp.sqrt(jnp.where(row < HEAD_DIM, lone, ltwo)) + 1e-07
     product = gram / (norm_value * norm_value)
-    eye = jnp.eye(HEAD_DIM, dtype=jnp.float32)[None]
+    eye = jnp.where(row == lane, 1.0, 0.0)
 
     def mul(left, right):
-        return jnp.einsum("bij,bjk->bik", left, right, precision=HIGHEST)
+        return jnp.dot(left, right, precision=HIGHEST, preferred_element_type=jnp.float32)
 
     total = None
     for newton_step in range(5):
@@ -756,7 +1135,354 @@
         total = mixer if total is None else mul(mixer, total)
         if newton_step < 4:
             product = mul(mul(mixer, product), mixer)
-    return total / norm_value
+    total = total / norm_value
+    return total[:HEAD_DIM] + total[HEAD_DIM:]
+
+
+def full_newton(parts, ident):
+    rows, lanes = parts.shape[4:]
+    half = rows // 2
+
+    def kernel(p_ref, o_ref, mine, theirs, in_a, in_b, in_c, in_d, in_z, whole, sent, got, own):
+        me = place()
+        z_at, y_at, x_at, core = me
+        greet([turned(me, flip) for flip in NEAR_FLIPS])
+        put = putter(sent, got)
+        swap = full_start(p_ref, me, mine, theirs, own.at[0], put)
+        value, copies = full_sum_steps(me, mine, theirs, in_a, in_b, in_c, in_d, in_z, put)
+        for i in range(rows // HEAD_DIM):
+            part = slice(i * HEAD_DIM, (i + 1) * HEAD_DIM)
+            whole[core, x_at, y_at, z_at, pl.ds(i * HEAD_DIM, HEAD_DIM)] = newton_pair(value[part])
+        first, second = pl.ds(0, half), pl.ds(half, half)
+        by_x, by_y = (turned(me, flip) for flip in ((0, 0, 1, 0), (0, 1, 0, 0)))
+        slot = whole.at[core, x_at, y_at, z_at]
+        over_z = [put(slot, slot, turned(me, (k, 0, 0, 0))) for k in (1, 2, 3)]
+        for copy in over_z:
+            copy.wait_recv()
+        part_a = whole.at[core, x_at, y_at, :, first]
+        part_b = whole.at[core, x_at, y_at, :, second]
+        over_x = put(part_a, part_a, by_x)
+        over_y = put(part_b, part_b, by_y)
+        over_x.wait_recv()
+        part_a = whole.at[core, :, y_at, :, first]
+        next_y = put(part_a, part_a, by_y)
+        over_y.wait_recv()
+        part_b = whole.at[core, x_at, :, :, second]
+        next_x = put(part_b, part_b, by_x)
+        next_y.wait_recv()
+        next_x.wait_recv()
+        last = put(whole.at[core], whole.at[core], turned(me, (0, 0, 0, 1)))
+        last.wait_recv()
+        done = pltpu.make_async_copy(whole, o_ref, own.at[1])
+        done.start()
+        done.wait()
+        for copy in [swap] + copies + over_z + [over_x, over_y, next_y, next_x, last]:
+            copy.wait_send()
+
+    dma = pltpu.SemaphoreType.DMA
+    return comm_call(
+        kernel,
+        jax.ShapeDtypeStruct(parts.shape, jnp.float32),
+        (parts,),
+        full_scratch(rows, lanes)
+        + [pltpu.VMEM((2, 2, 2, 4, rows, lanes), jnp.float32), dma((16,)), dma((16,)), dma((2,))],
+        ident,
+        vmem=True,
+    )
+
+
+def setup_exchange(slab, small, noisy, meta, ident):
+    planes = 4
+    flips_f = [flip for flip in LAYER_FLIPS if flip[1] == 0]
+
+    def kernel(
+        w_ref, s_ref, n_ref, m_ref, wo, so, no, mo, s_mid, n_mid, sent, got, csent, cgot, own
+    ):
+        me = place()
+        z_at, y_at, x_at, core = me
+        mine = rank_of(me)
+        f_at = 2 * x_at + core
+        layer = [turned(me, flip) for flip in LAYER_FLIPS]
+        line = [turned(me, (k, 0, 0, 0)) for k in (1, 2, 3)]
+        greet(layer + line)
+        put = putter(sent, got)
+        locals_ = [
+            pltpu.make_async_copy(w_ref.at[mine], wo.at[z_at, mine], own.at[0]),
+            pltpu.make_async_copy(s_ref, s_mid.at[z_at], own.at[1]),
+            pltpu.make_async_copy(n_ref, n_mid.at[y_at, f_at], own.at[2]),
+            pltpu.make_async_copy(m_ref, mo.at[f_at], own.at[3]),
+        ]
+        for copy in locals_:
+            copy.start()
+        small_line = [put(s_ref, s_mid.at[z_at], peer) for peer in line]
+        slabs = [put(w_ref.at[rank_of(peer)], wo.at[z_at, mine], peer) for peer in layer]
+        metas = [put(m_ref, mo.at[f_at], turned(me, flip)) for flip in flips_f]
+        noisies = [put(n_ref, n_mid.at[y_at, f_at], peer) for peer in layer]
+        for copy in locals_:
+            copy.wait()
+        for copy in slabs:
+            copy.wait_recv()
+
+        def along(which, target, source, step):
+            return pltpu.make_async_remote_copy(
+                src_ref=wo.at[source],
+                dst_ref=wo.at[source],
+                send_sem=csent.at[which, step],
+                recv_sem=cgot.at[which, step],
+                device_id=device_of((target, y_at, x_at, core)),
+                device_id_type=MESH,
+            )
+
+        def go(step):
+            @pl.when((z_at < planes - 1) & (z_at >= step))
+            def _():
+                along(0, z_at + 1, z_at - step, step).start()
+
+            @pl.when((z_at > 0) & (z_at + step < planes))
+            def _():
+                along(1, z_at - 1, z_at + step, step).start()
+
+        def come(step):
+            @pl.when(z_at >= step + 1)
+            def _():
+                along(0, z_at - 1, z_at - 1 - step, step).wait_recv()
+
+            @pl.when(z_at + step + 1 < planes)
+            def _():
+                along(1, z_at + 1, z_at + 1 + step, step).wait_recv()
+
+        go(0)
+        for copy in small_line:
+            copy.wait_recv()
+        smalls = [put(s_mid, so.at[:, mine], peer) for peer in layer]
+        small_own = pltpu.make_async_copy(s_mid, so.at[:, mine], own.at[4])
+        small_own.start()
+        for copy in noisies:
+            copy.wait_recv()
+        noisy_line = [put(n_mid.at[:, peer[0]], no.at[z_at], peer) for peer in line]
+        noisy_own = pltpu.make_async_copy(n_mid.at[:, z_at], no.at[z_at], own.at[5])
+        noisy_own.start()
+        come(0)
+        go(1)
+        come(1)
+        go(2)
+        come(2)
+        small_own.wait()
+        noisy_own.wait()
+        for copy in metas + smalls + noisy_line:
+            copy.wait_recv()
+        for copy in small_line + slabs + metas + noisies + smalls + noisy_line:
+            copy.wait_send()
+        for step in range(3):
+
+            @pl.when((z_at < planes - 1) & (z_at >= step))
+            def _():
+                along(0, z_at + 1, z_at - step, step).wait_send()
+
+            @pl.when((z_at > 0) & (z_at + step < planes))
+            def _():
+                along(1, z_at - 1, z_at + step, step).wait_send()
+
+    dma = pltpu.SemaphoreType.DMA
+    shape = jax.ShapeDtypeStruct
+    return comm_call(
+        kernel,
+        (
+            shape((planes,) + slab.shape, slab.dtype),
+            shape((planes, RANKS) + small.shape, small.dtype),
+            shape((planes, 2) + noisy.shape, noisy.dtype),
+            shape((4,) + meta.shape, meta.dtype),
+        ),
+        (slab, small, noisy, meta),
+        [
+            pltpu.VMEM((planes,) + small.shape, small.dtype),
+            pltpu.VMEM((2, 4) + noisy.shape, noisy.dtype),
+            dma((32,)),
+            dma((32,)),
+            dma((2, 3)),
+            dma((2, 3)),
+            dma((6,)),
+        ],
+        ident,
+        vmem=True,
+        cost_us=60,
+    )
+
+
+def swapped_halves(values):
+    half_dim = values.shape[1] // 2
+    return jnp.concatenate([values[:, half_dim:], values[:, :half_dim]], axis=1)
+
+
+def attend_kernel(lengths_ref, qkv_ref, cos_ref, sin_ref, qr_ref, kr_ref, vr_ref, o_ref, low_ref, lse_ref):
+    frames = qkv_ref.shape[1]
+    length = lengths_ref[pl.program_id(0)]
+    cosine, sine_table = cos_ref[...], sin_ref[...]
+    chunk = 256
+    live = lax.broadcasted_iota(jnp.int32, (chunk, frames), 1) < length
+    for head in range(LOCAL_HEADS):
+        at = slice(head * HEAD_DIM, (head + 1) * HEAD_DIM)
+
+        def column(which):
+            return qkv_ref[0, :, which * COLS + head * HEAD_DIM : which * COLS + (head + 1) * HEAD_DIM]
+
+        query, key = column(0), column(1)
+        queries = (query * cosine + swapped_halves(query) * sine_table).astype(LOW)
+        keys = (key * cosine + swapped_halves(key) * sine_table).astype(LOW)
+        values = column(2).astype(LOW)
+        qr_ref[0, head] = queries
+        kr_ref[0, head] = keys
+        vr_ref[0, head] = values
+        for part in range(frames // chunk):
+            rows = slice(part * chunk, (part + 1) * chunk)
+            scores = lax.dot_general(
+                queries[rows], keys, (((1,), (1,)), ((), ())), preferred_element_type=jnp.float32
+            ) * (1.0 / math.sqrt(HEAD_DIM))
+            scores = jnp.where(live, scores, -1e30)
+            top = jnp.max(scores, axis=1, keepdims=True)
+            grown = jnp.exp(scores - top)
+            total = jnp.sum(grown, axis=1, keepdims=True)
+            weights = (grown * (1.0 / total)).astype(LOW)
+            mixed = jnp.dot(weights, values, preferred_element_type=jnp.float32)
+            o_ref[0, head, rows, :] = mixed
+            span = low_ref.shape[2]
+            for k in range(chunk // span):
+                low_ref[part * (chunk // span) + k, 0, :, at] = mixed[
+                    k * span : (k + 1) * span
+                ].astype(LOW)
+            lse_ref[0, head, rows, :] = top + jnp.log(total)
+
+
+def attend(qkv, cosine, sine_table, lengths, span):
+    count, frames, width = qkv.shape
+    heads = pl.BlockSpec((1, LOCAL_HEADS, frames, HEAD_DIM), lambda i: (i, 0, 0, 0))
+    table = pl.BlockSpec((frames, HEAD_DIM), lambda i: (0, 0))
+    low = jax.ShapeDtypeStruct((count, LOCAL_HEADS, frames, HEAD_DIM), LOW)
+    return pl.pallas_call(
+        attend_kernel,
+        grid=(count,),
+        out_shape=(
+            low,
+            low,
+            low,
+            jax.ShapeDtypeStruct((count, LOCAL_HEADS, frames, HEAD_DIM), jnp.float32),
+            jax.ShapeDtypeStruct((RANKS, count, span, COLS), LOW),
+            jax.ShapeDtypeStruct((count, LOCAL_HEADS, frames, 1), jnp.float32),
+        ),
+        in_specs=[
+            pl.BlockSpec(memory_space=pltpu.SMEM),
+            pl.BlockSpec((1, frames, width), lambda i: (i, 0, 0)),
+            table,
+            table,
+        ],
+        out_specs=(
+            heads,
+            heads,
+            heads,
+            heads,
+            pl.BlockSpec((RANKS, 1, span, COLS), lambda i: (0, i, 0, 0)),
+            pl.BlockSpec((1, LOCAL_HEADS, frames, 1), lambda i: (i, 0, 0, 0)),
+        ),
+        compiler_params=pltpu.CompilerParams(vmem_limit_bytes=56 << 20),
+        cost_estimate=pl.CostEstimate(
+            flops=4 * count * frames * frames * COLS,
+            bytes_accessed=10 * count * frames * COLS,
+            transcendentals=count * LOCAL_HEADS * frames * frames,
+        ),
+    )(lengths, qkv, cosine, sine_table)
+
+
+def attend_back_kernel(
+    lengths_ref, q_ref, k_ref, v_ref, o_ref, lse_ref, do_ref, cos_ref, sin_ref, d_ref
+):
+    frames = q_ref.shape[2]
+    length = lengths_ref[pl.program_id(0)]
+    cosine, sine_table = cos_ref[...], sin_ref[...]
+    chunk = 256
+    scale = 1.0 / math.sqrt(HEAD_DIM)
+    span = do_ref.shape[2]
+    live = lax.broadcasted_iota(jnp.int32, (chunk, frames), 1) < length
+    for head in range(LOCAL_HEADS):
+        at = slice(head * HEAD_DIM, (head + 1) * HEAD_DIM)
+        keys = k_ref[0, head]
+        values = v_ref[0, head]
+        grad_key = jnp.zeros((frames, HEAD_DIM), jnp.float32)
+        grad_value = jnp.zeros((frames, HEAD_DIM), jnp.float32)
+        for part in range(frames // chunk):
+            rows = slice(part * chunk, (part + 1) * chunk)
+            queries = q_ref[0, head, rows, :]
+            grads = jnp.concatenate(
+                [
+                    do_ref[part * (chunk // span) + k, 0, :, at]
+                    for k in range(chunk // span)
+                ],
+                axis=0,
+            )
+            scores = (
+                lax.dot_general(
+                    queries, keys, (((1,), (1,)), ((), ())), preferred_element_type=jnp.float32
+                )
+                * scale
+            )
+            scores = jnp.where(live, scores, -1e30)
+            weights = jnp.exp(scores - lse_ref[0, head, rows, :])
+            delta = jnp.sum(
+                grads.astype(jnp.float32) * o_ref[0, head, rows, :], axis=1, keepdims=True
+            )
+            pulled = lax.dot_general(
+                grads, values, (((1,), (1,)), ((), ())), preferred_element_type=jnp.float32
+            )
+            pushed = (weights * (pulled - delta)).astype(LOW)
+            grad_query = jnp.dot(pushed, keys, preferred_element_type=jnp.float32) * scale
+            grad_key = grad_key + rows_product(pushed, queries)
+            grad_value = grad_value + rows_product(weights.astype(LOW), grads)
+            d_ref[0, rows, head * HEAD_DIM : (head + 1) * HEAD_DIM] = (
+                grad_query * cosine[rows] - swapped_halves(grad_query) * sine_table[rows]
+            ).astype(LOW)
+        grad_key = grad_key * scale
+        d_ref[0, :, COLS + head * HEAD_DIM : COLS + (head + 1) * HEAD_DIM] = (
+            grad_key * cosine - swapped_halves(grad_key) * sine_table
+        ).astype(LOW)
+        d_ref[0, :, 2 * COLS + head * HEAD_DIM : 2 * COLS + (head + 1) * HEAD_DIM] = (
+            grad_value.astype(LOW)
+        )
+
+
+def attend_back(queries, key_rows, values, mixed, log_total, grads, cosine, sine_table, lengths):
+    count, heads_here, frames, width = queries.shape
+    span = grads.shape[2]
+    heads = pl.BlockSpec((1, heads_here, frames, width), lambda i: (i, 0, 0, 0))
+    table = pl.BlockSpec((frames, width), lambda i: (0, 0))
+    return pl.pallas_call(
+        attend_back_kernel,
+        grid=(count,),
+        out_shape=jax.ShapeDtypeStruct((count, frames, 3 * COLS), LOW),
+        in_specs=[
+            pl.BlockSpec(memory_space=pltpu.SMEM),
+            heads,
+            heads,
+            heads,
+            heads,
+            pl.BlockSpec((1, heads_here, frames, 1), lambda i: (i, 0, 0, 0)),
+            pl.BlockSpec((RANKS, 1, span, COLS), lambda i: (0, i, 0, 0)),
+            table,
+            table,
+        ],
+        out_specs=pl.BlockSpec((1, frames, 3 * COLS), lambda i: (i, 0, 0)),
+        compiler_params=pltpu.CompilerParams(vmem_limit_bytes=56 << 20),
+        cost_estimate=pl.CostEstimate(
+            flops=10 * count * frames * frames * COLS,
+            bytes_accessed=24 * count * frames * COLS,
+            transcendentals=count * heads_here * frames * frames,
+        ),
+    )(lengths, queries, key_rows, values, mixed, log_total, grads, cosine, sine_table)
+
+
+def cross_forward(cross_query, cross_key, cross_value):
+    probs = jax.nn.softmax(scores_of(cross_query, cross_key), axis=-1)
+    probs_low = probs.astype(LOW)
+    out = jnp.einsum("bhqk,bkhd->bqhd", probs_low, cross_value, preferred_element_type=jnp.float32)
+    return probs, probs_low, out
 
 
 def fast_body(
@@ -807,16 +1533,39 @@
             norm_params,
         ],
         axis=0,
-    ).astype(LOW)
-    small_all = lax.all_gather(small_low, ALL, axis=1, tiled=True)
-    latent_in = small_all[:LAT]
-    latent_out = small_all[LAT : 2 * LAT]
-    timing = small_all[2 * LAT : 2 * LAT + FOUR]
-    norms = small_all[2 * LAT + FOUR :].astype(f32)
-
-    meta = lax.all_gather(
-        jnp.stack([timesteps, lengths.astype(f32), buckets.astype(f32)]), "f", axis=1, tiled=True
-    )
+    ).T.astype(LOW)
+    signal = jnp.cos(0.5 * math.pi * timesteps)[:, None, None]
+    noise_level = jnp.sin(0.5 * math.pi * timesteps)[:, None, None]
+    noisy_own = (signal * latents + noise_level * gaussian_noise).astype(LOW)
+    target_own = signal * gaussian_noise - noise_level * latents
+    local_meta = jnp.stack([timesteps, lengths.astype(f32), buckets.astype(f32)])
+    slab = jnp.concatenate(
+        [
+            attention_low[:3].reshape(-1, RANKS, COLS),
+            cross_low_t.reshape(-1, RANKS, COLS),
+        ],
+        axis=0,
+    )
+    slab_all, small_all, noisy_all, meta_all = setup_exchange(
+        jnp.swapaxes(slab, 0, 1),
+        small_low,
+        noisy_own.reshape(-1, latent_dim),
+        jnp.pad(local_meta, ((0, 5), (0, 128 - item_count))),
+        16,
+    )
+    attention_rest, slab_all = lax.optimization_barrier((attention_low[3:], slab_all))
+    small_all = small_all.reshape(D, -1)
+    latent_in = small_all[:, :LAT].T
+    latent_out = small_all[:, LAT : 2 * LAT].T
+    timing = small_all[:, 2 * LAT : 2 * LAT + FOUR].T
+    norms = small_all[:, 2 * LAT + FOUR :].astype(f32).T
+    qkv_rows = 3 * attention_low.shape[1]
+    qkv_slab = slab_all[:, :, :qkv_rows].reshape(planes * RANKS, 3, -1, COLS)
+    qkv_t = jnp.concatenate([qkv_slab[:, i].reshape(D, COLS) for i in range(3)], axis=1)
+    cross_w = jnp.moveaxis(
+        slab_all[:, :, qkv_rows:].reshape(planes * RANKS, 2, -1, COLS), 1, 0
+    ).reshape(2, E, COLS)
+    meta = jnp.swapaxes(meta_all[:, :3, :item_count], 0, 1).reshape(3, -1)
     times_all = meta[0]
     lengths_all = meta[1]
     onehot_all = (meta[2][:, None] == jnp.arange(NBUCK, dtype=f32)[None, :]).astype(f32)
@@ -830,14 +1579,8 @@
     features_all = time_features(times_all).astype(LOW)
     features = lax.dynamic_slice_in_dim(features_all, own_at, item_count, 0)
 
-    signal = jnp.cos(0.5 * math.pi * timesteps)[:, None, None]
-    noise_level = jnp.sin(0.5 * math.pi * timesteps)[:, None, None]
-    noisy_own = (signal * latents + noise_level * gaussian_noise).astype(LOW)
-    target_own = signal * gaussian_noise - noise_level * latents
-    noisy_all = lax.all_gather(noisy_own, ALL, axis=0, tiled=False)
-    noisy_all = noisy_all.reshape(RANKS, planes, item_count, span, latent_dim)
     noisy_low = jnp.swapaxes(
-        lax.dynamic_index_in_dim(noisy_all, z_at, 1, keepdims=False), 0, 1
+        noisy_all.reshape(RANKS, item_count, span, latent_dim), 0, 1
     ).reshape(item_count, frames, latent_dim)
     target = lax.ppermute(
         target_own, ALL, [(4 * s + g, RANKS * g + s) for s in range(RANKS) for g in range(planes)]
@@ -846,11 +1589,7 @@
     context_own = lax.dynamic_slice_in_dim(context_all, own_at, item_count, 0).reshape(-1, E)
     context_len = context.shape[1]
 
-    qkv_slab = lax.all_to_all(attention_low[:3], LAYER, split_axis=2, concat_axis=1, tiled=True)
-    qkv_t = lax.all_gather(qkv_slab, "z", axis=1, tiled=True)
-    cross_slab = lax.all_to_all(cross_low_t, LAYER, split_axis=2, concat_axis=1, tiled=True)
-    cross_w = lax.all_gather(cross_slab, "z", axis=1, tiled=True)
-    rest_t = lax.all_gather(attention_low[3:], ALL, axis=1, tiled=True)
+    rest_t = lax.all_gather(attention_rest, ALL, axis=1, tiled=True)
     gate_up = lax.all_gather(gate_up_weights.astype(LOW), "z", axis=0, tiled=True)
     down_pairs = []
     for p in range(planes):
@@ -863,8 +1602,8 @@
     half_dim = HEAD_DIM // 2
     inverse = 10000.0 ** (-jnp.arange(half_dim, dtype=f32) / half_dim)
     angles = jnp.arange(frames, dtype=f32)[:, None] * inverse[None, :]
-    cosine = jnp.cos(angles)[None, None]
-    sine_table = jnp.sin(angles)[None, None]
+    cosine = jnp.concatenate([jnp.cos(angles)] * 2, axis=1)
+    sine_table = jnp.concatenate([-jnp.sin(angles), jnp.sin(angles)], axis=1)
 
     timed = matmul_low(features, timing)
     start_all = (
@@ -882,41 +1621,15 @@
     )
     normed_one = normed_one.astype(LOW)
 
-    def heads_of(flat):
-        return jnp.swapaxes(
-            flat.reshape(item_count, frames, LOCAL_HEADS, HEAD_DIM), 1, 2
-        )
-
-    def packed(heads):
-        return heads.reshape(item_count * LOCAL_HEADS, frames, HEAD_DIM)
-
-    def flat_of(heads):
-        return jnp.swapaxes(
-            heads.reshape(item_count, LOCAL_HEADS, frames, HEAD_DIM), 1, 2
-        ).reshape(group_tokens, COLS)
-
-    queries = packed(
-        rotate(heads_of(matmul_low(normed_one, qkv_t[0])), cosine, sine_table).astype(LOW)
-    )
-    key_rows = packed(
-        rotate(heads_of(matmul_low(normed_one, qkv_t[1])), cosine, sine_table).astype(LOW)
-    )
-    values = packed(heads_of(matmul_low(normed_one, qkv_t[2])).astype(LOW))
-    mixed, log_total = attend(queries, key_rows, values, own_lengths)
-
-    def to_tokens(flat):
-        moved = flat.reshape(item_count, RANKS, span, COLS)
-        return lax.all_to_all(moved, LAYER, split_axis=1, concat_axis=3, tiled=True).reshape(
-            tokens, D
-        )
-
-    def to_heads(flat):
-        moved = flat.reshape(item_count, 1, span, D)
-        return lax.all_to_all(moved, LAYER, split_axis=3, concat_axis=1, tiled=True).reshape(
-            group_tokens, COLS
-        )
-
-    mixed_low = to_tokens(flat_of(mixed.astype(LOW)))
+    queries, key_rows, values, mixed, mixed_heads, log_total = attend(
+        matmul_low(normed_one, qkv_t).reshape(item_count, frames, 3 * COLS),
+        cosine,
+        sine_table,
+        own_lengths,
+        span,
+    )
+    mixed_heads = mixed_heads.reshape(RANKS, tokens, COLS)
+    mixed_low = jnp.swapaxes(layer_swap([mixed_heads], 1)[0], 0, 1).reshape(tokens, D)
     after_self = start_own + matmul_low(mixed_low, rest_t[0])
     normed_two, back_two = jax.vjp(layer_norm, after_self, norms[2], norms[3])
     normed_two = normed_two.astype(LOW)
@@ -926,23 +1639,23 @@
     pair_own = jnp.stack(
         [matmul_low(context_own, cross_w[0]), matmul_low(context_own, cross_w[1])]
     ).astype(LOW)
-    pair_all = lax.all_gather(pair_own, LAYER, axis=2, tiled=True).reshape(
-        2, item_count, context_len, HEADS, HEAD_DIM
-    )
+    pair_all = jnp.moveaxis(
+        layer_gather(pair_own.reshape(-1, COLS), 3).reshape(RANKS, -1, COLS), 0, 1
+    ).reshape(2, item_count, context_len, HEADS, HEAD_DIM)
     cross_key, cross_value = (pair_all[0], pair_all[1])
     probs, probs_low, cross_mixed = cross_forward(cross_query, cross_key, cross_value)
     cross_out = cross_mixed.reshape(tokens, D).astype(LOW)
     after_cross = after_self + matmul_low(cross_out, rest_t[2])
     normed_three, back_three = jax.vjp(layer_norm, after_cross, norms[4], norms[5])
     normed_three = normed_three.astype(LOW)
-    normed_group = lax.all_gather(normed_three, LAYER, axis=0, tiled=True)
+    normed_group = layer_gather(normed_three, 4).reshape(group_tokens, D)
     gate_both = times_transposed(normed_group, gate_up)
     units = gate_both.shape[1] // 2
     gate_half, up_half = (gate_both[:, :units], gate_both[:, units:])
     inner_act = (jax.nn.silu(gate_half) * up_half).astype(LOW)
     final_state = (
         after_cross
-        + lax.psum_scatter(matmul_low(inner_act, down), LAYER, scatter_dimension=0, tiled=True)
+        + layer_sum(matmul_low(inner_act, down).reshape(RANKS, tokens, D), 5)
     ).astype(LOW)
     predicted = times_transposed(final_state, latent_out)
 
@@ -957,27 +1670,32 @@
 
     grad_out_proj = rows_product(grad_pred, final_state)
     grad_state = matmul_low(grad_pred, latent_out)
-    grad_group = lax.all_gather(grad_state.astype(LOW), LAYER, axis=0, tiled=True)
-    down_slab = lax.psum_scatter(
-        rows_product(inner_act, grad_group), "z", scatter_dimension=0, tiled=True
-    )
-    down_grad = lax.ppermute(down_slab, ALL, [(b, a) for a, b in down_pairs])
+    grad_group = layer_gather(grad_state.astype(LOW), 6).reshape(group_tokens, D)
+    down_part = rows_product(inner_act, grad_group)
     grad_inner = times_transposed(grad_group, down)
     sigmoid_gate = jax.nn.sigmoid(gate_half)
     grad_gate = grad_inner * up_half * sigmoid_gate * (1.0 + gate_half * (1.0 - sigmoid_gate))
     grad_both = jnp.concatenate([grad_gate, grad_inner * gate_half * sigmoid_gate], axis=1).astype(
         LOW
     )
-    gate_up_grad = lax.psum_scatter(
-        rows_product(grad_both, normed_group), "z", scatter_dimension=0, tiled=True
-    )
-    grad_three = lax.psum_scatter(
-        matmul_low(grad_both, gate_up), LAYER, scatter_dimension=0, tiled=True
+    gate_up_part = rows_product(grad_both, normed_group)
+    down_slab = lax.psum_scatter(down_part, "z", scatter_dimension=0, tiled=True)
+    down_grad = lax.ppermute(down_slab, ALL, [(b, a) for a, b in down_pairs])
+    gate_up_part = gate_up_part.reshape(planes, -1, D)
+    early = gate_up_part.shape[1] * 5 // 8
+    early_tops, early_words = line_pack(gate_up_part[:, :early])
+    late_tops, late_words = line_pack(gate_up_part[:, early:])
+    grad_three, early_tops, early_words = layer_sum(
+        matmul_low(grad_both, gate_up).reshape(RANKS, tokens, D),
+        8,
+        (early_tops, early_words),
     )
     residual_part, gain_three, shift_three = back_three(grad_three)
     grad_state = grad_state + residual_part
     grad_branch = grad_state.astype(LOW)
-    grad_cross_out = rows_product(cross_out, grad_branch)
+    grad_cross_out = lax.psum_scatter(
+        rows_product(cross_out, grad_branch), ALL, scatter_dimension=0, tiled=True
+    )
     grad_mix = (
         times_transposed(grad_branch, rest_t[2])
         .astype(LOW)
@@ -999,41 +1717,58 @@
     grad_cross_key = (
         jnp.einsum("bhqk,bqhd->bkhd", pushed, cross_query, preferred_element_type=f32) / score_scale
     )
-    grad_pair = jnp.stack([grad_cross_key, grad_cross_value]).reshape(
-        2, item_count * context_len, D
-    )
-    grad_pair = lax.psum_scatter(grad_pair, LAYER, scatter_dimension=2, tiled=True)
+    grad_pair = jnp.stack([grad_cross_key, grad_cross_value]).reshape(-1, RANKS, COLS)
+    grad_pair = layer_sum(jnp.swapaxes(grad_pair, 0, 1), 9).reshape(
+        2, item_count * context_len, COLS
+    )
     grad_cross_w = jnp.einsum(
         "te,ptc->pec", context_own.astype(f32), grad_pair, precision=HIGHEST
     )
-    grad_cross_w = lax.psum_scatter(grad_cross_w, "z", scatter_dimension=1, tiled=True)
-    cross_grad = lax.all_to_all(grad_cross_w, LAYER, split_axis=1, concat_axis=2, tiled=True)
-    grad_cross_q = rows_product(normed_two, grad_cross_query)
+    grad_cross_q = lax.psum_scatter(
+        rows_product(normed_two, grad_cross_query), ALL, scatter_dimension=0, tiled=True
+    )
     residual_part, gain_two, shift_two = back_two(times_transposed(grad_cross_query, rest_t[1]))
     grad_state = grad_state + residual_part
     grad_branch = grad_state.astype(LOW)
-    grad_self_out = rows_product(mixed_low, grad_branch)
-    grad_mixed = times_transposed(grad_branch, rest_t[0]).astype(LOW)
-    rest_grad = lax.psum_scatter(
-        jnp.stack([grad_self_out, grad_cross_q, grad_cross_out]),
+    branch_group, late_tops, late_words = layer_gather(grad_branch, 2, (late_tops, late_words))
+    branch_group = branch_group.reshape(group_tokens, D)
+    gate_up_grad = jnp.concatenate(
+        [
+            line_total(gate_up_part[:, :early], early_tops, early_words),
+            line_total(gate_up_part[:, early:], late_tops, late_words),
+        ],
+        axis=0,
+    )
+    out_rows = lax.dynamic_slice_in_dim(rest_t[0], rank * COLS, COLS, 0)
+    grad_self_out = lax.psum_scatter(
+        rows_product(mixed_heads.reshape(group_tokens, COLS), branch_group),
+        "z",
+        scatter_dimension=0,
+        tiled=True,
+    )
+    grad_self_out = lax.ppermute(
+        grad_self_out,
         ALL,
-        scatter_dimension=1,
-        tiled=True,
-    )
-    grad_mixed = packed(heads_of(to_heads(grad_mixed)))
-    grad_query, grad_key, grad_value = attend_back(
-        queries, key_rows, values, mixed, log_total, grad_mixed, own_lengths
-    )
-    unpacked = lambda heads: heads.reshape(item_count, LOCAL_HEADS, frames, HEAD_DIM)
-    grad_triple = [
-        flat_of(rotate(unpacked(grad_query), cosine, -sine_table).astype(LOW)),
-        flat_of(rotate(unpacked(grad_key), cosine, -sine_table).astype(LOW)),
-        flat_of(grad_value.astype(LOW)),
-    ]
-    qkv_grad = jnp.stack([rows_product(normed_one, part) for part in grad_triple])
-    qkv_grad = lax.psum_scatter(qkv_grad, "z", scatter_dimension=1, tiled=True)
-    qkv_grad = lax.all_to_all(qkv_grad, LAYER, split_axis=1, concat_axis=2, tiled=True)
-    grad_one = sum(times_transposed(part, qkv_t[i]) for i, part in enumerate(grad_triple))
+        [(RANKS * z + r, planes * r + z) for z in range(planes) for r in range(RANKS)],
+    )
+    rest_grad = jnp.stack([grad_self_out, grad_cross_q, grad_cross_out])
+    grad_mixed = times_transposed(branch_group, out_rows).astype(LOW)
+    grad_triple = attend_back(
+        queries,
+        key_rows,
+        values,
+        mixed,
+        log_total,
+        grad_mixed.reshape(RANKS, item_count, span, COLS),
+        cosine,
+        sine_table,
+        own_lengths,
+    ).reshape(group_tokens, 3 * COLS)
+    qkv_part = rows_product(normed_one, grad_triple).reshape(planes, -1, 3 * COLS)
+    cross_part = jnp.moveaxis(grad_cross_w.reshape(2, planes, -1, COLS), 1, 0).reshape(
+        planes, -1, COLS
+    )
+    grad_one = times_transposed(grad_triple, qkv_t)
     residual_part, gain_one, shift_one = back_one(grad_one)
     grad_in_proj = rows_precise(
         noisy_low.reshape(group_tokens, latent_dim).astype(f32), residual_part
@@ -1053,7 +1788,19 @@
         ],
         axis=0,
     )
-    small_grad = lax.psum_scatter(small_grad, ALL, scatter_dimension=1, tiled=True)
+    by_target = small_grad.T.reshape(planes, 2, 2, 2, -1, small_grad.shape[0])
+    small_grad, qkv_tops, qkv_words, cross_tops, cross_words = full_scatter(
+        jnp.transpose(by_target, (3, 2, 1, 0, 4, 5)),
+        17,
+        line_pack(qkv_part) + line_pack(cross_part),
+    )
+    small_grad = small_grad.T
+    qkv_grad = line_total(qkv_part, qkv_tops, qkv_words)
+    cross_grad = line_total(cross_part, cross_tops, cross_words)
+    cross_grad = jnp.swapaxes(cross_grad.reshape(2, RANKS, -1, COLS), 0, 1)
+    qkv_grad, cross_grad = layer_swap([qkv_grad.reshape(RANKS, -1, 3 * COLS), cross_grad], 14)
+    qkv_grad = jnp.transpose(qkv_grad.reshape(RANKS, -1, 3, COLS), (2, 1, 0, 3)).reshape(3, -1, D)
+    cross_grad = jnp.transpose(cross_grad, (1, 2, 0, 3)).reshape(2, -1, D)
     latent_grad = small_grad[: 2 * LAT].reshape(2, LAT, -1)
     norm_grad = small_grad[2 * LAT : 2 * LAT + 6]
     timing_grad = rows_precise(features_all.astype(f32), small_grad[2 * LAT + 6 :])
@@ -1069,27 +1816,30 @@
         down_grad,
     )
     squares = sum((jnp.sum(grad * grad) for grad in everything))
-    squares, loss_value = lax.psum((squares, partial_loss), ALL)
+    totals = all_fold(lanes_of([squares, partial_loss]), 15, jnp.add)
+    squares, loss_value = (totals[0, 0], totals[0, 1])
     clip_norm = jnp.sqrt(squares)
     factor = CLIP_AT / jnp.maximum(clip_norm, CLIP_AT)
 
     moment_t = 0.95 * flip(attention_moment) + attention_grad * factor
     cross_moment_t = 0.95 * flip(cross_moment) + cross_grad * factor
+    pair = 2 * HEAD_DIM
     blocks = [
-        moment.reshape(moment.shape[0], moment.shape[1], D // HEAD_DIM, HEAD_DIM)
+        moment.reshape(moment.shape[0], moment.shape[1], D // pair, pair)
         for moment in (moment_t, cross_moment_t)
     ]
+    left_lane = jnp.arange(pair) < HEAD_DIM
     grams = jnp.concatenate(
         [
-            jnp.einsum("skbi,skbj->sbij", block, block, precision=HIGHEST).reshape(
-                -1, HEAD_DIM, HEAD_DIM
-            )
+            jnp.einsum("skbi,skbj->sbij", block, block, precision=HIGHEST).reshape(-1, pair, pair)
             for block in blocks
         ]
     )
-    mixers = newton_products(lax.psum_scatter(grams, ALL, scatter_dimension=0, tiled=True))
-    mixers = lax.all_gather(mixers, ALL, axis=0, tiled=True).reshape(
-        -1, D // HEAD_DIM, HEAD_DIM, HEAD_DIM
+    grams = jnp.where(left_lane, grams[:, :HEAD_DIM], grams[:, HEAD_DIM:])
+    mixers = full_newton(grams.reshape(2, 2, 2, planes, -1, pair), 18)
+    mixers = mixers.reshape(-1, D // pair, HEAD_DIM, pair)
+    mixers = jnp.concatenate(
+        [jnp.where(left_lane, mixers, 0.0), jnp.where(left_lane, 0.0, mixers)], axis=2
     )
     stacks = attention_t.shape[0]
     orth = [

time: 1940 us -> 1250 us (0.64)
  waiting for transfers between devices: 1210 us -> 69.3 us
  Pallas kernels: 39.7 us -> 710 us
  blocking collectives: 99.9 us -> 0 us
  matrix products: 225 us -> 188 us
  local copies, waits for them, and re-layouts: 154 us -> 120 us
  starting transfers between devices: 51.3 us -> 23.3 us
    reduce_scatter x8 -> x4, waiting for transfers between devices: 676 us -> 3.07 us  [the longest x1 3.03 us: fast_body(): lax.psum_scatter(rows_product(normed_two, grad_cross_query), ALL, scatter...]
    pallas_call x2 -> x15, Pallas kernels: 39.7 us -> 710 us  [the longest x12 621 us: comm_call(): pl.pallas_call(kernel, out_shape=out_shape, in_specs=[spec] * len(arrays)...]
    all_gather x8 -> x1, waiting for transfers between devices: 294 us -> 3.09 us  [fast_body(): rest_t = lax.all_gather(attention_rest, ALL, axis=1, tiled=True)]
    unnamed x23 -> x8, waiting for transfers between devices: 103 us -> 0.8 us
    all_to_all x4 -> x0, starting transfers between devices: 44.1 us -> none  [the longest x1 32.2 us: fast_body(): lax.all_to_all(qkv_grad, LAYER, split_axis=1, concat_axis=2, tiled=True)]
    all_to_all x4 -> x0, waiting for transfers between devices: 41.7 us -> none  [the longest x1 18.4 us: to_tokens(): lax.all_to_all(moved, LAYER, split_axis=1, concat_axis=3, tiled=True)]
    psum x1 -> x0, blocking collectives: 40.5 us -> none  [fast_body(): squares, loss_value = lax.psum((squares, partial_loss), ALL)]
    all_to_all x2 -> x0, blocking collectives: 32.7 us -> none  [the longest x1 17 us: fast_body(): lax.all_to_all(attention_low[:3], LAYER, split_axis=2, concat_axis=1, til...]
  transfers between devices with their start and end apart: 28 -> 12, of which waited for: 18 -> 4; matrix products, arithmetic and copies ran while one was open for 18% -> 23% of each run, Pallas kernels for 2% -> 41%
where the time goes in v2:
time: 1250 us
  Pallas kernels  710 us (57%)
  matrix products  188 us (15%)
  local copies, waits for them, and re-layouts  120 us (10%)
  other arithmetic  113 us (9%)
  waiting for transfers between devices  69.3 us (6%)
  between operations  23.8 us (2%)
  starting transfers between devices  23.3 us (2%)
    pallas_call x12, Pallas kernels, comm_call(): pl.pallas_call(kernel, out_shape=out_shape, in_specs=[spec] * len(arrays)...  621 us
    dot_general x7, matrix products, times_transposed(): lax.dot_general(left, weight, (((left.ndim - 1,), (1,)), ((), ())), prefe...  56.9 us
    dot_general x7, matrix products, rows_product(): lax.dot_general(left, right, (((0,), (0,)), ((), ())), preferred_element_...  47.9 us
    dot_general x11, matrix products, matmul_low(): return jnp.dot(left, right, preferred_element_type=jnp.float32)  47.1 us
    all_gather x1, waiting for transfers between devices, fast_body(): lax.all_gather(gate_up_weights.astype(LOW), 'z', axis=0, tiled=True)  34 us
    pallas_call x1, Pallas kernels, all_fold(): pl.pallas_call(kernel, out_shape=jax.ShapeDtypeStruct(vector.shape, vecto...  33.8 us
    pallas_call x1, Pallas kernels, attend_back(): pl.pallas_call(attend_back_kernel, grid=(count,), out_shape=jax.ShapeDtyp...  32.7 us
    all_gather x1, waiting for transfers between devices, fast_body(): lax.all_gather(lax.ppermute(down_weights.astype(LOW), ALL, down_pairs), '...  28.4 us
  transfers between devices with their start and end apart: 12, of which 4 were waited for; matrix products, arithmetic and copies ran while one was open for 23% of the time, Pallas kernels for 41%

profile of v2, /device:TPU:0, one launch (start us, length us, event | category | flops | bytes accessed | tf_op | source)
XLA Modules:
  0.0 1247.6 jit_solution(18034104636085045486)
XLA Ops:
  14.2 81.6 %shard_map.448 = (bf16[4,8,192,192]{3,2,1,0:T(8,128)(2,1)S(1)}, bf16[4,8,48,390]{3,2,1,0:T(8,128)(2,1)S(1)}, bf16[4,2,256,64]{3,2,1,0:T(8,128)(2,1)S(1)}, f32[4,8,128]{2,1,0:T(8,128)S(1)}) custom-call(bf16[8,192,192]{2,1,0:T(8,128)(2,1)S(1)} %maximum_bitcast_fusion.w_ref, bf16[48,390]{1,0:T(8,128)(2,1)S(1)} %maximum_bitcast_fusion.1.s_ref, ...), custom_call_target="tpu_custom_call" | custom-call | flops 60000002048 | bytes 1048576 | tf_op jit(solution)/shard_map/pallas_call | solution.py:674
  138.6 22.5 %shard_map.449 = (bf16[2,3,1024,64]{3,2,1,0:T(8,128)(2,1)}, bf16[2,3,1024,64]{3,2,1,0:T(8,128)(2,1)}, bf16[2,3,1024,64]{3,2,1,0:T(8,128)(2,1)}, f32[2,3,1024,64]...) custom-call(s32[2]{0:T(128)} %dynamic-slice_convert_fusion.lengths_ref, ...), custom_call_target="tpu_custom_call" | custom-call | flops 1610612736 | bytes 3932160 | tf_op jit(solution)/shard_map/pallas_call | solution.py:1361
  161.1 31.6 %shard_map.450 = bf16[8,256,192]{2,1,0:T(8,128)(2,1)} custom-call(bf16[8,256,192]{2,1,0:T(8,128)(2,1)} %bitcast.472), custom_call_target="tpu_custom_call" | custom-call | flops 20000000000 | bytes 1048576 | tf_op jit(solution)/shard_map/pallas_call | solution.py:674
  202.7 13.6 %shard_map.451 = bf16[8,512,192]{2,1,0:T(8,128)(2,1)} custom-call(bf16[512,192]{1,0:T(8,128)(2,1)} %bitcast.499), custom_call_target="tpu_custom_call" | custom-call | flops 30000001024 | bytes 1048576 | tf_op jit(solution)/shard_map/pallas_call | solution.py:674
  249.0 31.1 %shard_map.452 = bf16[8,256,1536]{2,1,0:T(8,128)(2,1)} custom-call(bf16[256,1536]{1,0:T(8,128)(2,1)} %add_convert_fusion.4.x_ref), custom_call_target="tpu_custom_call" | custom-call | flops 30000001024 | bytes 1048576 | tf_op jit(solution)/shard_map/pallas_call | solution.py:674
  280.1 34.0 %all-gather.9.cloned.1.call-done = bf16[1536,1536]{1,0:T(8,128)(2,1)} async-done(((bf16[384,1536]{1,0:T(8,128)(2,1)}), bf16[1536,1536]{1,0:T(8,128)(2,1)}) %all-gather.9.cloned.1.call-update) | async-done | bytes 4718608 | tf_op jit(solution)/shard_map/all_gather | solution.py:1593
  314.1 14.2 %fusion.176 = f32[2048,1536]{0,1:T(8,128)S(1)} fusion(bf16[2048,1536]{1,0:T(8,128)(2,1)} %bitcast.514, bf16[1536,1536]{1,0:T(8,128)(2,1)} %all-gather.9.cloned.1.call-done), kind=kOutput, calls=%fused_computation.399 | convolution fusion | flops 9663676416 | bytes 23592960 | tf_op jit(solution)/shard_map/dot_general | solution.py:31
  336.1 28.4 %all-gather.11.cloned.1.call-done = bf16[768,1536]{1,0:T(8,128)(2,1)} async-done(((bf16[192,1536]{1,0:T(8,128)(2,1)}), bf16[768,1536]{1,0:T(8,128)(2,1)}) %all-gather.11.cloned.1.call-update) | async-done | bytes 2359312 | tf_op jit(solution)/shard_map/all_gather | solution.py:1598
  372.2 66.9 %shard_map.453 = f32[256,1536]{1,0:T(8,128)S(1)} custom-call(f32[8,256,1536]{2,1,0:T(8,128)S(1)} %bitcast.446), custom_call_target="tpu_custom_call" | custom-call | flops 65000001536 | bytes 1048576 | tf_op jit(solution)/shard_map/pallas_call | solution.py:674
  444.9 30.6 %shard_map.454 = bf16[8,256,1536]{2,1,0:T(8,128)(2,1)} custom-call(bf16[256,1536]{1,0:T(8,128)(2,1)} %get-tuple-element.376.x_ref), custom_call_target="tpu_custom_call" | custom-call | flops 30000001024 | bytes 1048576 | tf_op jit(solution)/shard_map/pallas_call | solution.py:674
  484.9 12.5 multiply_convert_fusion.1
  498.5 12.3 fusion.178
  518.3 13.1 %fusion.149 = f32[2048,1536]{1,0:T(8,128)} fusion(bf16[1536,1536]{1,0:T(8,128)(2,1)S(1)} %bitcast.512, bf16[2048,768]{0,1:T(8,128)(2,1)S(1)} %get-tuple-element.291, bf16[2048,768]{0,1:T(8,128)(2,1)S(1)} %get-tuple-element.290), kind=kOutput, calls=%fused_computation.377 | convolution fusion | flops 9676259328 | bytes 23592960 | tf_op jit(solution)/shard_map/dot_general | solution.py:37
  531.4 67.1 %shard_map.455 = (f32[256,1536]{1,0:T(8,128)S(1)}, f32[3,4,240]{2,1,0:T(4,128)S(1)}, s32[3,120,1536]{2,1,0:T(8,128)S(1)}) custom-call(f32[8,256,1536]{2,1,0:T(8,128)} %bitcast.513, f32[4,240]{1,0:T(4,128)S(1)} %get-tuple-element.294.refs_0_, s32[4,120,1536]{2,1,0:T(8,128)S(1)} %fusion.17.refs_1_), custom_call_target="tpu_custom_call" | custom-call | flops 65000001536 | bytes 1048576 | tf_op jit(solution)/shard_map/pallas_call | solution.py:674
  628.7 63.0 %shard_map.456 = (bf16[8,256,1536]{2,1,0:T(8,128)(2,1)}, f32[3,4,144]{2,1,0:T(4,128)}, s32[3,72,1536]{2,1,0:T(8,128)}) custom-call(bf16[256,1536]{1,0:T(8,128)(2,1)} %convert_element_type.235.x_ref, f32[4,144]{1,0:T(4,128)} %copy-done.102, s32[4,72,1536]{2,1,0:T(8,128)} %fusion.32.refs_1_), custom_call_target="tpu_custom_call" | custom-call | flops 30000001024 | bytes 1048576 | tf_op jit(solution)/shard_map/pallas_call | solution.py:674
  716.3 32.7 %shard_map.457 = bf16[2,1024,576]{2,1,0:T(8,128)(2,1)} custom-call(s32[2]{0:T(128)} %dynamic-slice_convert_fusion.lengths_ref, bf16[2,3,1024,64]{3,2,1,0:T(8,128)(2,1)} %get-tuple-element.57.q_ref, bf16[2,3,1024,64]{3,2,1,0:T(8,128)(2,1)} %get-tuple-element.58.k_ref, bf16[2,3,1024,64]{3,2,1,0:T(8,128)(2,1)} %get-tuple-element.59.v_ref, ...), custom_call_target="tpu_custom_call" | custom-call | flops 4026531840 | bytes 9437184 | tf_op jit(solution)/shard_map/pallas_call | solution.py:1456
  749.1 14.2 %multiply_reduce_fusion = (f32[1536]{0:T(1024)S(1)}, f32[2048]{0:T(1024)S(1)}, f32[1536]{0:T(1024)S(1)}, f32[2048,1536]{1,0:T(8,128)}) fusion(f32[2,1024,1536]{2,1,0:T(8,128)} %copy-done.7, f32[2048]{0:T(1024)S(1)} %bitcast_rsqrt_fusion, f32[2048]{0:T(1024)S(1)} %bitcast.501, f32[1536]{0:T(1024)S(1)} %copy-done.91, bf16[2048,576]{1,0:T(8,128)(2,1)} %bitcast.481, ...), kind=kOutput, calls=%fused_computation.4 | convolution fusion | flops 3654347776 | bytes 29337600 | tf_op jit(solution)/shard_map/dot_general | solution.py:31
  763.4 13.6 %fusion.159 = (f32[2048]{0:T(1024)S(1)}, f32[2048,1536]{1,0:T(8,128)}, bf16[2048,1536]{1,0:T(8,128)(2,1)}) fusion(f32[2048]{0:T(1024)S(1)} %fusion.116, f32[2048]{0:T(1024)S(1)} %bitcast.502, f32[2,1024,1536]{2,1,0:T(8,128)S(1)} %bitcast.448, f32[2048]{0:T(1024)S(1)} %bitcast_rsqrt_fusion, f32[2048,1536]{1,0:T(8,128)} %get-tuple-element.381, ...), kind=kLoop, calls=%fused_computation.382 | loop fusion | flops 34600960 | bytes 44085248 | tf_op jit(solution)/shard_map/transpose(jvp())/reduce_sum | solution.py:51
  840.9 32.4 %shard_map.458 = f32[512,192]{1,0:T(8,128)S(1)} custom-call(f32[8,512,192]{2,1,0:T(8,128)S(1)} %bitcast.429), custom_call_target="tpu_custom_call" | custom-call | flops 24999999488 | bytes 1048576 | tf_op jit(solution)/shard_map/pallas_call | solution.py:674
  897.1 112.4 %shard_map.459 = (f32[48,142]{1,0:T(8,128)S(1)}, f32[3,4,384]{2,1,0:T(4,128)S(1)}, s32[3,192,576]{2,1,0:T(8,128)S(1)}, f32[3,4,384]{2,1,0:T(4,128)S(1)}, s32[3,192,192]{2,1,0:T(8,128)S(1)}) custom-call(f32[2,2,2,4,48,142]{5,4,3,2,1,0:T(8,128)S(1)} %bitcast.437, f32[4,384]{1,0:T(4,128)S(1)} %get-tuple-element.382.refs_0_, s32[4,192,576]{2,1,0:T(8,128)S(1)} %fusion.28.refs_1_, ...), custom_call_target="tpu_custom_call" | custom-call | flops 40000000000 | bytes 1048576 | tf_op jit(solution)/shard_map/pallas_call | solution.py:674
  1023.6 25.0 %shard_map.460 = (f32[8,48,576]{2,1,0:T(8,128)}, f32[8,2,24,192]{3,2,1,0:T(8,128)}) custom-call(f32[8,48,576]{2,1,0:T(8,128)} %multiply_add_fusion.2.refs_0_, f32[8,2,24,192]{3,2,1,0:T(8,128)} %fusion.87.refs_1_), custom_call_target="tpu_custom_call" | custom-call | flops 20000000000 | bytes 1048576 | tf_op jit(solution)/shard_map/pallas_call | solution.py:674
  1048.7 10.9 collective-permute-start.3
  1091.8 33.8 %shard_map.461 = f32[8,128]{1,0:T(8,128)} custom-call(f32[8,128]{1,0:T(8,128)} %broadcast_in_dim.95.v_ref), custom_call_target="tpu_custom_call" | custom-call | tf_op jit(solution)/shard_map/pallas_call | solution.py:978
  1149.4 66.1 %shard_map.462 = f32[2,2,2,4,192,128]{5,4,3,2,1,0:T(8,128)S(1)} custom-call(f32[2,2,2,4,192,128]{5,4,3,2,1,0:T(8,128)S(1)} %bitcast.436), custom_call_target="tpu_custom_call" | custom-call | flops 20000000000 | bytes 1048576 | tf_op jit(solution)/shard_map/pallas_call | solution.py:674
  (552 shorter events, 360.4 us)
Async XLA Ops:
  7.2 192.5 %all-gather.7.cloned.1.call-start = ((), (), s32[]{:S(2)}) async-start(), calls=%async_computation.5 | async-start | bytes 1966080 | tf_op jit(solution)/shard_map/all_gather | solution.py:1588
  7.9 216.2 %all-gather.5.cloned.1.call-start = ((), (), s32[]{:S(2)}) async-start(), calls=%async_computation.4 | async-start | bytes 14598144 | tf_op jit(solution)/shard_map/all_gather | solution.py:1592
  14.2 83.3 %copy-start.33 = (f32[192,1536]{1,0:T(8,128)S(1)}, f32[192,1536]{1,0:T(8,128)}, u32[]{:S(2)}) copy-start(f32[192,1536]{1,0:T(8,128)} %param.38) | copy-start | bytes 3538948
  97.5 216.5 %all-gather.9.cloned.1.call-start = ((), (), s32[]{:S(2)}) async-start(), calls=%async_computation.6 | async-start | bytes 5898240 | tf_op jit(solution)/shard_map/all_gather | solution.py:1593
  98.6 101.0 %collective-permute-start = (bf16[192,1536]{1,0:T(8,128)(2,1)}, bf16[192,1536]{1,0:T(8,128)(2,1)}, u32[]{:S(2)}, u32[]{:S(2)}) collective-permute-start(bf16[192,1536]{1,0:T(8,128)(2,1)} %convert_element_type.224), channel_id=1, source_target_pairs={{0,0},{2,1},{4,2},{6,3},{8,4},{10,5},{12,6},{14,7},{1,8},{3,9},{5,... | collective-permute-start | bytes 1769480 | tf_op jit(solution)/shard_map/ppermute | solution.py:1599
  104.6 334.9 %collective-permute-start.1 = (f32[2,128,64]{1,2,0:T(8,128)}, f32[2,128,64]{1,2,0:T(8,128)}, u32[]{:S(2)}, u32[]{:S(2)}) collective-permute-start(f32[2,128,64]{1,2,0:T(8,128)} %get-tuple-element.340), channel_id=1, source_target_pairs={{0,0},{1,8},{2,16},{3,24},{4,1},{5,9},{6,17},{7,25},{8,2},{9,10},{... | collective-permute-start | bytes 196616 | tf_op jit(solution)/shard_map/ppermute | solution.py:1585
  109.5 255.0 %all-gather.11.cloned.1.call-start = ((), (), s32[]{:S(2)}) async-start(), calls=%async_computation.7 | async-start | bytes 2949120 | tf_op jit(solution)/shard_map/all_gather | solution.py:1598
  110.8 81.9 %copy-start.122 = (s32[128]{0:T(128)}, s32[128]{0:T(128)S(1)}, u32[]{:S(2)}) copy-start(s32[128]{0:T(128)S(1)} %iota_add_fusion) | copy-start | bytes 1540
  119.5 73.2 %copy-start.124 = (f32[2]{0:T(128)}, f32[2]{0:T(128)S(1)}, u32[]{:S(2)}) copy-start(f32[2]{0:T(128)S(1)} %convolution_bitcast_fusion.2) | copy-start | bytes 28
  119.7 109.4 %copy-start.66 = (f32[1536]{0:T(1024)}, f32[1536]{0:T(1024)S(1)}, u32[]{:S(2)}) copy-start(f32[1536]{0:T(1024)S(1)} %get-tuple-element.251) | copy-start | bytes 18436
  119.7 109.4 %copy-start.78 = (f32[1536]{0:T(1024)}, f32[1536]{0:T(1024)S(1)}, u32[]{:S(2)}) copy-start(f32[1536]{0:T(1024)S(1)} %get-tuple-element.250) | copy-start | bytes 18436
  119.7 128.1 %copy-start.69 = (f32[1536]{0:T(1024)}, f32[1536]{0:T(1024)S(1)}, u32[]{:S(2)}) copy-start(f32[1536]{0:T(1024)S(1)} %get-tuple-element.248) | copy-start | bytes 18436
  199.6 849.0 %reduce-scatter.11.cloned.1.call-start = ((), (), s32[]{:S(2)}) async-start(), calls=%async_computation.11 | async-start | bytes 5898240 | tf_op jit(solution)/shard_map/reduce_scatter | solution.py:1682
  247.4 191.7 %copy-start.9 = (f32[256,1536]{1,0:T(8,128)}, f32[256,1536]{1,0:T(8,128)S(1)}, u32[]{:S(2)}) copy-start(f32[256,1536]{1,0:T(8,128)S(1)} %get-tuple-element.375) | copy-start | bytes 4718596
  531.4 68.5 %copy-start.94 = (f32[256]{0:T(256)S(1)}, f32[256]{0:T(256)}, u32[]{:S(2)}) copy-start(f32[256]{0:T(256)} %copy-done.93) | copy-start | bytes 3076
  531.4 68.5 %copy-start.107 = (f32[256]{0:T(256)S(1)}, f32[256]{0:T(256)}, u32[]{:S(2)}) copy-start(f32[256]{0:T(256)} %copy-done.106) | copy-start | bytes 3076
  600.6 463.5 %reduce-scatter.5.cloned.1.call-start = ((), (), s32[]{:S(2)}) async-start(), calls=%async_computation.8 | async-start | bytes 1474560 | tf_op jit(solution)/shard_map/reduce_scatter | solution.py:1743
  697.3 383.4 %reduce-scatter.9.cloned.1.call-start = ((), (), s32[]{:S(2)}) async-start(), calls=%async_computation.10 | async-start | bytes 9732096 | tf_op jit(solution)/shard_map/reduce_scatter | solution.py:1696
  706.3 377.3 %reduce-scatter.7.cloned.1.call-start = ((), (), s32[]{:S(2)}) async-start(), calls=%async_computation.9 | async-start | bytes 9732096 | tf_op jit(solution)/shard_map/reduce_scatter | solution.py:1727
  897.1 115.9 %copy-start.116 = (s32[2]{0:T(128)S(1)}, s32[2]{0:T(128)}, u32[]{:S(2)}) copy-start(s32[2]{0:T(128)} %dynamic-slice_convert_fusion.lengths_ref) | copy-start | bytes 28
  897.1 115.8 %copy-start.117 = (f32[256]{0:T(256)S(1)}, f32[256]{0:T(256)}, u32[]{:S(2)}) copy-start(f32[256]{0:T(256)} %get-tuple-element.343) | copy-start | bytes 3076
  897.1 115.8 %copy-start.123 = (s32[128]{0:T(128)S(1)}, s32[128]{0:T(128)}, u32[]{:S(2)}) copy-start(s32[128]{0:T(128)} %copy-done.122) | copy-start | bytes 1540
  1048.7 29.7 %collective-permute-start.3 = (f32[192,1536]{1,0:T(8,128)}, f32[192,1536]{1,0:T(8,128)}, u32[]{:S(2)}, u32[]{:S(2)}) collective-permute-start(f32[192,1536]{1,0:T(8,128)} %reduce-scatter.11.cloned.1.call-done), channel_id=1, source_target_pairs={{0,0},{1,2},{2,4},{3,6},{4,8},{5,10},{6,12},{7,14},{8,1},{9,3},{10... | collective-permute-start | bytes 3538952 | tf_op jit(solution)/shard_map/ppermute | solution.py:1683
  1064.2 16.5 %collective-permute-start.2 = (f32[48,1536]{1,0:T(8,128)}, f32[48,1536]{1,0:T(8,128)}, u32[]{:S(2)}, u32[]{:S(2)}) collective-permute-start(f32[48,1536]{1,0:T(8,128)} %reduce-scatter.5.cloned.1.call-done), channel_id=1, source_target_pairs={{0,0},{1,4},{2,8},{3,12},{4,16},{5,20},{6,24},{7,28},{8,1},{9,5},{... | collective-permute-start | bytes 884744 | tf_op jit(solution)/shard_map/ppermute | solution.py:1749
  (126 other events, 1108.7 us)
Sparse Core Ops, SparseCore 0:
  9.6 30.7 all-gather.6
  97.6 126.4 all-gather.4
  226.2 87.7 all-gather.8
  315.5 48.9 all-gather.10
  600.8 112.8 reduce-scatter.10
  716.4 37.7 reduce-scatter.4
  760.2 140.4 reduce-scatter.8
  907.6 176.0 reduce-scatter.6

commit v3 on v2

--- a/solution.py
+++ b/solution.py
@@ -1,3 +1,4 @@
+import functools
 import math
 
 import jax
@@ -736,257 +737,278 @@
     return total
 
 
-def layer_swap(arrays, ident):
-    count = len(arrays)
+def putter(sent, got):
+    count = [0]
+
+    def put(src, dst, peer):
+        at = count[0]
+        count[0] += 1
+        copy = pltpu.make_async_remote_copy(
+            src_ref=src,
+            dst_ref=dst,
+            send_sem=sent.at[at],
+            recv_sem=got.at[at],
+            device_id=device_of(peer),
+            device_id_type=MESH,
+        )
+        copy.start()
+        return copy
+
+    return put
+
+
+def swap_flow(me, put, x_ref, o_ref, own):
+    mine = rank_of(me)
+    peers = [turned(me, flip) for flip in LAYER_FLIPS]
+    copies = [put(x_ref.at[rank_of(peer)], o_ref.at[mine], peer) for peer in peers]
+    local = pltpu.make_async_copy(x_ref.at[mine], o_ref.at[mine], own)
+    local.start()
+    yield
+    local.wait()
+    for copy in copies:
+        copy.wait()
+
+
+def gather_flow(me, put, x_ref, o_ref, own):
+    half = x_ref.shape[0] // 2
+    by_x, by_y, by_xy = (turned(me, (0, y, x, 0)) for y, x in ((0, 1), (1, 0), (1, 1)))
+    other = turned(me, (0, 0, 0, 1))
+    slot = o_ref.at[rank_of(me)]
+    first, second = pl.ds(0, half), pl.ds(half, half)
+    copies = [
+        put(x_ref.at[first], slot.at[first], by_x),
+        put(x_ref.at[second], slot.at[second], by_y),
+        put(x_ref.at[second], slot.at[second], by_x),
+        put(x_ref.at[first], slot.at[first], by_y),
+        put(x_ref, slot, other),
+    ]
+    local = pltpu.make_async_copy(x_ref, slot, own)
+    local.start()
+    from_x, from_y, from_xy = (o_ref.at[rank_of(p)] for p in (by_x, by_y, by_xy))
+    yield
+    copies[0].wait_recv()
+    copies.append(put(from_x.at[first], from_x.at[first], by_y))
+    copies[1].wait_recv()
+    copies.append(put(from_y.at[second], from_y.at[second], by_x))
+    yield
+    copies[2].wait_recv()
+    copies.append(put(from_x, from_x, other))
+    copies[3].wait_recv()
+    copies.append(put(from_y, from_y, other))
+    yield
+    copies[5].wait_recv()
+    copies[6].wait_recv()
+    copies.append(put(from_xy, from_xy, other))
+    local.wait()
+    for i in (4, 7, 8, 9):
+        copies[i].wait_recv()
+    for copy in copies:
+        copy.wait_send()
+
+
+def encode(value, words, steps):
+    half = value.shape[0] // 2
+    top = jnp.max(jnp.abs(value), axis=1, keepdims=True)
+    codes = jnp.round(value * (LEVELS / jnp.maximum(top, 1e-30))).astype(jnp.int32)
+    words[...] = lax.shift_left(codes[:half], 16) | (codes[half:] & 65535)
+    steps[...] = jnp.broadcast_to(top * (1.0 / LEVELS), steps.shape)
+
+
+def decode(words, steps):
+    values = words[...]
+    high = lax.shift_right_arithmetic(values, 16)
+    low = lax.shift_right_arithmetic(lax.shift_left(values, 16), 16)
+    return jnp.concatenate([high, low], axis=0).astype(jnp.float32) * steps[:, 0:1]
+
+
+def sum_flow(me, put, p_ref, o_ref, own, mine, theirs, out_words, out_steps, in_words, in_steps):
+    half = mine.shape[1] // 2
+    by_x, by_y = (turned(me, flip) for flip in ((0, 0, 1, 0), (0, 1, 0, 0)))
+    other = turned(me, (0, 0, 0, 1))
+    cores, locals_ = [], []
+    for slot in (3, 2, 1, 0):
+        chip = turned(me, (0, slot // 2, slot % 2, 0))
+        local = pltpu.make_async_copy(p_ref.at[rank_of(chip)], mine.at[slot], own.at[slot])
+        local.start()
+        locals_.append(local)
+        cores.append(put(p_ref.at[rank_of(turned(chip, (0, 0, 0, 1)))], theirs.at[slot], other))
+    first, second = pl.ds(0, half), pl.ds(half, half)
+    copies = []
+
+    def pass_on(unit, slot, rows, peer):
+        encode(mine[slot, rows, :], out_words.at[unit], out_steps.at[unit])
+        copies.append(
+            (
+                put(out_words.at[unit], in_words.at[unit], peer),
+                put(out_steps.at[unit], in_steps.at[unit], peer),
+            )
+        )
+
+    def take_in(unit, slot, rows):
+        for copy in copies[unit]:
+            copy.wait_recv()
+        mine[slot, rows, :] = mine[slot, rows, :] + decode(in_words.at[unit], in_steps.at[unit])
+
+    for i, slot in enumerate((3, 2, 1, 0)):
+        locals_[i].wait()
+        cores[i].wait_recv()
+        mine[slot] = mine[slot] + theirs[slot]
+        if slot == 3:
+            pass_on(0, 3, first, by_x)
+            pass_on(1, 3, second, by_y)
+        if slot == 2:
+            pass_on(2, 2, second, by_y)
+        if slot == 1:
+            pass_on(3, 1, first, by_x)
+    yield
+    take_in(0, 2, first)
+    pass_on(4, 2, first, by_y)
+    take_in(1, 1, second)
+    pass_on(5, 1, second, by_x)
+    yield
+    take_in(3, 0, first)
+    take_in(2, 0, second)
+    yield
+    take_in(4, 0, first)
+    take_in(5, 0, second)
+    done = pltpu.make_async_copy(mine.at[0], o_ref, own.at[4])
+    done.start()
+    done.wait()
+    for copy in cores + [copy for pair in copies for copy in pair]:
+        copy.wait_send()
+
+
+def everyone_flow(me, put, x_ref, o_ref, own):
+    slot = o_ref.at[RANKS * me[0] + rank_of(me)]
+    copies = [put(x_ref, slot, turned(me, flip)) for flip in ALL_FLIPS]
+    local = pltpu.make_async_copy(x_ref, slot, own)
+    local.start()
+    yield
+    local.wait()
+    for copy in copies:
+        copy.wait()
+
+
+def down_owner(z_at, rank):
+    block = 2 * RANKS * (z_at // 2) + 2 * rank + z_at % 2
+    return block // RANKS, block % RANKS
+
+
+def move_flow(me, x_ref, o_ref, sent, got, own):
+    z_at, mine = me[0], rank_of(me)
+    to_z, to_rank = down_owner(z_at, mine)
+    stays = (to_z == z_at) & (to_rank == mine)
+    remote = pltpu.make_async_remote_copy(
+        src_ref=x_ref,
+        dst_ref=o_ref,
+        send_sem=sent,
+        recv_sem=got,
+        device_id=(to_z, to_rank // 4, to_rank % 4),
+        device_id_type=MESH,
+    )
+    local = pltpu.make_async_copy(x_ref, o_ref, own)
+
+    @pl.when(stays)
+    def _():
+        local.start()
+
+    @pl.when(jnp.logical_not(stays))
+    def _():
+        remote.start()
+
+    yield
+
+    @pl.when(stays)
+    def _():
+        local.wait()
+
+    @pl.when(jnp.logical_not(stays))
+    def _():
+        remote.wait()
+
+
+ALL_FLIPS = [(z, y, x, c) for z in range(4) for y in range(2) for x in range(2) for c in range(2)][1:]
+
+
+def plane_step(ident, cost_us, sums=(), gathers=(), swaps=(), everyone=(), moves=(), carry=()):
+    n_sum, n_gather, n_swap, n_carry = len(sums), len(gathers), len(swaps), len(carry)
+    n_all = len(everyone)
+    n_move = len(moves)
+    total = n_sum + n_gather + n_swap + n_all + n_move + n_carry
+    f32 = jnp.float32
+    n_put = 16 * n_sum + 10 * n_gather + 7 * n_swap + 31 * n_all + n_move
 
     def kernel(*refs):
-        x_refs, o_refs, (sent, got, own) = refs[:count], refs[count : 2 * count], refs[2 * count :]
+        ins, outs, scratch = refs[:total], refs[total : 2 * total], refs[2 * total :]
+        sent, got, own, line_sent, line_got = scratch[:5]
         me = place()
-        peers = [turned(me, flip) for flip in LAYER_FLIPS]
+        if n_all:
+            peers = [turned(me, flip) for flip in ALL_FLIPS]
+        elif n_swap:
+            peers = [turned(me, flip) for flip in LAYER_FLIPS]
+        else:
+            peers = [turned(me, flip) for flip in ((0, 0, 1, 0), (0, 1, 0, 0), (0, 0, 0, 1))]
+        if n_carry and not n_all:
+            peers = peers + [turned(me, flip) for flip in LINE_FLIPS]
         greet(peers)
-        mine = rank_of(me)
-        copies = [
-            pltpu.make_async_remote_copy(
-                src_ref=x_refs[j].at[rank_of(peer)],
-                dst_ref=o_refs[j].at[mine],
-                send_sem=sent.at[j, i],
-                recv_sem=got.at[j, i],
-                device_id=device_of(peer),
-                device_id_type=MESH,
-            )
-            for i, peer in enumerate(peers)
-            for j in range(count)
+        put = putter(sent, got)
+        carried = line_start(me, ins[total - n_carry :], outs[total - n_carry :], line_sent, line_got)
+        flows = []
+        for i in range(total - n_carry):
+            if i < n_sum:
+                flows.append(
+                    sum_flow(me, put, ins[i], outs[i], own.at[i], *scratch[5 + 6 * i : 11 + 6 * i])
+                )
+            elif i < n_sum + n_gather:
+                flows.append(gather_flow(me, put, ins[i], outs[i], own.at[i, 0]))
+            elif i >= n_sum + n_gather + n_swap + n_all:
+                at = n_put - n_move + (i - (n_sum + n_gather + n_swap + n_all))
+                flows.append(
+                    move_flow(me, ins[i], outs[i], sent.at[at], got.at[at], own.at[i, 0])
+                )
+            elif i >= n_sum + n_gather + n_swap:
+                flows.append(everyone_flow(me, put, ins[i], outs[i], own.at[i, 0]))
+            else:
+                flows.append(swap_flow(me, put, ins[i], outs[i], own.at[i, 0]))
+        for _ in range(8):
+            for flow in flows:
+                next(flow, None)
+        for copy in carried:
+            copy.wait()
+
+    dma = pltpu.SemaphoreType.DMA
+    shape = jax.ShapeDtypeStruct
+    outs = [shape(a.shape[1:], f32) for a in sums]
+    outs += [shape((RANKS,) + a.shape, a.dtype) for a in gathers]
+    outs += [shape(a.shape, a.dtype) for a in swaps]
+    outs += [shape((len(ALL_FLIPS) + 1,) + a.shape, a.dtype) for a in everyone]
+    outs += [shape(a.shape, a.dtype) for a in moves]
+    scratch = [
+        dma((n_put,)),
+        dma((n_put,)),
+        dma((total, 5)),
+        dma((max(n_carry, 1), 3)),
+        dma((max(n_carry, 1), 3)),
+    ]
+    for a in sums:
+        rows, lanes = a.shape[1:]
+        scratch += [
+            pltpu.VMEM((4, rows, lanes), f32),
+            pltpu.VMEM((4, rows, lanes), f32),
+            pltpu.VMEM((6, rows // 4, lanes), jnp.int32),
+            pltpu.VMEM((6, rows // 2, 128), f32),
+            pltpu.VMEM((6, rows // 4, lanes), jnp.int32),
+            pltpu.VMEM((6, rows // 2, 128), f32),
         ]
-        for copy in copies:
-            copy.start()
-        for j in range(count):
-            local = pltpu.make_async_copy(x_refs[j].at[mine], o_refs[j].at[mine], own.at[j])
-            local.start()
-            local.wait()
-        for copy in copies:
-            copy.wait()
-
-    dma = pltpu.SemaphoreType.DMA
     return comm_call(
         kernel,
-        tuple(jax.ShapeDtypeStruct(a.shape, a.dtype) for a in arrays),
-        tuple(arrays),
-        [dma((count, 7)), dma((count, 7)), dma((count,))],
+        tuple(outs) + line_shapes(carry),
+        tuple(sums) + tuple(gathers) + tuple(swaps) + tuple(everyone) + tuple(moves) + tuple(carry),
+        scratch,
         ident,
-    )
-
-
-def layer_gather(array, ident, carry=()):
-    half = array.shape[0] // 2
-    extra = len(carry)
-
-    def kernel(x_ref, *refs):
-        carry_in, o_ref, carry_out = refs[:extra], refs[extra], refs[extra + 1 : 2 * extra + 1]
-        sent, got, own, csent, cgot = refs[2 * extra + 1 :]
-        me = place()
-        by_x, by_y, by_xy = (turned(me, (0, y, x, 0)) for y, x in ((0, 1), (1, 0), (1, 1)))
-        other = turned(me, (0, 0, 0, 1))
-        line = [turned(me, flip) for flip in LINE_FLIPS] if extra else []
-        greet([by_x, by_y, other] + line)
-        carried = line_start(me, carry_in, carry_out, csent, cgot)
-
-        def send(which, src, dst, peer):
-            copy = pltpu.make_async_remote_copy(
-                src_ref=src,
-                dst_ref=dst,
-                send_sem=sent.at[which],
-                recv_sem=got.at[which],
-                device_id=device_of(peer),
-                device_id_type=MESH,
-            )
-            copy.start()
-            return copy
-
-        slot = o_ref.at[rank_of(me)]
-        first, second = pl.ds(0, half), pl.ds(half, half)
-        copies = [
-            send(0, x_ref.at[first], slot.at[first], by_x),
-            send(1, x_ref.at[second], slot.at[second], by_y),
-            send(2, x_ref.at[second], slot.at[second], by_x),
-            send(3, x_ref.at[first], slot.at[first], by_y),
-            send(4, x_ref, slot, other),
-        ]
-        local = pltpu.make_async_copy(x_ref, slot, own)
-        local.start()
-        from_x, from_y, from_xy = (o_ref.at[rank_of(p)] for p in (by_x, by_y, by_xy))
-        copies[0].wait_recv()
-        copies.append(send(5, from_x.at[first], from_x.at[first], by_y))
-        copies[1].wait_recv()
-        copies.append(send(6, from_y.at[second], from_y.at[second], by_x))
-        copies[2].wait_recv()
-        copies.append(send(7, from_x, from_x, other))
-        copies[3].wait_recv()
-        copies.append(send(8, from_y, from_y, other))
-        copies[5].wait_recv()
-        copies[6].wait_recv()
-        copies.append(send(9, from_xy, from_xy, other))
-        local.wait()
-        for i in (4, 7, 8, 9):
-            copies[i].wait_recv()
-        for copy in copies:
-            copy.wait_send()
-        for copy in carried:
-            copy.wait()
-
-    dma = pltpu.SemaphoreType.DMA
-    out = comm_call(
-        kernel,
-        (jax.ShapeDtypeStruct((RANKS,) + array.shape, array.dtype),) + line_shapes(carry),
-        (array,) + tuple(carry),
-        [dma((10,)), dma((10,)), dma] + [dma((max(extra, 1), 3))] * 2,
-        ident,
-        cost_us=30,
-    )
-    return out if extra else out[0]
-
-
-def layer_sum(array, ident, carry=(), low=jnp.float32):
-    _, rows, width = array.shape
-    half = rows // 2
-    f32 = jnp.float32
-
-    extra = len(carry)
-
-    def kernel(p_ref, *refs):
-        carry_in, o_ref, carry_out = refs[:extra], refs[extra], refs[extra + 1 : 2 * extra + 1]
-        mine, theirs, out_one, in_one, out_two, in_two, sent, got, own, csent, cgot = refs[
-            2 * extra + 1 :
-        ]
-        me = place()
-        z_at, y_at, x_at, core = me
-        by_x, by_y = (turned(me, flip) for flip in ((0, 0, 1, 0), (0, 1, 0, 0)))
-        other = turned(me, (0, 0, 0, 1))
-        line = [turned(me, flip) for flip in LINE_FLIPS] if extra else []
-        greet([by_x, by_y, other] + line)
-        carried = line_start(me, carry_in, carry_out, csent, cgot)
-
-        def send(which, src, dst, peer):
-            copy = pltpu.make_async_remote_copy(
-                src_ref=src,
-                dst_ref=dst,
-                send_sem=sent.at[which],
-                recv_sem=got.at[which],
-                device_id=device_of(peer),
-                device_id_type=MESH,
-            )
-            copy.start()
-            return copy
-
-        cores, locals_ = [], []
-        for dy in (1, 0):
-            for dx in (1, 0):
-                slot = 2 * dy + dx
-                chip = turned(me, (0, dy, dx, 0))
-                local = pltpu.make_async_copy(p_ref.at[rank_of(chip)], mine.at[slot], own.at[slot])
-                local.start()
-                locals_.append(local)
-                cores.append(
-                    send(slot, p_ref.at[rank_of(turned(chip, (0, 0, 0, 1)))], theirs.at[slot], other)
-                )
-        first, second = pl.ds(0, half), pl.ds(half, half)
-        for i, slot in enumerate((3, 2, 1, 0)):
-            locals_[i].wait()
-            cores[i].wait_recv()
-            mine[slot] = mine[slot] + theirs[slot]
-        for k, slot in enumerate((3, 1)):
-            out_one[0, k] = mine[slot, first, :].astype(low)
-        over_x = send(4, out_one.at[0], in_one.at[0], by_x)
-        for k, slot in enumerate((3, 2)):
-            out_one[1, k] = mine[slot, second, :].astype(low)
-        over_y = send(5, out_one.at[1], in_one.at[1], by_y)
-        over_x.wait_recv()
-        out_two[0] = (mine[2, first, :] + in_one[0, 0].astype(f32)).astype(low)
-        next_y = send(6, out_two.at[0], in_two.at[0], by_y)
-        over_y.wait_recv()
-        out_two[1] = (mine[1, second, :] + in_one[1, 0].astype(f32)).astype(low)
-        next_x = send(7, out_two.at[1], in_two.at[1], by_x)
-        mine[0, first, :] = mine[0, first, :] + in_one[0, 1].astype(f32)
-        mine[0, second, :] = mine[0, second, :] + in_one[1, 1].astype(f32)
-        next_y.wait_recv()
-        mine[0, first, :] = mine[0, first, :] + in_two[0].astype(f32)
-        next_x.wait_recv()
-        mine[0, second, :] = mine[0, second, :] + in_two[1].astype(f32)
-        done = pltpu.make_async_copy(mine.at[0], o_ref, own.at[4])
-        done.start()
-        done.wait()
-        for copy in cores + [over_x, over_y, next_y, next_x]:
-            copy.wait_send()
-        for copy in carried:
-            copy.wait()
-
-    dma = pltpu.SemaphoreType.DMA
-    out = comm_call(
-        kernel,
-        (jax.ShapeDtypeStruct((rows, width), f32),) + line_shapes(carry),
-        (array,) + tuple(carry),
-        [
-            pltpu.VMEM((4, rows, width), f32),
-            pltpu.VMEM((4, rows, width), f32),
-            pltpu.VMEM((2, 2, half, width), low),
-            pltpu.VMEM((2, 2, half, width), low),
-            pltpu.VMEM((2, half, width), low),
-            pltpu.VMEM((2, half, width), low),
-            dma((8,)),
-            dma((8,)),
-            dma((5,)),
-        ]
-        + [dma((max(extra, 1), 3))] * 2,
-        ident,
-        vmem=True,
-        cost_us=65 if rows * width > 300000 else 25,
-    )
-    return out if extra else out[0]
-
-
-def all_fold(vector, ident, fold):
-    flips = [(z, y, x, c) for z in range(4) for y in range(2) for x in range(2) for c in range(2)][1:]
-    count = len(flips)
-
-    def kernel(v_ref, o_ref, slots, sent, got):
-        me = place()
-        peers = [turned(me, flip) for flip in flips]
-        greet(peers)
-        mine = RANKS * me[0] + rank_of(me)
-        slots[mine] = v_ref[...]
-        copies = [
-            pltpu.make_async_remote_copy(
-                src_ref=v_ref,
-                dst_ref=slots.at[mine],
-                send_sem=sent.at[i],
-                recv_sem=got.at[i],
-                device_id=device_of(peer),
-                device_id_type=MESH,
-            )
-            for i, peer in enumerate(peers)
-        ]
-        for copy in copies:
-            copy.start()
-        for copy in copies:
-            copy.wait()
-        total = slots[0]
-        for i in range(1, count + 1):
-            total = fold(total, slots[i])
-        o_ref[...] = total
-
-    dma = pltpu.SemaphoreType.DMA
-    spec = pl.BlockSpec(memory_space=pltpu.VMEM)
-    return pl.pallas_call(
-        kernel,
-        out_shape=jax.ShapeDtypeStruct(vector.shape, vector.dtype),
-        in_specs=[spec],
-        out_specs=spec,
-        scratch_shapes=[
-            pltpu.VMEM((count + 1,) + vector.shape, vector.dtype),
-            dma((count,)),
-            dma((count,)),
-        ],
-        compiler_params=pltpu.CompilerParams(collective_id=ident, has_side_effects=True),
-    )(vector)
+        vmem=bool(sums),
+        cost_us=cost_us,
+    )
 
 
 def lanes_of(values):
@@ -1023,26 +1045,6 @@
         next_y,
         next_x,
     ] + sends
-
-
-def putter(sent, got):
-    count = [0]
-
-    def put(src, dst, peer):
-        at = count[0]
-        count[0] += 1
-        copy = pltpu.make_async_remote_copy(
-            src_ref=src,
-            dst_ref=dst,
-            send_sem=sent.at[at],
-            recv_sem=got.at[at],
-            device_id=device_of(peer),
-            device_id_type=MESH,
-        )
-        copy.start()
-        return copy
-
-    return put
 
 
 NEAR_FLIPS = [(0, 0, 0, 1), (0, 0, 1, 0), (0, 1, 0, 0), (1, 0, 0, 0), (2, 0, 0, 0), (3, 0, 0, 0)]
@@ -1191,12 +1193,12 @@
     )
 
 
-def setup_exchange(slab, small, noisy, meta, ident):
+def setup_exchange(slab, swap, small, noisy, meta, ident):
     planes = 4
     flips_f = [flip for flip in LAYER_FLIPS if flip[1] == 0]
 
     def kernel(
-        w_ref, s_ref, n_ref, m_ref, wo, so, no, mo, s_mid, n_mid, sent, got, csent, cgot, own
+        w_ref, c_ref, s_ref, n_ref, m_ref, wo, co, so, no, mo, s_mid, n_mid, sent, got, csent, cgot, own
     ):
         me = place()
         z_at, y_at, x_at, core = me
@@ -1211,11 +1213,12 @@
             pltpu.make_async_copy(s_ref, s_mid.at[z_at], own.at[1]),
             pltpu.make_async_copy(n_ref, n_mid.at[y_at, f_at], own.at[2]),
             pltpu.make_async_copy(m_ref, mo.at[f_at], own.at[3]),
+            pltpu.make_async_copy(c_ref.at[mine], co.at[mine], own.at[6]),
         ]
         for copy in locals_:
             copy.start()
+        slabs = [put(w_ref.at[rank_of(peer)], wo.at[z_at, mine], peer) for peer in layer]
         small_line = [put(s_ref, s_mid.at[z_at], peer) for peer in line]
-        slabs = [put(w_ref.at[rank_of(peer)], wo.at[z_at, mine], peer) for peer in layer]
         metas = [put(m_ref, mo.at[f_at], turned(me, flip)) for flip in flips_f]
         noisies = [put(n_ref, n_mid.at[y_at, f_at], peer) for peer in layer]
         for copy in locals_:
@@ -1262,6 +1265,7 @@
         noisy_line = [put(n_mid.at[:, peer[0]], no.at[z_at], peer) for peer in line]
         noisy_own = pltpu.make_async_copy(n_mid.at[:, z_at], no.at[z_at], own.at[5])
         noisy_own.start()
+        swaps = [put(c_ref.at[rank_of(peer)], co.at[mine], peer) for peer in layer]
         come(0)
         go(1)
         come(1)
@@ -1269,9 +1273,9 @@
         come(2)
         small_own.wait()
         noisy_own.wait()
-        for copy in metas + smalls + noisy_line:
+        for copy in metas + smalls + noisy_line + swaps:
             copy.wait_recv()
-        for copy in small_line + slabs + metas + noisies + smalls + noisy_line:
+        for copy in small_line + slabs + metas + noisies + smalls + noisy_line + swaps:
             copy.wait_send()
         for step in range(3):
 
@@ -1289,19 +1293,20 @@
         kernel,
         (
             shape((planes,) + slab.shape, slab.dtype),
+            shape(swap.shape, swap.dtype),
             shape((planes, RANKS) + small.shape, small.dtype),
             shape((planes, 2) + noisy.shape, noisy.dtype),
             shape((4,) + meta.shape, meta.dtype),
         ),
-        (slab, small, noisy, meta),
+        (slab, swap, small, noisy, meta),
         [
             pltpu.VMEM((planes,) + small.shape, small.dtype),
             pltpu.VMEM((2, 4) + noisy.shape, noisy.dtype),
-            dma((32,)),
-            dma((32,)),
+            dma((40,)),
+            dma((40,)),
             dma((2, 3)),
             dma((2, 3)),
-            dma((6,)),
+            dma((7,)),
         ],
         ident,
         vmem=True,
@@ -1478,11 +1483,202 @@
     )(lengths, queries, key_rows, values, mixed, log_total, grads, cosine, sine_table)
 
 
-def cross_forward(cross_query, cross_key, cross_value):
-    probs = jax.nn.softmax(scores_of(cross_query, cross_key), axis=-1)
-    probs_low = probs.astype(LOW)
-    out = jnp.einsum("bhqk,bkhd->bqhd", probs_low, cross_value, preferred_element_type=jnp.float32)
-    return probs, probs_low, out
+def first_state(noisy_ref, win_ref, timed_ref):
+    hidden = jnp.dot(noisy_ref[...], win_ref[...], preferred_element_type=jnp.float32) + timed_ref[0]
+    centred = hidden - jnp.mean(hidden, axis=1, keepdims=True)
+    spread = lax.rsqrt(jnp.mean(centred * centred, axis=1, keepdims=True) + 1e-05)
+    return centred * spread, spread
+
+
+def first_kernel(noisy_ref, win_ref, timed_ref, norm_ref, w_ref, qkv_ref):
+    unit, _ = first_state(noisy_ref, win_ref, timed_ref)
+    normed = (unit * norm_ref[0:1] + norm_ref[1:2]).astype(LOW)
+    qkv_ref[...] = jnp.dot(normed, w_ref[...], preferred_element_type=jnp.float32)
+
+
+def first_back_kernel(
+    items, noisy_ref, win_ref, timed_ref, norm_ref, w_ref, d_ref, dw_ref, in_ref, rows_ref
+):
+    step = pl.program_id(0)
+
+    @pl.when(step == 0)
+    def _():
+        dw_ref[...] = jnp.zeros_like(dw_ref)
+        in_ref[...] = jnp.zeros_like(in_ref)
+        rows_ref[...] = jnp.zeros_like(rows_ref)
+
+    unit, spread = first_state(noisy_ref, win_ref, timed_ref)
+    gain = norm_ref[0:1]
+    grads = d_ref[...]
+    dw_ref[...] += rows_product((unit * gain + norm_ref[1:2]).astype(LOW), grads)
+    grad_normed = times_transposed(grads, w_ref[...])
+    scaled = grad_normed * gain
+    grad_hidden = spread * (
+        scaled
+        - jnp.mean(scaled, axis=1, keepdims=True)
+        - unit * jnp.mean(scaled * unit, axis=1, keepdims=True)
+    )
+    high = grad_hidden.astype(LOW)
+    low = (grad_hidden - high.astype(jnp.float32)).astype(LOW)
+    in_ref[...] += rows_product(noisy_ref[...], high) + rows_product(noisy_ref[...], low)
+    item = step // (pl.num_programs(0) // items)
+    at = lax.broadcasted_iota(jnp.int32, rows_ref.shape, 0)
+    rows_ref[...] += (
+        jnp.where(at == 0, jnp.sum(grad_normed * unit, axis=0, keepdims=True), 0.0)
+        + jnp.where(at == 1, jnp.sum(grad_normed, axis=0, keepdims=True), 0.0)
+        + jnp.where(at == 2 + item, jnp.sum(grad_hidden, axis=0, keepdims=True), 0.0)
+    )
+
+
+def first_specs(noisy, timed, weight):
+    tokens, latent_dim = noisy.shape
+    items = timed.shape[0]
+    block = 256
+    each = tokens // items // block
+    rows = lambda lanes: pl.BlockSpec((block, lanes), lambda i: (i, 0))
+    whole = lambda shape: pl.BlockSpec(shape, lambda i: (0, 0))
+    specs = [
+        rows(latent_dim),
+        whole((latent_dim, D)),
+        pl.BlockSpec((1, 1, D), lambda i: (i // each, 0, 0)),
+        whole((2, D)),
+        whole(weight.shape),
+    ]
+    return tokens // block, rows, whole, specs
+
+
+def first_forward(noisy, win, timed, norm, weight):
+    steps, rows, _, specs = first_specs(noisy, timed, weight)
+    width = weight.shape[1]
+    return pl.pallas_call(
+        first_kernel,
+        grid=(steps,),
+        out_shape=jax.ShapeDtypeStruct((noisy.shape[0], width), jnp.float32),
+        in_specs=specs,
+        out_specs=rows(width),
+        compiler_params=pltpu.CompilerParams(vmem_limit_bytes=40 << 20),
+        cost_estimate=pl.CostEstimate(
+            flops=2 * noisy.shape[0] * D * width, bytes_accessed=8 << 20, transcendentals=0
+        ),
+    )(noisy, win, timed, norm, weight)
+
+
+def first_backward(noisy, win, timed, norm, weight, grads):
+    steps, rows, whole, specs = first_specs(noisy, timed, weight)
+    width = weight.shape[1]
+    f32 = jnp.float32
+    return pl.pallas_call(
+        functools.partial(first_back_kernel, timed.shape[0]),
+        grid=(steps,),
+        out_shape=(
+            jax.ShapeDtypeStruct((D, width), f32),
+            jax.ShapeDtypeStruct((noisy.shape[1], D), f32),
+            jax.ShapeDtypeStruct((8, D), f32),
+        ),
+        in_specs=specs + [rows(width)],
+        out_specs=(whole((D, width)), whole((noisy.shape[1], D)), whole((8, D))),
+        compiler_params=pltpu.CompilerParams(vmem_limit_bytes=40 << 20),
+        cost_estimate=pl.CostEstimate(
+            flops=8 * noisy.shape[0] * D * width, bytes_accessed=8 << 20, transcendentals=0
+        ),
+    )(noisy, win, timed, norm, weight, grads)
+
+
+def cross_probs(query, key):
+    scores = lax.dot_general(
+        query, key, (((1,), (1,)), ((), ())), preferred_element_type=jnp.float32
+    ) * (1.0 / math.sqrt(HEAD_DIM))
+    grown = jnp.exp(scores - jnp.max(scores, axis=1, keepdims=True))
+    return grown / jnp.sum(grown, axis=1, keepdims=True)
+
+
+def cross_kernel(q_ref, pair_ref, two_ref, self_ref, o_ref, *by_owner):
+    for head in range(HEADS):
+        rank, local = head // LOCAL_HEADS, head % LOCAL_HEADS
+        at = slice(head * HEAD_DIM, (head + 1) * HEAD_DIM)
+        own = slice(local * HEAD_DIM, (local + 1) * HEAD_DIM)
+        probs = cross_probs(q_ref[0, :, at], pair_ref[rank, 0, 0, :, own]).astype(LOW)
+        o_ref[0, :, at] = jnp.dot(
+            probs, pair_ref[rank, 1, 0, :, own], preferred_element_type=jnp.float32
+        ).astype(LOW)
+    planes = 4
+    share = D // (planes * RANKS)
+    for x_ref, out_ref in zip((self_ref, two_ref, o_ref), by_owner):
+        for rank in range(RANKS):
+            out_ref[rank, 0] = jnp.concatenate(
+                [
+                    x_ref[0, :, (plane * RANKS + rank) * share : (plane * RANKS + rank + 1) * share]
+                    for plane in range(planes)
+                ],
+                axis=1,
+            )
+
+
+def cross_back_kernel(q_ref, pair_ref, do_ref, dq_ref, dpair_ref):
+    scale = 1.0 / math.sqrt(HEAD_DIM)
+    for head in range(HEADS):
+        rank, local = head // LOCAL_HEADS, head % LOCAL_HEADS
+        at = slice(head * HEAD_DIM, (head + 1) * HEAD_DIM)
+        own = slice(local * HEAD_DIM, (local + 1) * HEAD_DIM)
+        query, grads = q_ref[0, :, at], do_ref[0, :, at]
+        key = pair_ref[rank, 0, 0, :, own]
+        probs = cross_probs(query, key)
+        pulled = lax.dot_general(
+            grads,
+            pair_ref[rank, 1, 0, :, own],
+            (((1,), (1,)), ((), ())),
+            preferred_element_type=jnp.float32,
+        )
+        delta = jnp.sum(probs * pulled, axis=1, keepdims=True)
+        pushed = (probs * (pulled - delta)).astype(LOW)
+        dq_ref[0, :, at] = (
+            jnp.dot(pushed, key, preferred_element_type=jnp.float32) * scale
+        ).astype(LOW)
+        dpair_ref[rank, 0, 0, :, own] = rows_product(pushed, query) * scale
+        dpair_ref[rank, 1, 0, :, own] = rows_product(probs.astype(LOW), grads)
+
+
+def cross_specs(count, span, context_len):
+    rows = pl.BlockSpec((1, span, D), lambda i: (i, 0, 0))
+    pair = pl.BlockSpec((RANKS, 2, 1, context_len, COLS), lambda i: (0, 0, i, 0, 0))
+    cost = pl.CostEstimate(
+        flops=10 * count * span * context_len * D,
+        bytes_accessed=8 * count * span * D,
+        transcendentals=count * HEADS * span * context_len,
+    )
+    return rows, pair, cost
+
+
+def cross_forward(queries, pair, two, own):
+    count, span, _ = queries.shape
+    rows, pair_spec, cost = cross_specs(count, span, pair.shape[3])
+    owned = jax.ShapeDtypeStruct((RANKS, count, span, COLS), LOW)
+    return pl.pallas_call(
+        cross_kernel,
+        grid=(count,),
+        out_shape=(jax.ShapeDtypeStruct(queries.shape, LOW),) + (owned,) * 3,
+        in_specs=[rows, pair_spec, rows, rows],
+        out_specs=(rows,) + (pl.BlockSpec((RANKS, 1, span, COLS), lambda i: (0, i, 0, 0)),) * 3,
+        compiler_params=pltpu.CompilerParams(vmem_limit_bytes=40 << 20),
+        cost_estimate=cost,
+    )(queries, pair, two, own)
+
+
+def cross_backward(queries, pair, grads):
+    count, span, _ = queries.shape
+    rows, pair_spec, cost = cross_specs(count, span, pair.shape[3])
+    return pl.pallas_call(
+        cross_back_kernel,
+        grid=(count,),
+        out_shape=(
+            jax.ShapeDtypeStruct(queries.shape, LOW),
+            jax.ShapeDtypeStruct(pair.shape, jnp.float32),
+        ),
+        in_specs=[rows, pair_spec, rows],
+        out_specs=(rows, pair_spec),
+        compiler_params=pltpu.CompilerParams(vmem_limit_bytes=40 << 20),
+        cost_estimate=cost,
+    )(queries, pair, grads)
 
 
 def fast_body(
@@ -1539,15 +1735,10 @@
     noisy_own = (signal * latents + noise_level * gaussian_noise).astype(LOW)
     target_own = signal * gaussian_noise - noise_level * latents
     local_meta = jnp.stack([timesteps, lengths.astype(f32), buckets.astype(f32)])
-    slab = jnp.concatenate(
-        [
-            attention_low[:3].reshape(-1, RANKS, COLS),
-            cross_low_t.reshape(-1, RANKS, COLS),
-        ],
-        axis=0,
-    )
-    slab_all, small_all, noisy_all, meta_all = setup_exchange(
-        jnp.swapaxes(slab, 0, 1),
+    slab_of = lambda array: jnp.swapaxes(array.reshape(-1, RANKS, COLS), 0, 1)
+    slab_all, cross_slab, small_all, noisy_all, meta_all = setup_exchange(
+        slab_of(attention_low[:3]),
+        slab_of(cross_low_t),
         small_low,
         noisy_own.reshape(-1, latent_dim),
         jnp.pad(local_meta, ((0, 5), (0, 128 - item_count))),
@@ -1559,12 +1750,8 @@
     latent_out = small_all[:, LAT : 2 * LAT].T
     timing = small_all[:, 2 * LAT : 2 * LAT + FOUR].T
     norms = small_all[:, 2 * LAT + FOUR :].astype(f32).T
-    qkv_rows = 3 * attention_low.shape[1]
-    qkv_slab = slab_all[:, :, :qkv_rows].reshape(planes * RANKS, 3, -1, COLS)
+    qkv_slab = slab_all.reshape(planes * RANKS, 3, -1, COLS)
     qkv_t = jnp.concatenate([qkv_slab[:, i].reshape(D, COLS) for i in range(3)], axis=1)
-    cross_w = jnp.moveaxis(
-        slab_all[:, :, qkv_rows:].reshape(planes * RANKS, 2, -1, COLS), 1, 0
-    ).reshape(2, E, COLS)
     meta = jnp.swapaxes(meta_all[:, :3, :item_count], 0, 1).reshape(3, -1)
     times_all = meta[0]
     lengths_all = meta[1]
@@ -1606,56 +1793,65 @@
     sine_table = jnp.concatenate([-jnp.sin(angles), jnp.sin(angles)], axis=1)
 
     timed = matmul_low(features, timing)
-    start_all = (
-        matmul_low(noisy_low.reshape(group_tokens, latent_dim), latent_in).reshape(
-            item_count, frames, D
-        )
+    noisy_mine = lax.dynamic_slice_in_dim(noisy_low, rank * span, span, 1)
+    start_own = (
+        matmul_low(noisy_mine.reshape(tokens, latent_dim), latent_in).reshape(item_count, span, D)
         + timed[:, None, :]
-    )
-    start_own = lax.dynamic_slice_in_dim(start_all, rank * span, span, 1).reshape(tokens, D)
-    noisy_mine = lax.dynamic_slice_in_dim(noisy_low, rank * span, span, 1).reshape(
-        tokens, latent_dim
-    )
-    normed_one, back_one = jax.vjp(
-        layer_norm, start_all.reshape(group_tokens, D), norms[0], norms[1]
-    )
-    normed_one = normed_one.astype(LOW)
-
+    ).reshape(tokens, D)
+    noisy_mine = noisy_mine.reshape(tokens, latent_dim)
+    first = (
+        noisy_low.reshape(group_tokens, latent_dim),
+        latent_in,
+        timed[:, None, :],
+        norms[:2],
+        qkv_t,
+    )
     queries, key_rows, values, mixed, mixed_heads, log_total = attend(
-        matmul_low(normed_one, qkv_t).reshape(item_count, frames, 3 * COLS),
+        first_forward(*first).reshape(item_count, frames, 3 * COLS),
         cosine,
         sine_table,
         own_lengths,
         span,
     )
     mixed_heads = mixed_heads.reshape(RANKS, tokens, COLS)
-    mixed_low = jnp.swapaxes(layer_swap([mixed_heads], 1)[0], 0, 1).reshape(tokens, D)
+    cross_slab = cross_slab.reshape(-1, COLS)
+    mixed_low, cross_slabs = plane_step(1, 25, swaps=[mixed_heads], carry=[cross_slab])
+    mixed_low = jnp.swapaxes(mixed_low, 0, 1).reshape(tokens, D)
+    cross_slabs = jnp.concatenate([cross_slab[None], cross_slabs], axis=0)
+    cross_slabs = jnp.take(cross_slabs, jnp.arange(planes) ^ z_at, axis=0, mode="clip")
+    cross_slabs = cross_slabs.reshape(planes * RANKS, 2, -1, COLS)
+    cross_w = [cross_slabs[:, i].reshape(E, COLS) for i in range(2)]
     after_self = start_own + matmul_low(mixed_low, rest_t[0])
     normed_two, back_two = jax.vjp(layer_norm, after_self, norms[2], norms[3])
     normed_two = normed_two.astype(LOW)
-    cross_query = (
-        matmul_low(normed_two, rest_t[1]).astype(LOW).reshape(item_count, span, HEADS, HEAD_DIM)
-    )
+    cross_query = matmul_low(normed_two, rest_t[1]).astype(LOW).reshape(item_count, span, D)
     pair_own = jnp.stack(
         [matmul_low(context_own, cross_w[0]), matmul_low(context_own, cross_w[1])]
     ).astype(LOW)
-    pair_all = jnp.moveaxis(
-        layer_gather(pair_own.reshape(-1, COLS), 3).reshape(RANKS, -1, COLS), 0, 1
-    ).reshape(2, item_count, context_len, HEADS, HEAD_DIM)
-    cross_key, cross_value = (pair_all[0], pair_all[1])
-    probs, probs_low, cross_mixed = cross_forward(cross_query, cross_key, cross_value)
-    cross_out = cross_mixed.reshape(tokens, D).astype(LOW)
+    (pair_all,) = plane_step(3, 12, gathers=[pair_own.reshape(-1, COLS)])
+    pair_all = pair_all.reshape(RANKS, 2, item_count, context_len, COLS)
+    cross_out, *owned = cross_forward(
+        cross_query,
+        pair_all,
+        normed_two.reshape(item_count, span, D),
+        mixed_low.reshape(item_count, span, D),
+    )
+    cross_out = cross_out.reshape(tokens, D)
+    owned = [array.reshape(RANKS, tokens, COLS) for array in owned]
     after_cross = after_self + matmul_low(cross_out, rest_t[2])
     normed_three, back_three = jax.vjp(layer_norm, after_cross, norms[4], norms[5])
     normed_three = normed_three.astype(LOW)
-    normed_group = layer_gather(normed_three, 4).reshape(group_tokens, D)
+    normed_group, self_heads, two_heads, out_heads = plane_step(
+        4, 70, gathers=[normed_three], swaps=owned
+    )
+    normed_group = normed_group.reshape(group_tokens, D)
     gate_both = times_transposed(normed_group, gate_up)
     units = gate_both.shape[1] // 2
     gate_half, up_half = (gate_both[:, :units], gate_both[:, units:])
     inner_act = (jax.nn.silu(gate_half) * up_half).astype(LOW)
     final_state = (
         after_cross
-        + layer_sum(matmul_low(inner_act, down).reshape(RANKS, tokens, D), 5)
+        + plane_step(5, 65, sums=[matmul_low(inner_act, down).reshape(RANKS, tokens, D)])[0]
     ).astype(LOW)
     predicted = times_transposed(final_state, latent_out)
 
@@ -1670,7 +1866,8 @@
 
     grad_out_proj = rows_product(grad_pred, final_state)
     grad_state = matmul_low(grad_pred, latent_out)
-    grad_group = layer_gather(grad_state.astype(LOW), 6).reshape(group_tokens, D)
+    (grad_group,) = plane_step(6, 30, gathers=[grad_state.astype(LOW)])
+    grad_group = grad_group.reshape(group_tokens, D)
     down_part = rows_product(inner_act, grad_group)
     grad_inner = times_transposed(grad_group, down)
     sigmoid_gate = jax.nn.sigmoid(gate_half)
@@ -1679,59 +1876,38 @@
         LOW
     )
     gate_up_part = rows_product(grad_both, normed_group)
-    down_slab = lax.psum_scatter(down_part, "z", scatter_dimension=0, tiled=True)
-    down_grad = lax.ppermute(down_slab, ALL, [(b, a) for a, b in down_pairs])
     gate_up_part = gate_up_part.reshape(planes, -1, D)
-    early = gate_up_part.shape[1] * 5 // 8
+    early = gate_up_part.shape[1] // 3
     early_tops, early_words = line_pack(gate_up_part[:, :early])
     late_tops, late_words = line_pack(gate_up_part[:, early:])
-    grad_three, early_tops, early_words = layer_sum(
-        matmul_low(grad_both, gate_up).reshape(RANKS, tokens, D),
+    grad_three, early_tops, early_words = plane_step(
         8,
-        (early_tops, early_words),
+        65,
+        sums=[matmul_low(grad_both, gate_up).reshape(RANKS, tokens, D)],
+        carry=[early_tops, early_words],
     )
     residual_part, gain_three, shift_three = back_three(grad_three)
     grad_state = grad_state + residual_part
     grad_branch = grad_state.astype(LOW)
-    grad_cross_out = lax.psum_scatter(
-        rows_product(cross_out, grad_branch), ALL, scatter_dimension=0, tiled=True
-    )
-    grad_mix = (
-        times_transposed(grad_branch, rest_t[2])
-        .astype(LOW)
-        .reshape(item_count, span, HEADS, HEAD_DIM)
-    )
-    grad_scores = jnp.einsum("bqhd,bkhd->bhqk", grad_mix, cross_value, preferred_element_type=f32)
-    grad_cross_value = jnp.einsum(
-        "bhqk,bqhd->bkhd", probs_low, grad_mix, preferred_element_type=f32
-    )
-    pushed = (probs * (grad_scores - jnp.sum(probs * grad_scores, axis=-1, keepdims=True))).astype(
-        LOW
-    )
-    score_scale = math.sqrt(HEAD_DIM)
-    grad_cross_query = (
-        (jnp.einsum("bhqk,bkhd->bqhd", pushed, cross_key, preferred_element_type=f32) / score_scale)
-        .astype(LOW)
-        .reshape(tokens, D)
-    )
-    grad_cross_key = (
-        jnp.einsum("bhqk,bqhd->bkhd", pushed, cross_query, preferred_element_type=f32) / score_scale
-    )
-    grad_pair = jnp.stack([grad_cross_key, grad_cross_value]).reshape(-1, RANKS, COLS)
-    grad_pair = layer_sum(jnp.swapaxes(grad_pair, 0, 1), 9).reshape(
-        2, item_count * context_len, COLS
-    )
-    grad_cross_w = jnp.einsum(
-        "te,ptc->pec", context_own.astype(f32), grad_pair, precision=HIGHEST
-    )
-    grad_cross_q = lax.psum_scatter(
-        rows_product(normed_two, grad_cross_query), ALL, scatter_dimension=0, tiled=True
-    )
-    residual_part, gain_two, shift_two = back_two(times_transposed(grad_cross_query, rest_t[1]))
-    grad_state = grad_state + residual_part
-    grad_branch = grad_state.astype(LOW)
-    branch_group, late_tops, late_words = layer_gather(grad_branch, 2, (late_tops, late_words))
-    branch_group = branch_group.reshape(group_tokens, D)
+    cross_branch = grad_branch
+    grad_mix = times_transposed(grad_branch, rest_t[2]).astype(LOW).reshape(item_count, span, D)
+    grad_cross_query, grad_pair = cross_backward(cross_query, pair_all, grad_mix)
+    grad_cross_query = grad_cross_query.reshape(tokens, D)
+    (
+        grad_pair,
+        cross_branch,
+        query_branch,
+        late_tops,
+        late_words,
+    ) = plane_step(
+        9,
+        90,
+        sums=[grad_pair.reshape(RANKS, -1, COLS)],
+        gathers=[cross_branch, grad_cross_query],
+        carry=[late_tops, late_words],
+    )
+    down_part, grad_pair = lax.optimization_barrier((down_part, grad_pair))
+    down_sum = lax.psum_scatter(down_part, "z", scatter_dimension=0, tiled=True)
     gate_up_grad = jnp.concatenate(
         [
             line_total(gate_up_part[:, :early], early_tops, early_words),
@@ -1739,19 +1915,48 @@
         ],
         axis=0,
     )
+    grad_pair = grad_pair.reshape(2, item_count * context_len, COLS)
+    cross_part = rows_precise(
+        context_own.astype(f32), jnp.concatenate([grad_pair[0], grad_pair[1]], axis=1)
+    ).reshape(planes, -1, 2 * COLS)
+    by_plane = lambda parts: parts.reshape(planes, -1, D)
+    cross_out_part = by_plane(
+        rows_product(out_heads.reshape(group_tokens, COLS), cross_branch.reshape(group_tokens, D))
+    )
+    cross_q_part = by_plane(
+        rows_product(two_heads.reshape(group_tokens, COLS), query_branch.reshape(group_tokens, D))
+    )
+    residual_part, gain_two, shift_two = back_two(times_transposed(grad_cross_query, rest_t[1]))
+    grad_state = grad_state + residual_part
+    grad_branch = grad_state.astype(LOW)
+    (
+        branch_group,
+        cq_tops,
+        cq_words,
+        co_tops,
+        co_words,
+        cross_tops,
+        cross_words,
+    ) = plane_step(
+        2,
+        35,
+        gathers=[grad_branch],
+        carry=line_pack(cross_q_part) + line_pack(cross_out_part) + line_pack(cross_part),
+    )
+    branch_group = branch_group.reshape(group_tokens, D)
+    cross_sums = jnp.stack(
+        [
+            line_total(cross_q_part, cq_tops, cq_words),
+            line_total(cross_out_part, co_tops, co_words),
+        ]
+    )
     out_rows = lax.dynamic_slice_in_dim(rest_t[0], rank * COLS, COLS, 0)
-    grad_self_out = lax.psum_scatter(
-        rows_product(mixed_heads.reshape(group_tokens, COLS), branch_group),
+    self_out_sum = lax.psum_scatter(
+        rows_product(self_heads.reshape(group_tokens, COLS), branch_group),
         "z",
         scatter_dimension=0,
         tiled=True,
     )
-    grad_self_out = lax.ppermute(
-        grad_self_out,
-        ALL,
-        [(RANKS * z + r, planes * r + z) for z in range(planes) for r in range(RANKS)],
-    )
-    rest_grad = jnp.stack([grad_self_out, grad_cross_q, grad_cross_out])
     grad_mixed = times_transposed(branch_group, out_rows).astype(LOW)
     grad_triple = attend_back(
         queries,
@@ -1764,16 +1969,11 @@
         sine_table,
         own_lengths,
     ).reshape(group_tokens, 3 * COLS)
-    qkv_part = rows_product(normed_one, grad_triple).reshape(planes, -1, 3 * COLS)
-    cross_part = jnp.moveaxis(grad_cross_w.reshape(2, planes, -1, COLS), 1, 0).reshape(
-        planes, -1, COLS
-    )
-    grad_one = times_transposed(grad_triple, qkv_t)
-    residual_part, gain_one, shift_one = back_one(grad_one)
-    grad_in_proj = rows_precise(
-        noisy_low.reshape(group_tokens, latent_dim).astype(f32), residual_part
-    ) + rows_precise(noisy_mine.astype(f32), grad_state)
-    grad_timed = jnp.sum(residual_part.reshape(item_count, frames, D), axis=1) + jnp.sum(
+    qkv_part, grad_in_proj, first_rows = first_backward(*first, grad_triple)
+    qkv_part = qkv_part.reshape(planes, -1, 3 * COLS)
+    gain_one, shift_one = (first_rows[0], first_rows[1])
+    grad_in_proj = grad_in_proj + rows_precise(noisy_mine.astype(f32), grad_state)
+    grad_timed = first_rows[2 : 2 + item_count] + jnp.sum(
         grad_state.reshape(item_count, span, D), axis=1
     )
     timed_slots = lax.dynamic_update_slice(
@@ -1783,41 +1983,67 @@
         [
             grad_in_proj,
             grad_out_proj,
+            timed_slots,
             jnp.stack([gain_one, shift_one, gain_two, shift_two, gain_three, shift_three]),
-            timed_slots,
+            jnp.zeros((2, D), f32),
         ],
         axis=0,
     )
+    small_grad, down_sum, self_out_sum = lax.optimization_barrier(
+        (small_grad, down_sum, self_out_sum)
+    )
     by_target = small_grad.T.reshape(planes, 2, 2, 2, -1, small_grad.shape[0])
-    small_grad, qkv_tops, qkv_words, cross_tops, cross_words = full_scatter(
+    small_grad, qkv_tops, qkv_words = full_scatter(
         jnp.transpose(by_target, (3, 2, 1, 0, 4, 5)),
         17,
-        line_pack(qkv_part) + line_pack(cross_part),
+        line_pack(qkv_part),
     )
     small_grad = small_grad.T
+    rest_grad = jnp.concatenate([self_out_sum[None], cross_sums], axis=0)
     qkv_grad = line_total(qkv_part, qkv_tops, qkv_words)
     cross_grad = line_total(cross_part, cross_tops, cross_words)
-    cross_grad = jnp.swapaxes(cross_grad.reshape(2, RANKS, -1, COLS), 0, 1)
-    qkv_grad, cross_grad = layer_swap([qkv_grad.reshape(RANKS, -1, 3 * COLS), cross_grad], 14)
-    qkv_grad = jnp.transpose(qkv_grad.reshape(RANKS, -1, 3, COLS), (2, 1, 0, 3)).reshape(3, -1, D)
-    cross_grad = jnp.transpose(cross_grad, (1, 2, 0, 3)).reshape(2, -1, D)
     latent_grad = small_grad[: 2 * LAT].reshape(2, LAT, -1)
-    norm_grad = small_grad[2 * LAT : 2 * LAT + 6]
-    timing_grad = rows_precise(features_all.astype(f32), small_grad[2 * LAT + 6 :])
-    attention_grad = jnp.concatenate([qkv_grad, rest_grad], axis=0)
-
+    timed_end = 2 * LAT + timed_slots.shape[0]
+    norm_grad = small_grad[timed_end : timed_end + 6]
+    timing_grad = rows_precise(features_all.astype(f32), small_grad[2 * LAT : timed_end])
     everything = (
-        attention_grad,
+        qkv_grad,
+        self_out_sum,
+        cross_sums,
         cross_grad,
         latent_grad,
         timing_grad,
         norm_grad,
         gate_up_grad,
-        down_grad,
+        down_sum,
     )
     squares = sum((jnp.sum(grad * grad) for grad in everything))
-    totals = all_fold(lanes_of([squares, partial_loss]), 15, jnp.add)
+    down_tops, down_words = line_pack(down_sum[None])
+    qkv_grad, cross_grad, totals, down_tops, down_words = plane_step(
+        14,
+        30,
+        swaps=[
+            qkv_grad.reshape(RANKS, -1, 3 * COLS),
+            cross_grad.reshape(RANKS, -1, 2 * COLS),
+        ],
+        everyone=[lanes_of([squares, partial_loss])],
+        moves=[down_tops, down_words[0]],
+    )
+    down_grad = jnp.concatenate(
+        [
+            lax.shift_right_arithmetic(down_words, 16),
+            lax.shift_right_arithmetic(lax.shift_left(down_words, 16), 16),
+        ],
+        axis=0,
+    ).astype(f32) * (down_tops[0] * (1.0 / LEVELS))[:, None]
+    totals = jnp.sum(totals, axis=0)
     squares, loss_value = (totals[0, 0], totals[0, 1])
+    qkv_grad = jnp.transpose(qkv_grad.reshape(RANKS, -1, 3, COLS), (2, 1, 0, 3)).reshape(3, -1, D)
+    cross_grad = jnp.transpose(cross_grad.reshape(RANKS, -1, 2, COLS), (2, 1, 0, 3)).reshape(
+        2, -1, D
+    )
+    attention_grad = jnp.concatenate([qkv_grad, rest_grad], axis=0)
+
     clip_norm = jnp.sqrt(squares)
     factor = CLIP_AT / jnp.maximum(clip_norm, CLIP_AT)
 

time: 1250 us -> 1080 us (0.86)
  waiting for transfers between devices: 69.3 us -> 18.9 us
  matrix products: 188 us -> 145 us
  local copies, waits for them, and re-layouts: 120 us -> 84.3 us
  Pallas kernels: 710 us -> 684 us
  starting transfers between devices: 23.3 us -> 8.33 us
    pallas_call x12, Pallas kernels: 621 us -> 552 us  [comm_call(): pl.pallas_call(kernel, out_shape=out_shape, in_specs=[spec] * len(arrays)...]
    pallas_call x1 -> x4, Pallas kernels: 33.8 us -> 76.3 us  [the longest x1 24.7 us: first_backward(): pl.pallas_call(functools.partial(first_back_kernel, timed.shape[0]), grid...]
    all_gather x1, waiting for transfers between devices: 34 us -> 0.02 us  [fast_body(): lax.all_gather(gate_up_weights.astype(LOW), 'z', axis=0, tiled=True)]
    reshape x12 -> x5, local copies, waits for them, and re-layouts: 25.6 us -> 1.6 us  [the longest x1 0.82 us: fast_body(): noisy_low = jnp.swapaxes(noisy_all.reshape(RANKS, item_count, span, laten...]
    ppermute x2 -> x0, starting transfers between devices: 14.7 us -> none  [the longest x1 10.9 us: fast_body(): down_grad = lax.ppermute(down_slab, ALL, [(b, a) for a, b in down_pairs])]
    reduce_sum x3 -> x2, other arithmetic: 14.6 us -> 1.06 us  [layer_norm(): centred = hidden - jnp.mean(hidden, axis=-1, keepdims=True)]
    dot_general x7 -> x6, matrix products: 56.9 us -> 43.8 us  [times_transposed(): lax.dot_general(left, weight, (((left.ndim - 1,), (1,)), ((), ())), prefe...]
    dot_general x7 -> x6, matrix products: 47.9 us -> 36 us  [rows_product(): lax.dot_general(left, right, (((0,), (0,)), ((), ())), preferred_element_...]
  transfers between devices with their start and end apart: 12 -> 8, of which waited for: 4 -> 3; matrix products, arithmetic and copies ran while one was open for 23% -> 13% of each run, Pallas kernels for 41% -> 30%
where the time goes in v3:
time: 1080 us; the launch traced here: 1070 us
  Pallas kernels  684 us (63%)
  matrix products  145 us (13%)
  other arithmetic  104 us (10%)
  local copies, waits for them, and re-layouts  84.3 us (8%)
  between operations  25.1 us (2%)
  waiting for transfers between devices  18.9 us (2%)
    pallas_call x12, Pallas kernels, comm_call(): pl.pallas_call(kernel, out_shape=out_shape, in_specs=[spec] * len(arrays)...  552 us
    dot_general x6, matrix products, times_transposed(): lax.dot_general(left, weight, (((left.ndim - 1,), (1,)), ((), ())), prefe...  43.8 us
    dot_general x10, matrix products, matmul_low(): return jnp.dot(left, right, preferred_element_type=jnp.float32)  40.8 us
    dot_general x6, matrix products, rows_product(): lax.dot_general(left, right, (((0,), (0,)), ((), ())), preferred_element_...  36 us
    pallas_call x1, Pallas kernels, attend_back(): pl.pallas_call(attend_back_kernel, grid=(count,), out_shape=jax.ShapeDtyp...  32.9 us
    unnamed x342, local copies, waits for them, and re-layouts  30.9 us
    pallas_call x1, Pallas kernels, first_backward(): pl.pallas_call(functools.partial(first_back_kernel, timed.shape[0]), grid...  24.7 us
    pallas_call x1, Pallas kernels, cross_backward(): pl.pallas_call(cross_back_kernel, grid=(count,), out_shape=(jax.ShapeDtyp...  23 us
  transfers between devices with their start and end apart: 8, of which 3 were waited for; matrix products, arithmetic and copies ran while one was open for 13% of the time, Pallas kernels for 30%

profile of v3, /device:TPU:0, one launch (start us, length us, event | category | flops | bytes accessed | tf_op | source)
XLA Modules:
  0.0 1068.9 jit_solution(3462254736459673961)
XLA Ops:
  13.1 70.0 %shard_map.448 = (bf16[4,8,144,192]{3,2,1,0:T(8,128)(2,1)S(1)}, bf16[8,48,192]{2,1,0:T(8,128)(2,1)S(1)}, bf16[4,8,48,390]{3,2,1,0:T(8,128)(2,1)S(1)}, bf16[4,2,2...) custom-call(bf16[8,144,192]{2,1,0:T(8,128)(2,1)S(1)} %bitcast.431, bf16[8,48,192]{2,1,0:T(8,128)(2,1)S(1)} %bitcast.441, ...), custom_call_target="tpu_custom_call" | custom-call | flops 60000002048 | bytes 1048576 | tf_op jit(solution)/shard_map/pallas_call | solution.py:675
  108.2 11.3 %shard_map.449 = f32[2048,576]{1,0:T(8,128)S(1)} custom-call(bf16[2048,64]{1,0:T(8,128)(2,1)S(1)} %bitcast.432, bf16[64,1536]{1,0:T(8,128)(2,1)S(1)} %bitcast.442, f32[2,1,1536]{2,1,0:T(1,128)S(1)} %broadcast_in_dim.50.timed_ref, f32[2,1536]{1,0:T(2,128)S(1)} %slice.433.norm_ref, bf16[1536,576]{1,0:T(8,128)(2,1)S(1)} %pad_maximum_fusion.6.w_ref), custom_call_target="tpu_custom_call" | custom-call | flops 3623878656 | bytes 8388608 | tf_op jit(solution)/shard_map/pallas_call | solution.py:1553
  121.8 22.6 %shard_map.450 = (bf16[2,3,1024,64]{3,2,1,0:T(8,128)(2,1)}, bf16[2,3,1024,64]{3,2,1,0:T(8,128)(2,1)}, bf16[2,3,1024,64]{3,2,1,0:T(8,128)(2,1)}, f32[2,3,1024,64]...) custom-call(s32[2]{0:T(128)} %dynamic-slice_convert_fusion.lengths_ref, ...), custom_call_target="tpu_custom_call" | custom-call | flops 1610612736 | bytes 3932160 | tf_op jit(solution)/shard_map/pallas_call | solution.py:1366
  144.4 26.9 %shard_map.451 = (bf16[8,256,192]{2,1,0:T(8,128)(2,1)}, bf16[3,384,192]{2,1,0:T(8,128)(2,1)}) custom-call(bf16[8,256,192]{2,1,0:T(8,128)(2,1)} %bitcast.510, bf16[384,192]{1,0:T(8,128)(2,1)} %bitcast.439), custom_call_target="tpu_custom_call" | custom-call | flops 24999999488 | bytes 1048576 | tf_op jit(solution)/shard_map/pallas_call | solution.py:675
  190.5 13.7 %shard_map.452 = bf16[8,512,192]{2,1,0:T(8,128)(2,1)} custom-call(bf16[512,192]{1,0:T(8,128)(2,1)} %bitcast.490), custom_call_target="tpu_custom_call" | custom-call | flops 12000000000 | bytes 1048576 | tf_op jit(solution)/shard_map/pallas_call | solution.py:675
  214.8 17.3 %shard_map.453 = (bf16[2,128,1536]{2,1,0:T(8,128)(2,1)S(1)}, bf16[8,2,128,192]{3,2,1,0:T(8,128)(2,1)S(1)}, bf16[8,2,128,192]{3,2,1,0:T(8,128)(2,1)S(1)}, bf16[8,2,128,192]{3,2,1,0:T(8,128)(2,1)S(1)}) custom-call(bf16[2,128,1536]{2,1,0:T(8,128)(2,1)S(1)} %bitcast.422, bf16[8,2,2,128,192]{4,3,2,1,0:T(8,128)(2,1)S(1)} %bitcast.412, ...), custom_call_target="tpu_custom_call" | custom-call | flops 503316480 | bytes 3145728 | tf_op jit(solution)/shard_map/pallas_call | solution.py:1656
  239.5 66.6 %shard_map.454 = (bf16[8,256,1536]{2,1,0:T(8,128)(2,1)}, bf16[8,256,192]{2,1,0:T(8,128)(2,1)}, bf16[8,256,192]{2,1,0:T(8,128)(2,1)}, bf16[8,256,192]{2,1,0:T(8,128)(2,1)}) custom-call(bf16[256,1536]{1,0:T(8,128)(2,1)} %add_convert_fusion.4.refs_0_, bf16[8,256,192]{2,1,0:T(8,128)(2,1)} %bitcast.446, bf16[8,256,192]{2,1,0:T(8,128)(2,1)} %bitcast.447, ...), custom_call_target="tpu_custom_call" | custom-call | flops 70000001024 | bytes 1048576 | tf_op jit(solution)/shard_map/pallas_call | solution.py:675
  306.1 16.1 %fusion.163 = f32[2048,1536]{0,1:T(8,128)} fusion(bf16[2048,1536]{1,0:T(8,128)(2,1)} %bitcast.502, bf16[1536,1536]{1,0:T(8,128)(2,1)} %all-gather.9.cloned.1.call-done), kind=kOutput, calls=%fused_computation.411 | convolution fusion | flops 9663676416 | bytes 23592960 | tf_op jit(solution)/shard_map/dot_general | solution.py:32
  328.1 17.7 %all-gather.11.cloned.1.call-done = bf16[768,1536]{1,0:T(8,128)(2,1)} async-done(((bf16[192,1536]{1,0:T(8,128)(2,1)}), bf16[768,1536]{1,0:T(8,128)(2,1)}) %all-gather.11.cloned.1.call-update) | async-done | bytes 2359312 | tf_op jit(solution)/shard_map/all_gather | solution.py:1785
  352.6 37.5 %shard_map.455 = f32[256,1536]{1,0:T(8,128)S(1)} custom-call(f32[8,256,1536]{2,1,0:T(8,128)S(1)} %bitcast.452), custom_call_target="tpu_custom_call" | custom-call | flops 65000001536 | bytes 1048576 | tf_op jit(solution)/shard_map/pallas_call | solution.py:675
  395.8 30.9 %shard_map.456 = bf16[8,256,1536]{2,1,0:T(8,128)(2,1)} custom-call(bf16[256,1536]{1,0:T(8,128)(2,1)} %get-tuple-element.453.refs_0_), custom_call_target="tpu_custom_call" | custom-call | flops 30000001024 | bytes 1048576 | tf_op jit(solution)/shard_map/pallas_call | solution.py:675
  426.7 12.3 %multiply_convert_fusion.1 = (bf16[2048,768]{0,1:T(8,128)(2,1)S(1)}, bf16[2048,768]{0,1:T(8,128)(2,1)S(1)}) fusion(f32[2048,1536]{0,1:T(8,128)} %fusion.163, bf16[2048,1536]{1,0:T(8,128)(2,1)} %bitcast.505, bf16[768,1536]{1,0:T(8,128)(2,1)} %all-gather.11.cloned.1.call-done), kind=kOutput, calls=%fused_computation.8 | convolution fusion | flops 4852285440 | bytes 27525120 | tf_op jit(solution)/shard_map/dot_general | solution.py:32
  441.6 12.5 %fusion.165 = f32[4,384,1536]{2,1,0:T(8,128)S(1)} fusion(bf16[4,384,2048]{2,1,0:T(8,128)(2,1)S(1)} %bitcast.456, bf16[2048,1536,1]{1,0,2:T(8,128)(2,1)} %bitcast.503), kind=kOutput, calls=%fused_computation.413 | convolution fusion | flops 9663676416 | bytes 22020096 | tf_op jit(solution)/shard_map/dot_general | solution.py:42
  475.5 15.4 %fusion.139 = f32[2048,1536]{1,0:T(8,128)} fusion(bf16[1536,1536]{1,0:T(8,128)(2,1)} %all-gather.9.cloned.1.call-done, bf16[2048,768]{0,1:T(8,128)(2,1)S(1)} %copy-done.70, bf16[2048,768]{0,1:T(8,128)(2,1)S(1)} %copy-done.68), kind=kOutput, calls=%fused_computation.392 | convolution fusion | flops 9676259328 | bytes 23592960 | tf_op jit(solution)/shard_map/dot_general | solution.py:38
  490.9 37.7 %shard_map.457 = (f32[256,1536]{1,0:T(8,128)S(1)}, f32[3,4,128]{2,1,0:T(4,128)S(1)}, s32[3,64,1536]{2,1,0:T(8,128)S(1)}) custom-call(f32[8,256,1536]{2,1,0:T(8,128)} %bitcast.501, f32[4,128]{1,0:T(4,128)S(1)} %get-tuple-element.354.refs_1_, s32[4,64,1536]{2,1,0:T(8,128)S(1)} %fusion.25.refs_2_), custom_call_target="tpu_custom_call" | custom-call | flops 65000001536 | bytes 1048576 | tf_op jit(solution)/shard_map/pallas_call | solution.py:675
  535.7 23.0 %shard_map.458 = (bf16[2,128,1536]{2,1,0:T(8,128)(2,1)S(1)}, f32[8,2,2,128,192]{4,3,2,1,0:T(8,128)S(1)}) custom-call(bf16[2,128,1536]{2,1,0:T(8,128)(2,1)S(1)} %bitcast.423, bf16[8,2,2,128,192]{4,3,2,1,0:T(8,128)(2,1)S(1)} %bitcast.413, bf16[2,128,1536]{2,1,0:T(8,128)(2,1)S(1)} %bitcast.430), custom_call_target="tpu_custom_call" | custom-call | flops 503316480 | bytes 3145728 | tf_op jit(solution)/shard_map/pallas_call | solution.py:1670
  575.8 76.9 %shard_map.459 = (f32[512,192]{1,0:T(8,128)S(1)}, bf16[8,256,1536]{2,1,0:T(8,128)(2,1)}, bf16[8,256,1536]{2,1,0:T(8,128)(2,1)}, f32[3,4,256]{2,1,0:T(4,128)S(1)}, s32[3,128,1536]{2,1,0:T(8,128)S(1)}) custom-call(f32[8,512,192]{2,1,0:T(8,128)S(1)} %bitcast.445, bf16[256,1536]{1,0:T(8,128)(2,1)S(1)} %copy-done.14, bf16[256,1536]{1,0:T(8,128)(2,1)S(1)} %bitcast.450, ...), custom_call_target="tpu_custom_call" | custom-call | flops 89999998976 | bytes 1048576 | tf_op jit(solution)/shard_map/pallas_call | solution.py:675
  670.0 41.1 %shard_map.460 = (bf16[8,256,1536]{2,1,0:T(8,128)(2,1)}, f32[3,4,48]{2,1,0:T(4,128)}, s32[3,24,1536]{2,1,0:T(8,128)}, f32[3,4,48]{2,1,0:T(4,128)}, s32[3,24,1536...) custom-call(bf16[256,1536]{1,0:T(8,128)(2,1)} %convert_element_type.271.refs_0_, f32[4,48]{1,0:T(4,128)} %copy-done.158, ...), custom_call_target="tpu_custom_call" | custom-call | flops 35000000512 | bytes 1048576 | tf_op jit(solution)/shard_map/pallas_call | solution.py:675
  731.3 32.9 %shard_map.461 = bf16[2,1024,576]{2,1,0:T(8,128)(2,1)} custom-call(s32[2]{0:T(128)} %dynamic-slice_convert_fusion.lengths_ref, bf16[2,3,1024,64]{3,2,1,0:T(8,128)(2,1)} %get-tuple-element.88.q_ref, bf16[2,3,1024,64]{3,2,1,0:T(8,128)(2,1)} %get-tuple-element.89.k_ref, bf16[2,3,1024,64]{3,2,1,0:T(8,128)(2,1)} %get-tuple-element.90.v_ref, ...), custom_call_target="tpu_custom_call" | custom-call | flops 4026531840 | bytes 9437184 | tf_op jit(solution)/shard_map/pallas_call | solution.py:1461
  765.9 24.7 %shard_map.462 = (f32[1536,576]{1,0:T(8,128)S(1)}, f32[64,1536]{1,0:T(8,128)S(1)}, f32[8,1536]{1,0:T(8,128)S(1)}) custom-call(bf16[2048,64]{1,0:T(8,128)(2,1)S(1)} %bitcast.433, bf16[64,1536]{1,0:T(8,128)(2,1)S(1)} %bitcast.443, f32[2,1,1536]{2,1,0:T(1,128)S(1)} %copy-done.25, f32[2,1536]{1,0:T(2,128)S(1)} %copy-done.27, bf16[1536,576]{1,0:T(8,128)(2,1)S(1)} %copy-done.12, ...), custom_call_target="tpu_custom_call" | custom-call | flops 14495514624 | bytes 8388608 | tf_op jit(solution)/shard_map/pallas_call | solution.py:1570
  836.1 51.6 %shard_map.463 = (f32[48,144]{1,0:T(8,128)S(1)}, f32[3,4,384]{2,1,0:T(4,128)S(1)}, s32[3,192,576]{2,1,0:T(8,128)S(1)}) custom-call(f32[2,2,2,4,48,144]{5,4,3,2,1,0:T(8,128)S(1)} %bitcast.429, f32[4,384]{1,0:T(4,128)S(1)} %reduce_max.73.refs_0_, s32[4,192,576]{2,1,0:T(8,128)S(1)} %fusion.18.refs_1_), custom_call_target="tpu_custom_call" | custom-call | flops 40000000000 | bytes 1048576 | tf_op jit(solution)/shard_map/pallas_call | solution.py:675
  911.5 28.2 %shard_map.464 = (f32[8,48,576]{2,1,0:T(8,128)}, f32[8,24,384]{2,1,0:T(8,128)}, f32[32,8,128]{2,1,0:T(8,128)}, f32[1,192]{1,0:T(1,128)}, s32[96,1536]{1,0:T(8,128)}) custom-call(f32[8,48,576]{2,1,0:T(8,128)} %multiply_add_fusion.2.refs_0_, f32[8,24,384]{2,1,0:T(8,128)} %multiply_add_fusion.3.refs_1_, f32[8,128]{1,0:T(8,128)} %broadcast_in_dim.100.refs_2_, ...), custom_call_target="tpu_custom_call" | custom-call | flops 30000001024 | bytes 1048576 | tf_op jit(solution)/shard_map/pallas_call | solution.py:675
  949.4 9.5 fusion.20
  966.6 71.2 %shard_map.465 = f32[2,2,2,4,192,128]{5,4,3,2,1,0:T(8,128)S(1)} custom-call(f32[2,2,2,4,192,128]{5,4,3,2,1,0:T(8,128)S(1)} %bitcast.421), custom_call_target="tpu_custom_call" | custom-call | flops 20000000000 | bytes 1048576 | tf_op jit(solution)/shard_map/pallas_call | solution.py:675
  (589 shorter events, 276.3 us)
Async XLA Ops:
  7.2 180.7 %all-gather.7.cloned.1.call-start = ((), (), s32[]{:S(2)}) async-start(), calls=%async_computation.3 | async-start | bytes 1966080 | tf_op jit(solution)/shard_map/all_gather | solution.py:1775
  7.9 197.3 %all-gather.5.cloned.1.call-start = ((), (), s32[]{:S(2)}) async-start(), calls=%async_computation.2 | async-start | bytes 14598144 | tf_op jit(solution)/shard_map/all_gather | solution.py:1779
  85.2 100.2 %copy-start.4 = (bf16[4,8,48,390]{3,2,1,0:T(8,128)(2,1)}, bf16[4,8,48,390]{3,2,1,0:T(8,128)(2,1)S(1)}, u32[]{:S(2)}) copy-start(bf16[4,8,48,390]{3,2,1,0:T(8,128)(2,1)S(1)} %get-tuple-element.84) | copy-start | bytes 3594244
  85.3 220.9 %all-gather.9.cloned.1.call-start = ((), (), s32[]{:S(2)}) async-start(), calls=%async_computation.4 | async-start | bytes 5898240 | tf_op jit(solution)/shard_map/all_gather | solution.py:1780
  88.0 99.8 %collective-permute-start = (bf16[192,1536]{1,0:T(8,128)(2,1)}, bf16[192,1536]{1,0:T(8,128)(2,1)}, u32[]{:S(2)}, u32[]{:S(2)}) collective-permute-start(bf16[192,1536]{1,0:T(8,128)(2,1)} %convert_element_type.263), channel_id=1, source_target_pairs={{0,0},{2,1},{4,2},{6,3},{8,4},{10,5},{12,6},{14,7},{1,8},{3,9},{5,... | collective-permute-start | bytes 1769480 | tf_op jit(solution)/shard_map/ppermute | solution.py:1786
  93.9 296.4 %collective-permute-start.1 = (f32[2,128,64]{1,2,0:T(8,128)}, f32[2,128,64]{1,2,0:T(8,128)}, u32[]{:S(2)}, u32[]{:S(2)}) collective-permute-start(f32[2,128,64]{1,2,0:T(8,128)} %get-tuple-element.414), channel_id=1, source_target_pairs={{0,0},{1,8},{2,16},{3,24},{4,1},{5,9},{6,17},{7,25},{8,2},{9,10},{... | collective-permute-start | bytes 196616 | tf_op jit(solution)/shard_map/ppermute | solution.py:1772
  98.9 246.9 %all-gather.11.cloned.1.call-start = ((), (), s32[]{:S(2)}) async-start(), calls=%async_computation.5 | async-start | bytes 2949120 | tf_op jit(solution)/shard_map/all_gather | solution.py:1785
  184.6 53.7 %copy-start.102 = (f32[1536]{0:T(1024)}, f32[1536]{0:T(1024)S(1)}, u32[]{:S(2)}) copy-start(f32[1536]{0:T(1024)S(1)} %get-tuple-element.309) | copy-start | bytes 18436
  187.8 644.1 %reduce-scatter.5.cloned.1.call-start = ((), (), s32[]{:S(2)}) async-start(), calls=%async_computation.7 | async-start | bytes 1474560 | tf_op jit(solution)/shard_map/reduce_scatter | solution.py:1954
  352.5 37.5 %copy-start.40 = (f32[256,1536]{1,0:T(8,128)S(1)}, f32[256,1536]{1,0:T(8,128)}, u32[]{:S(2)}) copy-start(f32[256,1536]{1,0:T(8,128)} %copy-done.39) | copy-start | bytes 4718596
  490.9 37.8 %copy-start.41 = (f32[256,1536]{1,0:T(8,128)S(1)}, f32[256,1536]{1,0:T(8,128)}, u32[]{:S(2)}) copy-start(f32[256,1536]{1,0:T(8,128)} %copy-done.39) | copy-start | bytes 4718596
  490.9 37.8 %copy-start.103 = (f32[1536]{0:T(1024)S(1)}, f32[1536]{0:T(1024)}, u32[]{:S(2)}) copy-start(f32[1536]{0:T(1024)} %copy-done.102) | copy-start | bytes 18436
  490.9 37.8 %copy-start.123 = (f32[256]{0:T(256)S(1)}, f32[256]{0:T(256)}, u32[]{:S(2)}) copy-start(f32[256]{0:T(256)} %copy-done.122) | copy-start | bytes 3076
  490.9 37.8 %copy-start.136 = (f32[256]{0:T(256)S(1)}, f32[256]{0:T(256)}, u32[]{:S(2)}) copy-start(f32[256]{0:T(256)} %copy-done.135) | copy-start | bytes 3076
  575.8 77.0 %copy-start.88 = (bf16[192,2048]{1,0:T(8,128)(2,1)S(1)}, bf16[192,2048]{1,0:T(8,128)(2,1)}, u32[]{:S(2)}) copy-start(bf16[192,2048]{1,0:T(8,128)(2,1)} %copy.297) | copy-start | bytes 2359300
  716.7 115.5 %reduce-scatter.3.cloned.1.call-start = ((), (), s32[]{:S(2)}) async-start(), calls=%async_computation.6 | async-start | bytes 5898240 | tf_op jit(solution)/shard_map/reduce_scatter | solution.py:1910
  731.2 32.9 %copy-start.12 = (bf16[1536,576]{1,0:T(8,128)(2,1)S(1)}, bf16[1536,576]{1,0:T(8,128)(2,1)}, u32[]{:S(2)}) copy-start(bf16[1536,576]{1,0:T(8,128)(2,1)} %copy-done.11) | copy-start | bytes 5308420
  731.2 32.9 %copy-start.16 = (bf16[8,2,128,64]{3,2,0,1:T(8,128)(2,1)S(1)}, bf16[8,2,128,64]{3,2,0,1:T(8,128)(2,1)}, u32[]{:S(2)}) copy-start(bf16[8,2,128,64]{3,2,0,1:T(8,128)(2,1)} %copy-done.15) | copy-start | bytes 786436
  731.2 32.9 %copy-start.23 = (bf16[1536,64]{0,1:T(8,128)(2,1)S(1)}, bf16[1536,64]{0,1:T(8,128)(2,1)}, u32[]{:S(2)}) copy-start(bf16[1536,64]{0,1:T(8,128)(2,1)} %copy-done.22) | copy-start | bytes 589828
  731.2 32.9 %copy-start.25 = (f32[2,1,1536]{2,1,0:T(1,128)S(1)}, f32[2,1,1536]{2,1,0:T(1,128)}, u32[]{:S(2)}) copy-start(f32[2,1,1536]{2,1,0:T(1,128)} %copy-done.24) | copy-start | bytes 36868
  731.3 32.9 %copy-start.27 = (f32[2,1536]{1,0:T(2,128)S(1)}, f32[2,1536]{1,0:T(2,128)}, u32[]{:S(2)}) copy-start(f32[2,1536]{1,0:T(2,128)} %copy-done.26) | copy-start | bytes 36868
  765.9 26.1 %copy-start.145 = (f32[1536]{0:T(1024)S(1)}, f32[1536]{0:T(1024)}, u32[]{:S(2)}) copy-start(f32[1536]{0:T(1024)} %get-tuple-element.306) | copy-start | bytes 18436
  765.9 27.2 %copy-start.121 = (f32[1536]{0:T(1024)S(1)}, f32[1536]{0:T(1024)}, u32[]{:S(2)}) copy-start(f32[1536]{0:T(1024)} %get-tuple-element.301) | copy-start | bytes 18436
  765.9 27.8 %copy-start.120 = (f32[1536]{0:T(1024)S(1)}, f32[1536]{0:T(1024)}, u32[]{:S(2)}) copy-start(f32[1536]{0:T(1024)} %get-tuple-element.305) | copy-start | bytes 18436
  (152 other events, 709.8 us)
Sparse Core Ops, SparseCore 0:
  9.6 30.7 all-gather.6
  85.4 119.8 all-gather.4
  207.4 87.9 all-gather.8
  296.8 48.9 all-gather.10
  716.8 29.1 reduce-scatter.4
  748.2 83.9 reduce-scatter.2

commit v4 on v3

--- a/solution.py
+++ b/solution.py
@@ -971,7 +971,7 @@
             else:
                 flows.append(swap_flow(me, put, ins[i], outs[i], own.at[i, 0]))
         for _ in range(8):
-            for flow in flows:
+            for flow in flows[n_sum:] + flows[:n_sum]:
                 next(flow, None)
         for copy in carried:
             copy.wait()

time: 1080 us -> 1070 us (level)
  transfers between devices with their start and end apart: 8 -> 8, of which waited for: 3 -> 2; matrix products, arithmetic and copies ran while one was open for 13% -> 13% of each run, Pallas kernels for 30% -> 30%
where the time goes in v4:
time: 1070 us; the launch traced here: 1060 us
  Pallas kernels  679 us (63%)
  matrix products  145 us (14%)
  other arithmetic  104 us (10%)
  local copies, waits for them, and re-layouts  84.3 us (8%)
  between operations  25.1 us (2%)
  waiting for transfers between devices  18.6 us (2%)
    pallas_call x12, Pallas kernels, comm_call(): pl.pallas_call(kernel, out_shape=out_shape, in_specs=[spec] * len(arrays)...  547 us
    dot_general x6, matrix products, times_transposed(): lax.dot_general(left, weight, (((left.ndim - 1,), (1,)), ((), ())), prefe...  43.8 us
    dot_general x10, matrix products, matmul_low(): return jnp.dot(left, right, preferred_element_type=jnp.float32)  40.8 us
    dot_general x6, matrix products, rows_product(): lax.dot_general(left, right, (((0,), (0,)), ((), ())), preferred_element_...  36 us
    pallas_call x1, Pallas kernels, attend_back(): pl.pallas_call(attend_back_kernel, grid=(count,), out_shape=jax.ShapeDtyp...  32.8 us
    unnamed x342, local copies, waits for them, and re-layouts  31.1 us
    pallas_call x1, Pallas kernels, first_backward(): pl.pallas_call(functools.partial(first_back_kernel, timed.shape[0]), grid...  24.7 us
    pallas_call x1, Pallas kernels, cross_backward(): pl.pallas_call(cross_back_kernel, grid=(count,), out_shape=(jax.ShapeDtyp...  23 us
  transfers between devices with their start and end apart: 8, of which 2 were waited for; matrix products, arithmetic and copies ran while one was open for 13% of the time, Pallas kernels for 30%

profile of v4, /device:TPU:0, one launch (start us, length us, event | category | flops | bytes accessed | tf_op | source)
XLA Modules:
  0.0 1063.6 jit_solution(2124992479221998760)
XLA Ops:
  13.1 70.0 %shard_map.448 = (bf16[4,8,144,192]{3,2,1,0:T(8,128)(2,1)S(1)}, bf16[8,48,192]{2,1,0:T(8,128)(2,1)S(1)}, bf16[4,8,48,390]{3,2,1,0:T(8,128)(2,1)S(1)}, bf16[4,2,2...) custom-call(bf16[8,144,192]{2,1,0:T(8,128)(2,1)S(1)} %bitcast.431, bf16[8,48,192]{2,1,0:T(8,128)(2,1)S(1)} %bitcast.441, ...), custom_call_target="tpu_custom_call" | custom-call | flops 60000002048 | bytes 1048576 | tf_op jit(solution)/shard_map/pallas_call | solution.py:675
  108.2 11.3 %shard_map.449 = f32[2048,576]{1,0:T(8,128)S(1)} custom-call(bf16[2048,64]{1,0:T(8,128)(2,1)S(1)} %bitcast.432, bf16[64,1536]{1,0:T(8,128)(2,1)S(1)} %bitcast.442, f32[2,1,1536]{2,1,0:T(1,128)S(1)} %broadcast_in_dim.50.timed_ref, f32[2,1536]{1,0:T(2,128)S(1)} %slice.433.norm_ref, bf16[1536,576]{1,0:T(8,128)(2,1)S(1)} %pad_maximum_fusion.6.w_ref), custom_call_target="tpu_custom_call" | custom-call | flops 3623878656 | bytes 8388608 | tf_op jit(solution)/shard_map/pallas_call | solution.py:1553
  121.8 22.6 %shard_map.450 = (bf16[2,3,1024,64]{3,2,1,0:T(8,128)(2,1)}, bf16[2,3,1024,64]{3,2,1,0:T(8,128)(2,1)}, bf16[2,3,1024,64]{3,2,1,0:T(8,128)(2,1)}, f32[2,3,1024,64]...) custom-call(s32[2]{0:T(128)} %dynamic-slice_convert_fusion.lengths_ref, ...), custom_call_target="tpu_custom_call" | custom-call | flops 1610612736 | bytes 3932160 | tf_op jit(solution)/shard_map/pallas_call | solution.py:1366
  144.4 26.9 %shard_map.451 = (bf16[8,256,192]{2,1,0:T(8,128)(2,1)}, bf16[3,384,192]{2,1,0:T(8,128)(2,1)}) custom-call(bf16[8,256,192]{2,1,0:T(8,128)(2,1)} %bitcast.510, bf16[384,192]{1,0:T(8,128)(2,1)} %bitcast.439), custom_call_target="tpu_custom_call" | custom-call | flops 24999999488 | bytes 1048576 | tf_op jit(solution)/shard_map/pallas_call | solution.py:675
  190.5 13.7 %shard_map.452 = bf16[8,512,192]{2,1,0:T(8,128)(2,1)} custom-call(bf16[512,192]{1,0:T(8,128)(2,1)} %bitcast.490), custom_call_target="tpu_custom_call" | custom-call | flops 12000000000 | bytes 1048576 | tf_op jit(solution)/shard_map/pallas_call | solution.py:675
  214.8 17.3 %shard_map.453 = (bf16[2,128,1536]{2,1,0:T(8,128)(2,1)S(1)}, bf16[8,2,128,192]{3,2,1,0:T(8,128)(2,1)S(1)}, bf16[8,2,128,192]{3,2,1,0:T(8,128)(2,1)S(1)}, bf16[8,2,128,192]{3,2,1,0:T(8,128)(2,1)S(1)}) custom-call(bf16[2,128,1536]{2,1,0:T(8,128)(2,1)S(1)} %bitcast.422, bf16[8,2,2,128,192]{4,3,2,1,0:T(8,128)(2,1)S(1)} %bitcast.412, ...), custom_call_target="tpu_custom_call" | custom-call | flops 503316480 | bytes 3145728 | tf_op jit(solution)/shard_map/pallas_call | solution.py:1656
  239.5 66.6 %shard_map.454 = (bf16[8,256,1536]{2,1,0:T(8,128)(2,1)}, bf16[8,256,192]{2,1,0:T(8,128)(2,1)}, bf16[8,256,192]{2,1,0:T(8,128)(2,1)}, bf16[8,256,192]{2,1,0:T(8,128)(2,1)}) custom-call(bf16[256,1536]{1,0:T(8,128)(2,1)} %add_convert_fusion.4.refs_0_, bf16[8,256,192]{2,1,0:T(8,128)(2,1)} %bitcast.446, bf16[8,256,192]{2,1,0:T(8,128)(2,1)} %bitcast.447, ...), custom_call_target="tpu_custom_call" | custom-call | flops 70000001024 | bytes 1048576 | tf_op jit(solution)/shard_map/pallas_call | solution.py:675
  306.1 16.1 %fusion.163 = f32[2048,1536]{0,1:T(8,128)} fusion(bf16[2048,1536]{1,0:T(8,128)(2,1)} %bitcast.502, bf16[1536,1536]{1,0:T(8,128)(2,1)} %all-gather.9.cloned.1.call-done), kind=kOutput, calls=%fused_computation.411 | convolution fusion | flops 9663676416 | bytes 23592960 | tf_op jit(solution)/shard_map/dot_general | solution.py:32
  328.1 17.7 %all-gather.11.cloned.1.call-done = bf16[768,1536]{1,0:T(8,128)(2,1)} async-done(((bf16[192,1536]{1,0:T(8,128)(2,1)}), bf16[768,1536]{1,0:T(8,128)(2,1)}) %all-gather.11.cloned.1.call-update) | async-done | bytes 2359312 | tf_op jit(solution)/shard_map/all_gather | solution.py:1785
  352.6 37.5 %shard_map.455 = f32[256,1536]{1,0:T(8,128)S(1)} custom-call(f32[8,256,1536]{2,1,0:T(8,128)S(1)} %bitcast.452), custom_call_target="tpu_custom_call" | custom-call | flops 65000001536 | bytes 1048576 | tf_op jit(solution)/shard_map/pallas_call | solution.py:675
  395.8 30.9 %shard_map.456 = bf16[8,256,1536]{2,1,0:T(8,128)(2,1)} custom-call(bf16[256,1536]{1,0:T(8,128)(2,1)} %get-tuple-element.453.refs_0_), custom_call_target="tpu_custom_call" | custom-call | flops 30000001024 | bytes 1048576 | tf_op jit(solution)/shard_map/pallas_call | solution.py:675
  426.7 12.3 %multiply_convert_fusion.1 = (bf16[2048,768]{0,1:T(8,128)(2,1)S(1)}, bf16[2048,768]{0,1:T(8,128)(2,1)S(1)}) fusion(f32[2048,1536]{0,1:T(8,128)} %fusion.163, bf16[2048,1536]{1,0:T(8,128)(2,1)} %bitcast.505, bf16[768,1536]{1,0:T(8,128)(2,1)} %all-gather.11.cloned.1.call-done), kind=kOutput, calls=%fused_computation.8 | convolution fusion | flops 4852285440 | bytes 27525120 | tf_op jit(solution)/shard_map/dot_general | solution.py:32
  441.6 12.5 %fusion.165 = f32[4,384,1536]{2,1,0:T(8,128)S(1)} fusion(bf16[4,384,2048]{2,1,0:T(8,128)(2,1)S(1)} %bitcast.456, bf16[2048,1536,1]{1,0,2:T(8,128)(2,1)} %bitcast.503), kind=kOutput, calls=%fused_computation.413 | convolution fusion | flops 9663676416 | bytes 22020096 | tf_op jit(solution)/shard_map/dot_general | solution.py:42
  475.5 15.4 %fusion.139 = f32[2048,1536]{1,0:T(8,128)} fusion(bf16[1536,1536]{1,0:T(8,128)(2,1)} %all-gather.9.cloned.1.call-done, bf16[2048,768]{0,1:T(8,128)(2,1)S(1)} %copy-done.70, bf16[2048,768]{0,1:T(8,128)(2,1)S(1)} %copy-done.68), kind=kOutput, calls=%fused_computation.392 | convolution fusion | flops 9676259328 | bytes 23592960 | tf_op jit(solution)/shard_map/dot_general | solution.py:38
  490.9 37.7 %shard_map.457 = (f32[256,1536]{1,0:T(8,128)S(1)}, f32[3,4,128]{2,1,0:T(4,128)S(1)}, s32[3,64,1536]{2,1,0:T(8,128)S(1)}) custom-call(f32[8,256,1536]{2,1,0:T(8,128)} %bitcast.501, f32[4,128]{1,0:T(4,128)S(1)} %get-tuple-element.354.refs_1_, s32[4,64,1536]{2,1,0:T(8,128)S(1)} %fusion.25.refs_2_), custom_call_target="tpu_custom_call" | custom-call | flops 65000001536 | bytes 1048576 | tf_op jit(solution)/shard_map/pallas_call | solution.py:675
  535.7 23.0 %shard_map.458 = (bf16[2,128,1536]{2,1,0:T(8,128)(2,1)S(1)}, f32[8,2,2,128,192]{4,3,2,1,0:T(8,128)S(1)}) custom-call(bf16[2,128,1536]{2,1,0:T(8,128)(2,1)S(1)} %bitcast.423, bf16[8,2,2,128,192]{4,3,2,1,0:T(8,128)(2,1)S(1)} %bitcast.413, bf16[2,128,1536]{2,1,0:T(8,128)(2,1)S(1)} %bitcast.430), custom_call_target="tpu_custom_call" | custom-call | flops 503316480 | bytes 3145728 | tf_op jit(solution)/shard_map/pallas_call | solution.py:1670
  575.8 72.7 %shard_map.459 = (f32[512,192]{1,0:T(8,128)S(1)}, bf16[8,256,1536]{2,1,0:T(8,128)(2,1)}, bf16[8,256,1536]{2,1,0:T(8,128)(2,1)}, f32[3,4,256]{2,1,0:T(4,128)S(1)}, s32[3,128,1536]{2,1,0:T(8,128)S(1)}) custom-call(f32[8,512,192]{2,1,0:T(8,128)S(1)} %bitcast.445, bf16[256,1536]{1,0:T(8,128)(2,1)S(1)} %copy-done.14, bf16[256,1536]{1,0:T(8,128)(2,1)S(1)} %bitcast.450, ...), custom_call_target="tpu_custom_call" | custom-call | flops 89999998976 | bytes 1048576 | tf_op jit(solution)/shard_map/pallas_call | solution.py:675
  665.8 40.7 %shard_map.460 = (bf16[8,256,1536]{2,1,0:T(8,128)(2,1)}, f32[3,4,48]{2,1,0:T(4,128)}, s32[3,24,1536]{2,1,0:T(8,128)}, f32[3,4,48]{2,1,0:T(4,128)}, s32[3,24,1536...) custom-call(bf16[256,1536]{1,0:T(8,128)(2,1)} %convert_element_type.271.refs_0_, f32[4,48]{1,0:T(4,128)} %copy-done.158, ...), custom_call_target="tpu_custom_call" | custom-call | flops 35000000512 | bytes 1048576 | tf_op jit(solution)/shard_map/pallas_call | solution.py:675
  726.5 32.8 %shard_map.461 = bf16[2,1024,576]{2,1,0:T(8,128)(2,1)} custom-call(s32[2]{0:T(128)} %dynamic-slice_convert_fusion.lengths_ref, bf16[2,3,1024,64]{3,2,1,0:T(8,128)(2,1)} %get-tuple-element.88.q_ref, bf16[2,3,1024,64]{3,2,1,0:T(8,128)(2,1)} %get-tuple-element.89.k_ref, bf16[2,3,1024,64]{3,2,1,0:T(8,128)(2,1)} %get-tuple-element.90.v_ref, ...), custom_call_target="tpu_custom_call" | custom-call | flops 4026531840 | bytes 9437184 | tf_op jit(solution)/shard_map/pallas_call | solution.py:1461
  761.2 24.7 %shard_map.462 = (f32[1536,576]{1,0:T(8,128)S(1)}, f32[64,1536]{1,0:T(8,128)S(1)}, f32[8,1536]{1,0:T(8,128)S(1)}) custom-call(bf16[2048,64]{1,0:T(8,128)(2,1)S(1)} %bitcast.433, bf16[64,1536]{1,0:T(8,128)(2,1)S(1)} %bitcast.443, f32[2,1,1536]{2,1,0:T(1,128)S(1)} %copy-done.25, f32[2,1536]{1,0:T(2,128)S(1)} %copy-done.27, bf16[1536,576]{1,0:T(8,128)(2,1)S(1)} %copy-done.12, ...), custom_call_target="tpu_custom_call" | custom-call | flops 14495514624 | bytes 8388608 | tf_op jit(solution)/shard_map/pallas_call | solution.py:1570
  831.2 50.8 %shard_map.463 = (f32[48,144]{1,0:T(8,128)S(1)}, f32[3,4,384]{2,1,0:T(4,128)S(1)}, s32[3,192,576]{2,1,0:T(8,128)S(1)}) custom-call(f32[2,2,2,4,48,144]{5,4,3,2,1,0:T(8,128)S(1)} %bitcast.429, f32[4,384]{1,0:T(4,128)S(1)} %reduce_max.73.refs_0_, s32[4,192,576]{2,1,0:T(8,128)S(1)} %fusion.18.refs_1_), custom_call_target="tpu_custom_call" | custom-call | flops 40000000000 | bytes 1048576 | tf_op jit(solution)/shard_map/pallas_call | solution.py:675
  905.8 28.2 %shard_map.464 = (f32[8,48,576]{2,1,0:T(8,128)}, f32[8,24,384]{2,1,0:T(8,128)}, f32[32,8,128]{2,1,0:T(8,128)}, f32[1,192]{1,0:T(1,128)}, s32[96,1536]{1,0:T(8,128)}) custom-call(f32[8,48,576]{2,1,0:T(8,128)} %multiply_add_fusion.2.refs_0_, f32[8,24,384]{2,1,0:T(8,128)} %multiply_add_fusion.3.refs_1_, f32[8,128]{1,0:T(8,128)} %broadcast_in_dim.100.refs_2_, ...), custom_call_target="tpu_custom_call" | custom-call | flops 30000001024 | bytes 1048576 | tf_op jit(solution)/shard_map/pallas_call | solution.py:675
  943.7 9.5 fusion.20
  961.0 71.6 %shard_map.465 = f32[2,2,2,4,192,128]{5,4,3,2,1,0:T(8,128)S(1)} custom-call(f32[2,2,2,4,192,128]{5,4,3,2,1,0:T(8,128)S(1)} %bitcast.421), custom_call_target="tpu_custom_call" | custom-call | flops 20000000000 | bytes 1048576 | tf_op jit(solution)/shard_map/pallas_call | solution.py:675
  (589 shorter events, 276.0 us)
Async XLA Ops:
  7.2 180.7 %all-gather.7.cloned.1.call-start = ((), (), s32[]{:S(2)}) async-start(), calls=%async_computation.3 | async-start | bytes 1966080 | tf_op jit(solution)/shard_map/all_gather | solution.py:1775
  7.9 197.3 %all-gather.5.cloned.1.call-start = ((), (), s32[]{:S(2)}) async-start(), calls=%async_computation.2 | async-start | bytes 14598144 | tf_op jit(solution)/shard_map/all_gather | solution.py:1779
  85.2 100.2 %copy-start.4 = (bf16[4,8,48,390]{3,2,1,0:T(8,128)(2,1)}, bf16[4,8,48,390]{3,2,1,0:T(8,128)(2,1)S(1)}, u32[]{:S(2)}) copy-start(bf16[4,8,48,390]{3,2,1,0:T(8,128)(2,1)S(1)} %get-tuple-element.84) | copy-start | bytes 3594244
  85.3 220.9 %all-gather.9.cloned.1.call-start = ((), (), s32[]{:S(2)}) async-start(), calls=%async_computation.4 | async-start | bytes 5898240 | tf_op jit(solution)/shard_map/all_gather | solution.py:1780
  88.0 99.8 %collective-permute-start = (bf16[192,1536]{1,0:T(8,128)(2,1)}, bf16[192,1536]{1,0:T(8,128)(2,1)}, u32[]{:S(2)}, u32[]{:S(2)}) collective-permute-start(bf16[192,1536]{1,0:T(8,128)(2,1)} %convert_element_type.263), channel_id=1, source_target_pairs={{0,0},{2,1},{4,2},{6,3},{8,4},{10,5},{12,6},{14,7},{1,8},{3,9},{5,... | collective-permute-start | bytes 1769480 | tf_op jit(solution)/shard_map/ppermute | solution.py:1786
  93.9 296.4 %collective-permute-start.1 = (f32[2,128,64]{1,2,0:T(8,128)}, f32[2,128,64]{1,2,0:T(8,128)}, u32[]{:S(2)}, u32[]{:S(2)}) collective-permute-start(f32[2,128,64]{1,2,0:T(8,128)} %get-tuple-element.414), channel_id=1, source_target_pairs={{0,0},{1,8},{2,16},{3,24},{4,1},{5,9},{6,17},{7,25},{8,2},{9,10},{... | collective-permute-start | bytes 196616 | tf_op jit(solution)/shard_map/ppermute | solution.py:1772
  98.9 246.9 %all-gather.11.cloned.1.call-start = ((), (), s32[]{:S(2)}) async-start(), calls=%async_computation.5 | async-start | bytes 2949120 | tf_op jit(solution)/shard_map/all_gather | solution.py:1785
  184.6 53.7 %copy-start.102 = (f32[1536]{0:T(1024)}, f32[1536]{0:T(1024)S(1)}, u32[]{:S(2)}) copy-start(f32[1536]{0:T(1024)S(1)} %get-tuple-element.309) | copy-start | bytes 18436
  187.8 639.3 %reduce-scatter.5.cloned.1.call-start = ((), (), s32[]{:S(2)}) async-start(), calls=%async_computation.7 | async-start | bytes 1474560 | tf_op jit(solution)/shard_map/reduce_scatter | solution.py:1954
  352.5 37.5 %copy-start.40 = (f32[256,1536]{1,0:T(8,128)S(1)}, f32[256,1536]{1,0:T(8,128)}, u32[]{:S(2)}) copy-start(f32[256,1536]{1,0:T(8,128)} %copy-done.39) | copy-start | bytes 4718596
  490.9 37.8 %copy-start.41 = (f32[256,1536]{1,0:T(8,128)S(1)}, f32[256,1536]{1,0:T(8,128)}, u32[]{:S(2)}) copy-start(f32[256,1536]{1,0:T(8,128)} %copy-done.39) | copy-start | bytes 4718596
  490.9 37.8 %copy-start.103 = (f32[1536]{0:T(1024)S(1)}, f32[1536]{0:T(1024)}, u32[]{:S(2)}) copy-start(f32[1536]{0:T(1024)} %copy-done.102) | copy-start | bytes 18436
  490.9 37.8 %copy-start.123 = (f32[256]{0:T(256)S(1)}, f32[256]{0:T(256)}, u32[]{:S(2)}) copy-start(f32[256]{0:T(256)} %copy-done.122) | copy-start | bytes 3076
  490.9 37.8 %copy-start.136 = (f32[256]{0:T(256)S(1)}, f32[256]{0:T(256)}, u32[]{:S(2)}) copy-start(f32[256]{0:T(256)} %copy-done.135) | copy-start | bytes 3076
  575.8 72.7 %copy-start.88 = (bf16[192,2048]{1,0:T(8,128)(2,1)S(1)}, bf16[192,2048]{1,0:T(8,128)(2,1)}, u32[]{:S(2)}) copy-start(bf16[192,2048]{1,0:T(8,128)(2,1)} %copy.297) | copy-start | bytes 2359300
  712.1 115.1 %reduce-scatter.3.cloned.1.call-start = ((), (), s32[]{:S(2)}) async-start(), calls=%async_computation.6 | async-start | bytes 5898240 | tf_op jit(solution)/shard_map/reduce_scatter | solution.py:1910
  726.5 32.9 %copy-start.12 = (bf16[1536,576]{1,0:T(8,128)(2,1)S(1)}, bf16[1536,576]{1,0:T(8,128)(2,1)}, u32[]{:S(2)}) copy-start(bf16[1536,576]{1,0:T(8,128)(2,1)} %copy-done.11) | copy-start | bytes 5308420
  726.5 32.9 %copy-start.16 = (bf16[8,2,128,64]{3,2,0,1:T(8,128)(2,1)S(1)}, bf16[8,2,128,64]{3,2,0,1:T(8,128)(2,1)}, u32[]{:S(2)}) copy-start(bf16[8,2,128,64]{3,2,0,1:T(8,128)(2,1)} %copy-done.15) | copy-start | bytes 786436
  726.5 32.9 %copy-start.23 = (bf16[1536,64]{0,1:T(8,128)(2,1)S(1)}, bf16[1536,64]{0,1:T(8,128)(2,1)}, u32[]{:S(2)}) copy-start(bf16[1536,64]{0,1:T(8,128)(2,1)} %copy-done.22) | copy-start | bytes 589828
  726.5 32.9 %copy-start.25 = (f32[2,1,1536]{2,1,0:T(1,128)S(1)}, f32[2,1,1536]{2,1,0:T(1,128)}, u32[]{:S(2)}) copy-start(f32[2,1,1536]{2,1,0:T(1,128)} %copy-done.24) | copy-start | bytes 36868
  726.5 32.9 %copy-start.27 = (f32[2,1536]{1,0:T(2,128)S(1)}, f32[2,1536]{1,0:T(2,128)}, u32[]{:S(2)}) copy-start(f32[2,1536]{1,0:T(2,128)} %copy-done.26) | copy-start | bytes 36868
  761.2 26.1 %copy-start.145 = (f32[1536]{0:T(1024)S(1)}, f32[1536]{0:T(1024)}, u32[]{:S(2)}) copy-start(f32[1536]{0:T(1024)} %get-tuple-element.306) | copy-start | bytes 18436
  761.2 27.2 %copy-start.121 = (f32[1536]{0:T(1024)S(1)}, f32[1536]{0:T(1024)}, u32[]{:S(2)}) copy-start(f32[1536]{0:T(1024)} %get-tuple-element.301) | copy-start | bytes 18436
  761.2 27.8 %copy-start.120 = (f32[1536]{0:T(1024)S(1)}, f32[1536]{0:T(1024)}, u32[]{:S(2)}) copy-start(f32[1536]{0:T(1024)} %get-tuple-element.305) | copy-start | bytes 18436
  (152 other events, 709.5 us)
Sparse Core Ops, SparseCore 0:
  9.6 30.7 all-gather.6
  85.4 119.8 all-gather.4
  207.4 87.9 all-gather.8
  296.8 48.9 all-gather.10
  712.2 28.3 reduce-scatter.4
  742.7 83.9 reduce-scatter.2
